TPU v7x, 1024 devices: a whole 4x4x32 slice. The times are simulated.
1024 devices in a mesh: dp: 128 (over x_hi, z, core), emb: 8 (over y, x_lo).
Axes of the slice: x: 4 (x_hi: 2, x_lo: 2; x = x_hi * 2 + x_lo), y: 4, z: 32, core: 2. Of those that a mesh axis runs over, the one named last changes fastest.
Arguments:
- img_feat: bfloat16 [65536, 1152], P('dp'), may hold values from -6 to 6
- w_proj: bfloat16 [1152, 1152], P(None, 'emb'), may hold values from -0.1875 to 0.1875
- txt_emb: bfloat16 [65536, 1152], P(('dp', 'emb')), may hold values from -0.19921875 to 0.19921875
- logit_scale: float32 [1], replicated, may hold values from 1 to 3
- logit_bias: float32 [1], replicated, may hold values from -3 to -1
Outputs:
- d_weight: float32 [1152, 1152], P(None, 'emb')
- d_text: float32 [65536, 1152], P(('dp', 'emb'))
All inputs are finite; a program needn't handle non-finite values.
Results may differ from a plain program's by a relative error of at most 0.0059.
Values may be sent and summed in bfloat16 or wider, within the bound.
No kernel may reach another device: no remote copies, remote signals or barrier semaphores. Data moves between devices by JAX's collectives and lax.ppermute only.
A program may use at most 32 MiB of HBM per device.

v0:
```python
import jax
import jax.numpy as jnp
from jax import lax
from jax.sharding import PartitionSpec as P

STEPS = 3


epsilon = 1e-06


def passed_along(array, axis, by):
    count = lax.axis_size(axis)
    return lax.ppermute(array, axis, [(i, (i + by) % count) for i in range(count)])


def unit_rows(values):
    widened = values.astype(jnp.float32)
    inverse = lax.rsqrt(jnp.sum(widened * widened, axis=1, keepdims=True) + epsilon)
    return (widened * inverse, inverse)


def local(img_feat, w_proj, txt_emb, logit_scale, logit_bias):
    image_rows = img_feat.shape[0]
    text_rows = txt_emb.shape[0]
    slice_width = w_proj.shape[1]
    member = lax.axis_index("emb")
    multiplier = logit_scale[0]
    offset = logit_bias[0]
    local_proj = jnp.dot(img_feat, w_proj, preferred_element_type=jnp.float32).astype(jnp.bfloat16)
    projected = lax.all_gather(local_proj, "emb", axis=1, tiled=True)
    unit_img, inv_img = unit_rows(projected)
    z_img = unit_img.astype(jnp.bfloat16)
    unit_txt, inv_txt = unit_rows(txt_emb)
    z_txt = unit_txt.astype(jnp.bfloat16)
    row_index = lax.broadcasted_iota(jnp.int32, (image_rows, text_rows), 0)
    col_index = lax.broadcasted_iota(jnp.int32, (image_rows, text_rows), 1)
    first_signs = jnp.where(row_index == member * text_rows + col_index, 1.0, -1.0).astype(
        jnp.float32
    )

    def visit_block(visitor, signs):
        cosines = lax.dot_general(
            z_img, visitor, (((1,), (1,)), ((), ())), preferred_element_type=jnp.float32
        )
        logits = multiplier * cosines + offset
        pair_grad = (-signs * jax.nn.sigmoid(-signs * logits)).astype(jnp.bfloat16)
        img_term = multiplier * jnp.dot(pair_grad, visitor, preferred_element_type=jnp.float32)
        txt_term = multiplier * lax.dot_general(
            pair_grad, z_img, (((0,), (0,)), ((), ())), preferred_element_type=jnp.float32
        )
        return (img_term, txt_term, pair_grad)

    grad_img, own_term, first_pairs = visit_block(z_txt, first_signs)
    pair_list = [first_pairs]
    visitor_list = [z_txt]
    visitor = z_txt
    grad_txt = own_term
    for distance in range(1, STEPS):
        visitor = passed_along(visitor, "dp", 1)
        img_term, txt_term, pair_grad = visit_block(visitor, -1.0)
        pair_list.append(pair_grad)
        visitor_list.append(visitor)
        grad_img = grad_img + img_term
        grad_txt = grad_txt + passed_along(txt_term.astype(jnp.bfloat16), "dp", -distance).astype(
            txt_term.dtype
        )
    unit_part = lax.dynamic_slice_in_dim(unit_img, member * slice_width, slice_width, 1)
    needs_inner = True
    grad_part = lax.psum_scatter(grad_img, "emb", scatter_dimension=1, tiled=True)
    inner_prod = lax.psum(jnp.sum(unit_part * grad_part, axis=1, keepdims=True), "emb")
    grad_proj = (inv_img * (grad_part - unit_part * inner_prod)).astype(jnp.bfloat16)
    local_weight = lax.dot_general(
        img_feat, grad_proj, (((0,), (0,)), ((), ())), preferred_element_type=jnp.float32
    )
    d_weight = lax.psum(local_weight, "dp")
    inner_txt = jnp.sum(unit_txt * grad_txt, axis=1, keepdims=True)
    d_text = inv_txt * (grad_txt - unit_txt * inner_txt)
    return (d_weight, d_text)


def solution(mesh):
    in_specs = (P("dp", None), P(None, "emb"), P(("dp", "emb"), None), P(), P())
    out_specs = (P(None, "emb"), P(("dp", "emb"), None))
    return jax.shard_map(local, mesh=mesh, in_specs=in_specs, out_specs=out_specs, check_vma=False)
```

profile of v0, /device:TPU:1, one launch (start us, length us, event | category | flops | bytes accessed | tf_op | source)
XLA Modules:
  0.0 1155.4 jit_solution(1301824872539154389)
XLA Ops:
  7.2 0.0 all-gather.2.cloned.1.call-start
  7.2 1.2 copy-done
  8.4 2.2 convolution_convert_fusion
  10.6 0.0 all-gather.2.cloned.1.call-update
  10.6 0.0 reduce-scatter.2.cloned.1.call-start
  10.7 1.0 fusion.37
  11.7 1.0 fusion.33
  12.7 4.9 collective-permute-start
  19.0 10.7 collective-permute-done
  29.7 1.9 collective-permute-start.1
  31.6 42.4 %all-gather.2.cloned.1.call-done = bf16[512,1152]{0,1:T(8,128)(2,1)} async-done(((bf16[512,144]{0,1:T(8,128)(2,1)}), bf16[512,1152]{0,1:T(8,128)(2,1)}) %all-gather.2.cloned.1.call-update) | async-done | bytes 1179664 | tf_op jit(solution)/shard_map/all_gather | solution.py:31
  74.0 1.6 fusion.1
  75.6 1.8 fusion.21
  77.3 0.5 fusion.43
  77.9 0.4 fusion.22
  78.3 0.5 convolution_add_fusion.1
  78.8 0.4 fusion.23
  79.2 1.9 fusion
  81.2 0.0 all-reduce.2.cloned.1.call-start
  81.2 0.5 fusion.3
  81.7 8.7 collective-permute-start.3
  90.4 0.5 fusion.2
  90.9 7.6 collective-permute-start.2
  98.6 1.7 convert_multiply_fusion
  100.3 60.0 %reduce-scatter.2.cloned.1.call-done = f32[512,144]{0,1:T(8,128)} async-done(((f32[512,1152]{0,1:T(8,128)}), f32[512,144]{0,1:T(8,128)}) %reduce-scatter.2.cloned.1.call-update) | async-done | bytes 294928 | tf_op jit(solution)/shard_map/reduce_scatter | solution.py:70
  160.3 1.1 multiply_reduce_fusion
  161.4 13.1 %psum.14 = f32[512]{0:T(512)S(1)} all-reduce(f32[512]{0:T(512)S(1)} %multiply_reduce_fusion), channel_id=1, replica_groups=mesh['dp'=128,'emb'=8] {'emb'}, use_global_device_ids=true, to_apply=%region_4.5 | all-reduce | flops 512 | bytes 4096 | tf_op jit(solution)/shard_map/psum | solution.py:71
  174.5 2.3 convolution_bitcast_fusion
  176.8 0.6 fusion.34
  177.4 0.8 fusion.36
  178.3 968.6 %all-reduce.2.cloned.1.call-done = f32[1152,144]{0,1:T(8,128)} async-done(((f32[1152,144]{0,1:T(8,128)}), f32[1152,144]{0,1:T(8,128)}) %all-reduce.2.cloned.1.call-update) | async-done | bytes 663568 | tf_op jit(solution)/shard_map/psum | solution.py:76
  1146.9 2.0 copy.10
  (13 shorter events, 0.1 us)
Async XLA Ops:
  7.2 1.3 copy-start
  7.2 66.8 %all-gather.2.cloned.1.call-start = ((), (), s32[]{:S(2)}) async-start(), calls=%async_computation.1 | async-start | bytes 1327104 | tf_op jit(solution)/shard_map/all_gather | solution.py:31
  10.6 149.6 %reduce-scatter.2.cloned.1.call-start = ((), (), s32[]{:S(2)}) async-start(), calls=%async_computation.2 | async-start | bytes 2654208 | tf_op jit(solution)/shard_map/reduce_scatter | solution.py:70
  12.7 16.9 %collective-permute-start = (bf16[64,1152]{1,0:T(8,128)(2,1)S(1)}, bf16[64,1152]{1,0:T(8,128)(2,1)S(1)}, u32[]{:S(2)}, u32[]{:S(2)}) collective-permute-start(bf16[64,1152]{1,0:T(8,128)(2,1)S(1)} %fusion.33), channel_id=1, source_target_pairs={{0,8},{8,16},{16,24},{24,32},{32,40},{40,48},{48,56},{56,64},{64,7... | collective-permute-start | bytes 442376 | tf_op jit(solution)/shard_map/ppermute | solution.py:14
  29.7 49.1 %collective-permute-start.1 = (bf16[64,1152]{1,0:T(8,128)(2,1)S(1)}, bf16[64,1152]{1,0:T(8,128)(2,1)S(1)}, u32[]{:S(2)}, u32[]{:S(2)}) collective-permute-start(bf16[64,1152]{1,0:T(8,128)(2,1)S(1)} %collective-permute-done), channel_id=1, source_target_pairs={{0,8},{8,16},{16,24},{24,32},{32,40},{40,48},{48,56},{56,64},{64,7... | collective-permute-start | bytes 442376 | tf_op jit(solution)/shard_map/ppermute | solution.py:14
  75.6 2.3 copy-start.1
  81.2 1065.7 %all-reduce.2.cloned.1.call-start = ((), (), s32[]{:S(2)}) async-start(), calls=%async_computation.3 | async-start | bytes 1327104 | tf_op jit(solution)/shard_map/psum | solution.py:76
  81.7 95.1 %collective-permute-start.3 = (bf16[64,1152]{1,0:T(8,128)(2,1)S(1)}, bf16[64,1152]{1,0:T(8,128)(2,1)S(1)}, u32[]{:S(2)}, u32[]{:S(2)}) collective-permute-start(bf16[64,1152]{1,0:T(8,128)(2,1)S(1)} %fusion.3), channel_id=1, source_target_pairs={{0,1008},{8,1016},{16,0},{24,8},{32,16},{40,24},{48,32},{56,40},{6... | collective-permute-start | bytes 442376 | tf_op jit(solution)/shard_map/ppermute | solution.py:14
  90.9 85.9 %collective-permute-start.2 = (bf16[64,1152]{1,0:T(8,128)(2,1)S(1)}, bf16[64,1152]{1,0:T(8,128)(2,1)S(1)}, u32[]{:S(2)}, u32[]{:S(2)}) collective-permute-start(bf16[64,1152]{1,0:T(8,128)(2,1)S(1)} %fusion.2), channel_id=1, source_target_pairs={{0,1016},{8,0},{16,8},{24,16},{32,24},{40,32},{48,40},{56,48},{64,... | collective-permute-start | bytes 442376 | tf_op jit(solution)/shard_map/ppermute | solution.py:14
  100.3 76.6 %copy-start.2 = (bf16[64,1152]{1,0:T(8,128)(2,1)S(1)}, bf16[64,1152]{1,0:T(8,128)(2,1)}, u32[]{:S(2)}) copy-start(bf16[64,1152]{1,0:T(8,128)(2,1)} %param.7) | copy-start | bytes 442372
Sparse Core Ops, SparseCore 0:
  11.2 62.6 all-gather.1
  81.3 78.9 reduce-scatter.1
  176.9 969.9 all-reduce.1
where the time goes:
time: 1160 us
  waiting for transfers between devices  1080 us (93%)
  starting transfers between devices  23.3 us (2%)
  between operations  15.2 us (1%)
  blocking collectives  13.1 us (1%)
    psum x1, waiting for transfers between devices, local(): d_weight = lax.psum(local_weight, 'dp')  969 us
    reduce_scatter x1, waiting for transfers between devices, local(): lax.psum_scatter(grad_img, 'emb', scatter_dimension=1, tiled=True)  60 us
    all_gather x1, waiting for transfers between devices, local(): projected = lax.all_gather(local_proj, 'emb', axis=1, tiled=True)  42.4 us
  transfers between devices with their start and end apart: 7, of which 4 were waited for; matrix products, arithmetic and copies ran while one was open for 1% of the time, Pallas kernels for 0%

commit v1 on v0

v1 whole, which is shorter than its diff:
```python
import jax
import jax.numpy as jnp
from jax import lax
from jax.sharding import PartitionSpec as P

STEPS = 3
EPSILON = 1e-06
LANES = 128
UNIT = 16


def passed_along(array, axis, by):
    count = lax.axis_size(axis)
    return lax.ppermute(array, axis, [(i, (i + by) % count) for i in range(count)])


def line_groups(count):
    z_len = count // 4
    index = lambda hi, z, core: (hi * z_len + z) * 2 + core
    lines = [[index(hi, z, c) for z in range(z_len)] for hi in range(2) for c in range(2)]
    quads = [[index(hi, z, c) for hi in range(2) for c in range(2)] for z in range(z_len)]
    return z_len, lines, quads


def swap(parts, axis, groups=None):
    return lax.all_to_all(parts, axis, 0, 0, axis_index_groups=groups)


def gathered(part, count, axis, groups=None):
    return swap(jnp.broadcast_to(part[None], (count,) + part.shape), axis, groups)


def summed(parts):
    return jnp.sum(parts.astype(jnp.float32), axis=0)


def sum_over_dp(grad_t):
    width, features = grad_t.shape
    tiles = features // LANES
    z_len, lines, quads = line_groups(lax.axis_size("dp"))
    units = tiles * width // UNIT
    per_quad = -(-units // 4)
    rows = jnp.concatenate(
        [grad_t[:, LANES * t : LANES * (t + 1)] for t in range(tiles)], axis=0
    ).astype(jnp.bfloat16)
    rows = jnp.pad(rows, ((0, (4 * per_quad - units) * UNIT), (0, 0)))
    quad = summed(swap(rows.reshape(4, per_quad * UNIT, LANES), "dp", quads)).astype(jnp.bfloat16)
    per_line = -(-per_quad // z_len)
    quad = jnp.pad(quad, ((0, (z_len * per_line - per_quad) * UNIT), (0, 0)))
    line = summed(swap(quad.reshape(z_len, per_line * UNIT, LANES), "dp", lines))
    back = gathered(line.astype(jnp.bfloat16), z_len, "dp", lines)
    back = back.reshape(z_len * per_line * UNIT, LANES)[: per_quad * UNIT]
    whole = gathered(back, 4, "dp", quads).reshape(4 * per_quad * UNIT, LANES)[: units * UNIT]
    whole = whole.astype(jnp.float32).reshape(tiles, width, LANES)
    return jnp.swapaxes(whole, 1, 2).reshape(features, width)


def local(img_feat, w_proj, txt_emb, logit_scale, logit_bias):
    image_rows, features = img_feat.shape
    text_rows = txt_emb.shape[0]
    width = w_proj.shape[1]
    members = lax.axis_size("emb")
    member = lax.axis_index("emb")
    scale = logit_scale[0]
    offset = logit_bias[0]

    wide_txt = txt_emb.astype(jnp.float32)
    inv_txt = lax.rsqrt(jnp.sum(wide_txt * wide_txt, axis=1, keepdims=True) + EPSILON)
    unit_txt = wide_txt * inv_txt
    z_txt = unit_txt.astype(jnp.bfloat16)
    visitors = [z_txt] + [passed_along(z_txt, "dp", k) for k in range(1, STEPS)]

    local_proj = lax.dot_general(
        w_proj, img_feat, (((0,), (1,)), ((), ())), preferred_element_type=jnp.float32
    ).astype(jnp.bfloat16)
    projected = gathered(local_proj, members, "emb").reshape(features, image_rows)
    wide_img = projected.astype(jnp.float32)
    inv_img = lax.rsqrt(jnp.sum(wide_img * wide_img, axis=0, keepdims=True) + EPSILON)
    unit_img = wide_img * inv_img
    z_img = unit_img.astype(jnp.bfloat16)

    texts = jnp.concatenate(visitors, axis=0)
    cosines = jnp.dot(texts, z_img, preferred_element_type=jnp.float32)
    text_index = lax.broadcasted_iota(jnp.int32, cosines.shape, 0)
    image_index = lax.broadcasted_iota(jnp.int32, cosines.shape, 1)
    own = (text_index < text_rows) & (image_index == member * text_rows + text_index)
    signs = jnp.where(own, 1.0, -1.0)
    pair_grad = (-signs * jax.nn.sigmoid(-signs * (scale * cosines + offset))).astype(jnp.bfloat16)
    inner_img = jnp.sum(pair_grad.astype(jnp.float32) * cosines, axis=0, keepdims=True)

    txt_terms = scale * lax.dot_general(
        pair_grad, z_img, (((1,), (1,)), ((), ())), preferred_element_type=jnp.float32
    )
    sent = [
        passed_along(txt_terms[k * text_rows : (k + 1) * text_rows].astype(jnp.bfloat16), "dp", -k)
        for k in range(1, STEPS)
    ]

    grad_img = lax.dot_general(
        texts, pair_grad, (((0,), (0,)), ((), ())), preferred_element_type=jnp.float32
    )
    grad_proj = (scale * inv_img) * (grad_img - unit_img * inner_img)
    parts = grad_proj.astype(jnp.bfloat16).reshape(members, width, image_rows)
    grad_part = summed(swap(parts, "emb")).astype(jnp.bfloat16)
    local_weight = jnp.dot(grad_part, img_feat, preferred_element_type=jnp.float32)
    d_weight = sum_over_dp(local_weight)

    grad_txt = txt_terms[:text_rows]
    for term in sent:
        grad_txt = grad_txt + term.astype(jnp.float32)
    inner_txt = jnp.sum(unit_txt * grad_txt, axis=1, keepdims=True)
    d_text = inv_txt * (grad_txt - unit_txt * inner_txt)
    return (d_weight, d_text)


def solution(mesh):
    in_specs = (P("dp", None), P(None, "emb"), P(("dp", "emb"), None), P(), P())
    out_specs = (P(None, "emb"), P(("dp", "emb"), None))
    return jax.shard_map(local, mesh=mesh, in_specs=in_specs, out_specs=out_specs, check_vma=False)
```

time: 1160 us -> 172 us (0.15)
  waiting for transfers between devices: 1080 us -> 34.9 us
  blocking collectives: 13.1 us -> 84.5 us
  starting transfers between devices: 23.3 us -> 37.5 us
  between operations: 15.2 us -> 2.18 us
    psum x1 -> x0, waiting for transfers between devices: 969 us -> none  [local(): d_weight = lax.psum(local_weight, 'dp')]
    all_to_all x0 -> x3, blocking collectives: none -> 84.5 us  [swap(): return lax.all_to_all(parts, axis, 0, 0, axis_index_groups=groups)]
    reduce_scatter x1 -> x0, waiting for transfers between devices: 60 us -> none  [local(): lax.psum_scatter(grad_img, 'emb', scatter_dimension=1, tiled=True)]
    all_gather x1 -> x0, waiting for transfers between devices: 42.4 us -> none  [local(): projected = lax.all_gather(local_proj, 'emb', axis=1, tiled=True)]
    all_to_all x0 -> x3, starting transfers between devices: none -> 19.8 us  [swap(): return lax.all_to_all(parts, axis, 0, 0, axis_index_groups=groups)]
    all_to_all x0 -> x3, waiting for transfers between devices: none -> 15.6 us  [swap(): return lax.all_to_all(parts, axis, 0, 0, axis_index_groups=groups)]
    psum x1 -> x0, blocking collectives: 13.1 us -> none  [local(): lax.psum(jnp.sum(unit_part * grad_part, axis=1, keepdims=True), 'emb')]
  transfers between devices with their start and end apart: 7 -> 7, of which waited for: 4 -> 6; matrix products, arithmetic and copies ran while one was open for 1% -> 2% of each run, Pallas kernels for 0% -> 0%
where the time goes in v1:
time: 172 us; the launch traced here: 171 us
  blocking collectives  84.5 us (49%)
  starting transfers between devices  37.5 us (22%)
  waiting for transfers between devices  34.9 us (20%)
  other arithmetic  4.12 us (2%)
  local copies, waits for them, and re-layouts  4.03 us (2%)
  matrix products  3.83 us (2%)
  between operations  2.18 us (1%)
    all_to_all x3, blocking collectives, swap(): return lax.all_to_all(parts, axis, 0, 0, axis_index_groups=groups)  84.5 us
    all_to_all x3, starting transfers between devices, swap(): return lax.all_to_all(parts, axis, 0, 0, axis_index_groups=groups)  19.8 us
    ppermute x4, waiting for transfers between devices, passed_along(): lax.ppermute(array, axis, [(i, (i + by) % count) for i in range(count)])  19.3 us
    ppermute x4, starting transfers between devices, passed_along(): lax.ppermute(array, axis, [(i, (i + by) % count) for i in range(count)])  17.7 us
    all_to_all x3, waiting for transfers between devices, swap(): return lax.all_to_all(parts, axis, 0, 0, axis_index_groups=groups)  15.6 us
  transfers between devices with their start and end apart: 7, of which 6 were waited for; matrix products, arithmetic and copies ran while one was open for 2% of the time, Pallas kernels for 0%

profile of v1, /device:TPU:1, one launch (start us, length us, event | category | flops | bytes accessed | tf_op | source)
XLA Modules:
  0.0 171.0 jit_solution(10931084927728582050)
XLA Ops:
  0.6 1.3 copy-done
  1.9 1.5 convolution_convert_fusion.1
  3.4 1.1 broadcast_in_dim.16
  4.5 6.1 %all-to-all-start = ((bf16[8,144,512]{2,1,0:T(8,128)(2,1)}), bf16[8,144,512]{2,1,0:T(8,128)(2,1)S(1)}, u32[]{:S(2)}, u32[]{:S(2)}) async-start(bf16[8,144,512]{2,1,0:T(8,128)(2,1)} %broadcast_in_dim.16), calls=%async_computation | async-start | bytes 2359296 | tf_op jit(solution)/shard_map/all_to_all | solution.py:26
  10.6 0.1 fusion.10
  10.9 3.5 %collective-permute-start.1 = (bf16[64,1152]{1,0:T(8,128)(2,1)S(1)}, bf16[64,1152]{1,0:T(8,128)(2,1)S(1)}, u32[]{:S(2)}, u32[]{:S(2)}) collective-permute-start(bf16[64,1152]{1,0:T(8,128)(2,1)S(1)} %fusion.6), channel_id=1, source_target_pairs={{0,16},{8,24},{16,32},{24,40},{32,48},{40,56},{48,64},{56,72},{64,... | collective-permute-start | bytes 442376 | tf_op jit(solution)/shard_map/ppermute | solution.py:14
  14.4 4.7 %collective-permute-start = (bf16[64,1152]{1,0:T(8,128)(2,1)S(1)}, bf16[64,1152]{1,0:T(8,128)(2,1)S(1)}, u32[]{:S(2)}, u32[]{:S(2)}) collective-permute-start(bf16[64,1152]{1,0:T(8,128)(2,1)S(1)} %fusion.6), channel_id=1, source_target_pairs={{0,8},{8,16},{16,24},{24,32},{32,40},{40,48},{48,56},{56,64},{64,7... | collective-permute-start | bytes 442376 | tf_op jit(solution)/shard_map/ppermute | solution.py:14
  20.4 1.3 all-to-all-done
  21.7 0.3 multiply_reduce_fusion
  22.0 0.4 fusion.2
  22.4 12.2 %collective-permute-done.1 = bf16[64,1152]{1,0:T(8,128)(2,1)S(1)} collective-permute-done((bf16[64,1152]{1,0:T(8,128)(2,1)S(1)}, bf16[64,1152]{1,0:T(8,128)(2,1)S(1)}, u32[]{:S(2)}, u32[]{:S(2)}) %collective-permute-start.1) | collective-permute-done | bytes 147488 | tf_op jit(solution)/shard_map/ppermute | solution.py:14
  34.7 0.6 multiply_reduce_fusion.1
  35.3 0.7 fusion.1
  36.0 16.6 %all_to_all.30 = bf16[8,144,512]{2,1,0:T(8,128)(2,1)S(1)} all-to-all(bf16[8,144,512]{2,1,0:T(8,128)(2,1)S(1)} %bitcast.35), channel_id=1, replica_groups=mesh['dp'=128,'emb'=8] {'emb'}, dimensions={0} | all-to-all | bytes 2359296 | tf_op jit(solution)/shard_map/all_to_all | solution.py:26
  52.6 0.2 reduce_sum.75
  52.8 0.4 convolution_convert_fusion
  53.4 16.4 %all_to_all.31 = bf16[4,336,128]{2,1,0:T(8,128)(2,1)S(1)} all-to-all(bf16[4,336,128]{2,1,0:T(8,128)(2,1)S(1)} %bitcast.32), channel_id=1, replica_groups={{0,8,512,520},{16,24,528,536},{32,40,544,552},{48,56,560,568},{64,72,57..., dimensions={0} | all-to-all | bytes 688128 | tf_op jit(solution)/shard_map/all_to_all | solution.py:26
  69.8 51.5 %all_to_all.32 = bf16[32,16,128]{2,1,0:T(8,128)(2,1)S(1)} all-to-all(bf16[32,16,128]{2,1,0:T(8,128)(2,1)S(1)} %bitcast.36), channel_id=1, replica_groups={{0,16,32,48,64,80,96,112,128,144,160,176,192,208,224,240,256,272,288,30..., dimensions={0} | all-to-all | bytes 262144 | tf_op jit(solution)/shard_map/all_to_all | solution.py:26
  121.3 0.7 broadcast_in_dim.19
  122.0 3.9 %all-to-all-start.4 = ((bf16[32,16,128]{2,1,0:T(8,128)(2,1)}), bf16[32,16,128]{2,1,0:T(8,128)(2,1)S(1)}, u32[]{:S(2)}, u32[]{:S(2)}) async-start(bf16[32,16,128]{2,1,0:T(8,128)(2,1)} %broadcast_in_dim.19), calls=%async_computation.4 | async-start | bytes 262144 | tf_op jit(solution)/shard_map/all_to_all | solution.py:26
  125.9 0.7 fusion.16
  126.6 4.7 %collective-permute-start.2 = (bf16[64,1152]{1,0:T(8,128)(2,1)S(1)}, bf16[64,1152]{1,0:T(8,128)(2,1)S(1)}, u32[]{:S(2)}, u32[]{:S(2)}) collective-permute-start(bf16[64,1152]{1,0:T(8,128)(2,1)S(1)} %get-tuple-element.4), channel_id=1, source_target_pairs={{0,1016},{8,0},{16,8},{24,16},{32,24},{40,32},{48,40},{56,48},{64,... | collective-permute-start | bytes 442376 | tf_op jit(solution)/shard_map/ppermute | solution.py:14
  131.3 4.8 %collective-permute-start.3 = (bf16[64,1152]{1,0:T(8,128)(2,1)S(1)}, bf16[64,1152]{1,0:T(8,128)(2,1)S(1)}, u32[]{:S(2)}, u32[]{:S(2)}) collective-permute-start(bf16[64,1152]{1,0:T(8,128)(2,1)S(1)} %get-tuple-element.5), channel_id=1, source_target_pairs={{0,1008},{8,1016},{16,0},{24,8},{32,16},{40,24},{48,32},{56,40},{6... | collective-permute-start | bytes 442376 | tf_op jit(solution)/shard_map/ppermute | solution.py:14
  136.1 6.5 %collective-permute-done.2 = bf16[64,1152]{1,0:T(8,128)(2,1)S(1)} collective-permute-done((bf16[64,1152]{1,0:T(8,128)(2,1)S(1)}, bf16[64,1152]{1,0:T(8,128)(2,1)S(1)}, u32[]{:S(2)}, u32[]{:S(2)}) %collective-permute-start.2) | collective-permute-done | bytes 147488 | tf_op jit(solution)/shard_map/ppermute | solution.py:14
  142.5 0.6 collective-permute-done.3
  143.2 0.2 fusion.7
  143.4 8.5 %all-to-all-done.4 = bf16[32,16,128]{2,1,0:T(8,128)(2,1)S(1)} async-done(((bf16[32,16,128]{2,1,0:T(8,128)(2,1)}), bf16[32,16,128]{2,1,0:T(8,128)(2,1)S(1)}, u32[]{:S(2)}, u32[]{:S(2)}) %all-to-all-start.4) | async-done | bytes 131104 | tf_op jit(solution)/shard_map/all_to_all | solution.py:26
  151.9 0.8 broadcast_in_dim.37
  152.7 9.9 %all-to-all-start.5 = ((bf16[4,336,128]{2,1,0:T(8,128)(2,1)}), bf16[4,336,128]{2,1,0:T(8,128)(2,1)S(1)}, u32[]{:S(2)}, u32[]{:S(2)}) async-start(bf16[4,336,128]{2,1,0:T(8,128)(2,1)} %broadcast_in_dim.37), calls=%async_computation.5 | async-start | bytes 688128 | tf_op jit(solution)/shard_map/all_to_all | solution.py:26
  162.6 1.8 %fusion.9 = f32[64,1152]{1,0:T(8,128)} fusion(bf16[64,1152]{1,0:T(8,128)(2,1)S(1)} %copy-done.1, f32[64]{0:T(128)S(1)} %fusion.7, f32[64]{0:T(128)S(1)} %add_rsqrt_fusion.1, bf16[64,1152]{1,0:T(8,128)(2,1)S(1)} %collective-permute-done.3, bf16[64,1152]{1,0:T(8,128)(2,1)S(1)} %collective-permute-done.2, f32[192,1152]{1,0:T(8,128)} %copy-done.4), kind=kLoop, calls=%fused_computation.23 | loop fusion | flops 663552 | bytes 1032704 | tf_op jit(solution)/shard_map/mul | solution.py:112
  164.4 5.8 %all-to-all-done.5 = bf16[4,336,128]{2,1,0:T(8,128)(2,1)S(1)} async-done(((bf16[4,336,128]{2,1,0:T(8,128)(2,1)}), bf16[4,336,128]{2,1,0:T(8,128)(2,1)S(1)}, u32[]{:S(2)}, u32[]{:S(2)}) %all-to-all-start.5) | async-done | bytes 344096 | tf_op jit(solution)/shard_map/all_to_all | solution.py:26
  170.1 0.9 copy_bitcast_fusion
  (31 shorter events, 0.4 us)
Async XLA Ops:
  0.6 1.3 copy-start
  4.5 6.1 %copy-start.1 = (bf16[64,1152]{1,0:T(8,128)(2,1)S(1)}, bf16[64,1152]{1,0:T(8,128)(2,1)}, u32[]{:S(2)}) copy-start(bf16[64,1152]{1,0:T(8,128)(2,1)} %param.7) | copy-start | bytes 442372
  4.5 17.2 %all-to-all-start = ((bf16[8,144,512]{2,1,0:T(8,128)(2,1)}), bf16[8,144,512]{2,1,0:T(8,128)(2,1)S(1)}, u32[]{:S(2)}, u32[]{:S(2)}) async-start(bf16[8,144,512]{2,1,0:T(8,128)(2,1)} %broadcast_in_dim.16), calls=%async_computation | async-start | bytes 2359296 | tf_op jit(solution)/shard_map/all_to_all | solution.py:26
  10.9 23.8 %collective-permute-start.1 = (bf16[64,1152]{1,0:T(8,128)(2,1)S(1)}, bf16[64,1152]{1,0:T(8,128)(2,1)S(1)}, u32[]{:S(2)}, u32[]{:S(2)}) collective-permute-start(bf16[64,1152]{1,0:T(8,128)(2,1)S(1)} %fusion.6), channel_id=1, source_target_pairs={{0,16},{8,24},{16,32},{24,40},{32,48},{40,56},{48,64},{56,72},{64,... | collective-permute-start | bytes 442376 | tf_op jit(solution)/shard_map/ppermute | solution.py:14
  14.4 20.3 %collective-permute-start = (bf16[64,1152]{1,0:T(8,128)(2,1)S(1)}, bf16[64,1152]{1,0:T(8,128)(2,1)S(1)}, u32[]{:S(2)}, u32[]{:S(2)}) collective-permute-start(bf16[64,1152]{1,0:T(8,128)(2,1)S(1)} %fusion.6), channel_id=1, source_target_pairs={{0,8},{8,16},{16,24},{24,32},{32,40},{40,48},{48,56},{56,64},{64,7... | collective-permute-start | bytes 442376 | tf_op jit(solution)/shard_map/ppermute | solution.py:14
  22.4 12.8 %copy-start.2 = (bf16[1152,512]{1,0:T(8,128)(2,1)}, bf16[1152,512]{1,0:T(8,128)(2,1)S(1)}, u32[]{:S(2)}) copy-start(bf16[1152,512]{1,0:T(8,128)(2,1)S(1)} %get-tuple-element.2) | copy-start | bytes 3538948
  53.3 72.5 %copy-start.3 = (bf16[1152,512]{1,0:T(8,128)(2,1)S(1)}, bf16[1152,512]{1,0:T(8,128)(2,1)}, u32[]{:S(2)}) copy-start(bf16[1152,512]{1,0:T(8,128)(2,1)} %copy-done.2) | copy-start | bytes 3538948
  122.0 29.9 %all-to-all-start.4 = ((bf16[32,16,128]{2,1,0:T(8,128)(2,1)}), bf16[32,16,128]{2,1,0:T(8,128)(2,1)S(1)}, u32[]{:S(2)}, u32[]{:S(2)}) async-start(bf16[32,16,128]{2,1,0:T(8,128)(2,1)} %broadcast_in_dim.19), calls=%async_computation.4 | async-start | bytes 262144 | tf_op jit(solution)/shard_map/all_to_all | solution.py:26
  126.5 16.6 %copy-start.4 = (f32[192,1152]{1,0:T(8,128)}, f32[192,1152]{1,0:T(8,128)S(1)}, u32[]{:S(2)}) copy-start(f32[192,1152]{1,0:T(8,128)S(1)} %get-tuple-element.11) | copy-start | bytes 2654212
  126.6 16.0 %collective-permute-start.2 = (bf16[64,1152]{1,0:T(8,128)(2,1)S(1)}, bf16[64,1152]{1,0:T(8,128)(2,1)S(1)}, u32[]{:S(2)}, u32[]{:S(2)}) collective-permute-start(bf16[64,1152]{1,0:T(8,128)(2,1)S(1)} %get-tuple-element.4), channel_id=1, source_target_pairs={{0,1016},{8,0},{16,8},{24,16},{32,24},{40,32},{48,40},{56,48},{64,... | collective-permute-start | bytes 442376 | tf_op jit(solution)/shard_map/ppermute | solution.py:14
  131.3 11.9 %collective-permute-start.3 = (bf16[64,1152]{1,0:T(8,128)(2,1)S(1)}, bf16[64,1152]{1,0:T(8,128)(2,1)S(1)}, u32[]{:S(2)}, u32[]{:S(2)}) collective-permute-start(bf16[64,1152]{1,0:T(8,128)(2,1)S(1)} %get-tuple-element.5), channel_id=1, source_target_pairs={{0,1008},{8,1016},{16,0},{24,8},{32,16},{40,24},{48,32},{56,40},{6... | collective-permute-start | bytes 442376 | tf_op jit(solution)/shard_map/ppermute | solution.py:14
  152.7 17.4 %all-to-all-start.5 = ((bf16[4,336,128]{2,1,0:T(8,128)(2,1)}), bf16[4,336,128]{2,1,0:T(8,128)(2,1)S(1)}, u32[]{:S(2)}, u32[]{:S(2)}) async-start(bf16[4,336,128]{2,1,0:T(8,128)(2,1)} %broadcast_in_dim.37), calls=%async_computation.5 | async-start | bytes 688128 | tf_op jit(solution)/shard_map/all_to_all | solution.py:26

commit v2 on v1

--- a/solution.py
+++ b/solution.py
@@ -6,7 +6,7 @@
 STEPS = 3
 EPSILON = 1e-06
 LANES = 128
-UNIT = 16
+ROWS = 8
 
 
 def passed_along(array, axis, by):
@@ -14,12 +14,15 @@
     return lax.ppermute(array, axis, [(i, (i + by) % count) for i in range(count)])
 
 
-def line_groups(count):
+def dp_groups(count):
     z_len = count // 4
     index = lambda hi, z, core: (hi * z_len + z) * 2 + core
-    lines = [[index(hi, z, c) for z in range(z_len)] for hi in range(2) for c in range(2)]
-    quads = [[index(hi, z, c) for hi in range(2) for c in range(2)] for z in range(z_len)]
-    return z_len, lines, quads
+    near = [
+        [index(hi, z + dz, c) for hi in range(2) for dz in range(2) for c in range(2)]
+        for z in range(0, z_len, 2)
+    ]
+    far = [list(members) for members in zip(*near)]
+    return near, far
 
 
 def swap(parts, axis, groups=None):
@@ -37,20 +40,16 @@
 def sum_over_dp(grad_t):
     width, features = grad_t.shape
     tiles = features // LANES
-    z_len, lines, quads = line_groups(lax.axis_size("dp"))
-    units = tiles * width // UNIT
-    per_quad = -(-units // 4)
+    near, far = dp_groups(lax.axis_size("dp"))
+    count = len(near[0])
+    share = -(-tiles * width // (count * ROWS)) * ROWS
     rows = jnp.concatenate(
         [grad_t[:, LANES * t : LANES * (t + 1)] for t in range(tiles)], axis=0
     ).astype(jnp.bfloat16)
-    rows = jnp.pad(rows, ((0, (4 * per_quad - units) * UNIT), (0, 0)))
-    quad = summed(swap(rows.reshape(4, per_quad * UNIT, LANES), "dp", quads)).astype(jnp.bfloat16)
-    per_line = -(-per_quad // z_len)
-    quad = jnp.pad(quad, ((0, (z_len * per_line - per_quad) * UNIT), (0, 0)))
-    line = summed(swap(quad.reshape(z_len, per_line * UNIT, LANES), "dp", lines))
-    back = gathered(line.astype(jnp.bfloat16), z_len, "dp", lines)
-    back = back.reshape(z_len * per_line * UNIT, LANES)[: per_quad * UNIT]
-    whole = gathered(back, 4, "dp", quads).reshape(4 * per_quad * UNIT, LANES)[: units * UNIT]
+    rows = jnp.pad(rows, ((0, count * share - tiles * width), (0, 0)))
+    part = summed(swap(rows.reshape(count, share, LANES), "dp", near)).astype(jnp.bfloat16)
+    total = summed(lax.all_gather(part, "dp", axis=0, axis_index_groups=far)).astype(jnp.bfloat16)
+    whole = gathered(total, count, "dp", near).reshape(count * share, LANES)[: tiles * width]
     whole = whole.astype(jnp.float32).reshape(tiles, width, LANES)
     return jnp.swapaxes(whole, 1, 2).reshape(features, width)
 

time: 172 us -> 139 us (0.81)
  waiting for transfers between devices: 34.9 us -> 16.4 us
  blocking collectives: 84.5 us -> 73.9 us
  starting transfers between devices: 37.5 us -> 34.8 us
    all_to_all x3 -> x2, blocking collectives: 84.5 us -> 33.8 us  [swap(): return lax.all_to_all(parts, axis, 0, 0, axis_index_groups=groups)]
    all_gather x0 -> x1, blocking collectives: none -> 40.1 us  [sum_over_dp(): lax.all_gather(part, 'dp', axis=0, axis_index_groups=far)]
    all_to_all x3 -> x2, waiting for transfers between devices: 15.6 us -> 1.29 us  [swap(): return lax.all_to_all(parts, axis, 0, 0, axis_index_groups=groups)]
    ppermute x4, waiting for transfers between devices: 19.3 us -> 15.1 us  [passed_along(): lax.ppermute(array, axis, [(i, (i + by) % count) for i in range(count)])]
    all_to_all x3 -> x2, starting transfers between devices: 19.8 us -> 17.2 us  [swap(): return lax.all_to_all(parts, axis, 0, 0, axis_index_groups=groups)]
  transfers between devices with their start and end apart: 7 -> 6, of which waited for: 6 -> 3; matrix products, arithmetic and copies ran while one was open for 2% -> 3% of each run, Pallas kernels for 0% -> 0%
where the time goes in v2:
time: 139 us
  blocking collectives  73.9 us (53%)
  starting transfers between devices  34.8 us (25%)
  waiting for transfers between devices  16.4 us (12%)
  matrix products  4.83 us (3%)
  local copies, waits for them, and re-layouts  3.36 us (2%)
  other arithmetic  3.22 us (2%)
  between operations  2.16 us (2%)
    all_gather x1, blocking collectives, sum_over_dp(): lax.all_gather(part, 'dp', axis=0, axis_index_groups=far)  40.1 us
    all_to_all x2, blocking collectives, swap(): return lax.all_to_all(parts, axis, 0, 0, axis_index_groups=groups)  33.8 us
    ppermute x4, starting transfers between devices, passed_along(): lax.ppermute(array, axis, [(i, (i + by) % count) for i in range(count)])  17.6 us
    all_to_all x2, starting transfers between devices, swap(): return lax.all_to_all(parts, axis, 0, 0, axis_index_groups=groups)  17.2 us
    ppermute x4, waiting for transfers between devices, passed_along(): lax.ppermute(array, axis, [(i, (i + by) % count) for i in range(count)])  15.1 us
  transfers between devices with their start and end apart: 6, of which 3 were waited for; matrix products, arithmetic and copies ran while one was open for 3% of the time, Pallas kernels for 0%

profile of v2, /device:TPU:1, one launch (start us, length us, event | category | flops | bytes accessed | tf_op | source)
XLA Modules:
  0.0 138.7 jit_solution(2127258031119865193)
XLA Ops:
  0.6 0.0 copy-start
  0.6 1.3 copy-done
  1.9 1.5 %convolution_convert_fusion.1 = bf16[144,512]{1,0:T(8,128)(2,1)S(1)} fusion(bf16[1152,144]{0,1:T(8,128)(2,1)} %param.6, bf16[512,1152]{1,0:T(8,128)(2,1)S(1)} %copy-done), kind=kOutput, calls=%fused_computation.8 | convolution fusion | flops 169943040 | bytes 1658880 | tf_op jit(solution)/shard_map/dot_general | solution.py:72
  3.4 1.1 broadcast_in_dim.12
  4.5 6.1 %all-to-all-start = ((bf16[8,144,512]{2,1,0:T(8,128)(2,1)}), bf16[8,144,512]{2,1,0:T(8,128)(2,1)S(1)}, u32[]{:S(2)}, u32[]{:S(2)}) async-start(bf16[8,144,512]{2,1,0:T(8,128)(2,1)} %broadcast_in_dim.12), calls=%async_computation | async-start | bytes 2359296 | tf_op jit(solution)/shard_map/all_to_all | solution.py:29
  10.6 0.1 fusion.10
  10.7 0.1 fusion.6
  10.9 3.5 %collective-permute-start.1 = (bf16[64,1152]{1,0:T(8,128)(2,1)S(1)}, bf16[64,1152]{1,0:T(8,128)(2,1)S(1)}, u32[]{:S(2)}, u32[]{:S(2)}) collective-permute-start(bf16[64,1152]{1,0:T(8,128)(2,1)S(1)} %fusion.6), channel_id=1, source_target_pairs={{0,16},{8,24},{16,32},{24,40},{32,48},{40,56},{48,64},{56,72},{64,... | collective-permute-start | bytes 442376 | tf_op jit(solution)/shard_map/ppermute | solution.py:14
  14.4 4.7 %collective-permute-start = (bf16[64,1152]{1,0:T(8,128)(2,1)S(1)}, bf16[64,1152]{1,0:T(8,128)(2,1)S(1)}, u32[]{:S(2)}, u32[]{:S(2)}) collective-permute-start(bf16[64,1152]{1,0:T(8,128)(2,1)S(1)} %fusion.6), channel_id=1, source_target_pairs={{0,8},{8,16},{16,24},{24,32},{32,40},{40,48},{48,56},{56,64},{64,7... | collective-permute-start | bytes 442376 | tf_op jit(solution)/shard_map/ppermute | solution.py:14
  20.4 1.3 all-to-all-done
  21.7 0.3 multiply_reduce_fusion
  22.0 0.4 fusion.2
  22.4 12.2 %collective-permute-done.1 = bf16[64,1152]{1,0:T(8,128)(2,1)S(1)} collective-permute-done((bf16[64,1152]{1,0:T(8,128)(2,1)S(1)}, bf16[64,1152]{1,0:T(8,128)(2,1)S(1)}, u32[]{:S(2)}, u32[]{:S(2)}) %collective-permute-start.1) | collective-permute-done | bytes 147488 | tf_op jit(solution)/shard_map/ppermute | solution.py:14
  34.7 0.6 multiply_reduce_fusion.1
  35.3 0.0 copy-start.4
  35.3 0.7 fusion.1
  36.0 16.6 %all_to_all.20 = bf16[8,144,512]{2,1,0:T(8,128)(2,1)S(1)} all-to-all(bf16[8,144,512]{2,1,0:T(8,128)(2,1)S(1)} %bitcast.35), channel_id=1, replica_groups=mesh['dp'=128,'emb'=8] {'emb'}, dimensions={0} | all-to-all | bytes 2359296 | tf_op jit(solution)/shard_map/all_to_all | solution.py:29
  52.7 0.2 reduce_sum.75
  52.8 0.4 convolution_convert_fusion
  53.4 17.1 %all_to_all.21 = bf16[8,168,128]{2,1,0:T(8,128)(2,1)S(1)} all-to-all(bf16[8,168,128]{2,1,0:T(8,128)(2,1)S(1)} %bitcast.32), channel_id=1, replica_groups={{0,8,16,24,512,520,528,536},{32,40,48,56,544,552,560,568},{64,72,80,88,..., dimensions={0} | all-to-all | bytes 688128 | tf_op jit(solution)/shard_map/all_to_all | solution.py:29
  70.5 0.1 reduce_sum.76
  70.6 40.1 %all-gather = bf16[2688,128]{1,0:T(8,128)(2,1)S(1)} all-gather(bf16[168,128]{1,0:T(8,128)(2,1)S(1)} %reduce_sum.76), channel_id=2, replica_groups={{0,32,64,96,128,160,192,224,256,288,320,352,384,416,448,480},{8,40,72,1..., dimensions={0}, use_global_device_ids=true | all-gather | bytes 731136 | tf_op jit(solution)/shard_map/all_gather | solution.py:51
  110.7 0.1 reduce_sum.77
  110.8 0.8 broadcast_in_dim.15
  111.6 11.2 %all-to-all-start.3 = ((bf16[8,168,128]{2,1,0:T(8,128)(2,1)}), bf16[8,168,128]{2,1,0:T(8,128)(2,1)S(1)}, u32[]{:S(2)}, u32[]{:S(2)}) async-start(bf16[8,168,128]{2,1,0:T(8,128)(2,1)} %broadcast_in_dim.15), calls=%async_computation.3 | async-start | bytes 688128 | tf_op jit(solution)/shard_map/all_to_all | solution.py:29
  122.8 1.7 %fusion.16 = (bf16[192,1152]{1,0:T(8,128)(2,1)S(1)}, f32[192,1152]{1,0:T(8,128)S(1)}) fusion(bf16[1152,512]{1,0:T(8,128)(2,1)S(1)} %copy-done.3, f32[192,512]{1,0:T(8,128)} %copy-done.4, f32[]{:T(128)} %bitcast.29, f32[]{:T(128)} %bitcast.26, s32[192]{0:T(256)S(1)} %iota_add_fusion, pred[192]{0:T(512)(128)(4,1)S(1)} %iota_compare_fusion.1), kind=kOutput, calls=%fused_computation.45 | convolution fusion | flops 228114432 | bytes 2900936 | tf_op jit(solution)/shard_map/dot_general | solution.py:90
  124.5 2.0 %collective-permute-start.2 = (bf16[64,1152]{1,0:T(8,128)(2,1)S(1)}, bf16[64,1152]{1,0:T(8,128)(2,1)S(1)}, u32[]{:S(2)}, u32[]{:S(2)}) collective-permute-start(bf16[64,1152]{1,0:T(8,128)(2,1)S(1)} %get-tuple-element.4), channel_id=1, source_target_pairs={{0,1016},{8,0},{16,8},{24,16},{32,24},{40,32},{48,40},{56,48},{64,... | collective-permute-start | bytes 442376 | tf_op jit(solution)/shard_map/ppermute | solution.py:14
  126.5 7.3 %collective-permute-start.3 = (bf16[64,1152]{1,0:T(8,128)(2,1)S(1)}, bf16[64,1152]{1,0:T(8,128)(2,1)S(1)}, u32[]{:S(2)}, u32[]{:S(2)}) collective-permute-start(bf16[64,1152]{1,0:T(8,128)(2,1)S(1)} %get-tuple-element.5), channel_id=1, source_target_pairs={{0,1008},{8,1016},{16,0},{24,8},{32,16},{40,24},{48,32},{56,40},{6... | collective-permute-start | bytes 442376 | tf_op jit(solution)/shard_map/ppermute | solution.py:14
  133.9 2.9 %collective-permute-done.3 = bf16[64,1152]{1,0:T(8,128)(2,1)S(1)} collective-permute-done((bf16[64,1152]{1,0:T(8,128)(2,1)S(1)}, bf16[64,1152]{1,0:T(8,128)(2,1)S(1)}, u32[]{:S(2)}, u32[]{:S(2)}) %collective-permute-start.3) | collective-permute-done | bytes 147488 | tf_op jit(solution)/shard_map/ppermute | solution.py:14
  136.8 0.2 fusion.7
  137.0 0.8 fusion.9
  137.9 0.9 copy_bitcast_fusion
  (26 shorter events, 0.2 us)
Async XLA Ops:
  0.6 1.3 copy-start
  4.5 6.1 %copy-start.1 = (bf16[64,1152]{1,0:T(8,128)(2,1)S(1)}, bf16[64,1152]{1,0:T(8,128)(2,1)}, u32[]{:S(2)}) copy-start(bf16[64,1152]{1,0:T(8,128)(2,1)} %param.7) | copy-start | bytes 442372
  4.5 17.2 %all-to-all-start = ((bf16[8,144,512]{2,1,0:T(8,128)(2,1)}), bf16[8,144,512]{2,1,0:T(8,128)(2,1)S(1)}, u32[]{:S(2)}, u32[]{:S(2)}) async-start(bf16[8,144,512]{2,1,0:T(8,128)(2,1)} %broadcast_in_dim.12), calls=%async_computation | async-start | bytes 2359296 | tf_op jit(solution)/shard_map/all_to_all | solution.py:29
  10.9 23.8 %collective-permute-start.1 = (bf16[64,1152]{1,0:T(8,128)(2,1)S(1)}, bf16[64,1152]{1,0:T(8,128)(2,1)S(1)}, u32[]{:S(2)}, u32[]{:S(2)}) collective-permute-start(bf16[64,1152]{1,0:T(8,128)(2,1)S(1)} %fusion.6), channel_id=1, source_target_pairs={{0,16},{8,24},{16,32},{24,40},{32,48},{40,56},{48,64},{56,72},{64,... | collective-permute-start | bytes 442376 | tf_op jit(solution)/shard_map/ppermute | solution.py:14
  14.4 20.3 %collective-permute-start = (bf16[64,1152]{1,0:T(8,128)(2,1)S(1)}, bf16[64,1152]{1,0:T(8,128)(2,1)S(1)}, u32[]{:S(2)}, u32[]{:S(2)}) collective-permute-start(bf16[64,1152]{1,0:T(8,128)(2,1)S(1)} %fusion.6), channel_id=1, source_target_pairs={{0,8},{8,16},{16,24},{24,32},{32,40},{40,48},{48,56},{56,64},{64,7... | collective-permute-start | bytes 442376 | tf_op jit(solution)/shard_map/ppermute | solution.py:14
  22.4 12.8 %copy-start.2 = (bf16[1152,512]{1,0:T(8,128)(2,1)}, bf16[1152,512]{1,0:T(8,128)(2,1)S(1)}, u32[]{:S(2)}) copy-start(bf16[1152,512]{1,0:T(8,128)(2,1)S(1)} %get-tuple-element.2) | copy-start | bytes 3538948
  35.3 0.8 copy-start.4
  70.6 52.2 %copy-start.3 = (bf16[1152,512]{1,0:T(8,128)(2,1)S(1)}, bf16[1152,512]{1,0:T(8,128)(2,1)}, u32[]{:S(2)}) copy-start(bf16[1152,512]{1,0:T(8,128)(2,1)} %copy-done.2) | copy-start | bytes 3538948
  111.6 26.2 %all-to-all-start.3 = ((bf16[8,168,128]{2,1,0:T(8,128)(2,1)}), bf16[8,168,128]{2,1,0:T(8,128)(2,1)S(1)}, u32[]{:S(2)}, u32[]{:S(2)}) async-start(bf16[8,168,128]{2,1,0:T(8,128)(2,1)} %broadcast_in_dim.15), calls=%async_computation.3 | async-start | bytes 688128 | tf_op jit(solution)/shard_map/all_to_all | solution.py:29
  124.5 9.4 %collective-permute-start.2 = (bf16[64,1152]{1,0:T(8,128)(2,1)S(1)}, bf16[64,1152]{1,0:T(8,128)(2,1)S(1)}, u32[]{:S(2)}, u32[]{:S(2)}) collective-permute-start(bf16[64,1152]{1,0:T(8,128)(2,1)S(1)} %get-tuple-element.4), channel_id=1, source_target_pairs={{0,1016},{8,0},{16,8},{24,16},{32,24},{40,32},{48,40},{56,48},{64,... | collective-permute-start | bytes 442376 | tf_op jit(solution)/shard_map/ppermute | solution.py:14
  126.5 10.3 %collective-permute-start.3 = (bf16[64,1152]{1,0:T(8,128)(2,1)S(1)}, bf16[64,1152]{1,0:T(8,128)(2,1)S(1)}, u32[]{:S(2)}, u32[]{:S(2)}) collective-permute-start(bf16[64,1152]{1,0:T(8,128)(2,1)S(1)} %get-tuple-element.5), channel_id=1, source_target_pairs={{0,1008},{8,1016},{16,0},{24,8},{32,16},{40,24},{48,32},{56,40},{6... | collective-permute-start | bytes 442376 | tf_op jit(solution)/shard_map/ppermute | solution.py:14

commit v3 on v2

--- a/solution.py
+++ b/solution.py
@@ -37,7 +37,7 @@
     return jnp.sum(parts.astype(jnp.float32), axis=0)
 
 
-def sum_over_dp(grad_t):
+def sum_over_dp(grad_t, early):
     width, features = grad_t.shape
     tiles = features // LANES
     near, far = dp_groups(lax.axis_size("dp"))
@@ -48,10 +48,11 @@
     ).astype(jnp.bfloat16)
     rows = jnp.pad(rows, ((0, count * share - tiles * width), (0, 0)))
     part = summed(swap(rows.reshape(count, share, LANES), "dp", near)).astype(jnp.bfloat16)
+    part, early = lax.optimization_barrier((part, early))
     total = summed(lax.all_gather(part, "dp", axis=0, axis_index_groups=far)).astype(jnp.bfloat16)
     whole = gathered(total, count, "dp", near).reshape(count * share, LANES)[: tiles * width]
     whole = whole.astype(jnp.float32).reshape(tiles, width, LANES)
-    return jnp.swapaxes(whole, 1, 2).reshape(features, width)
+    return jnp.swapaxes(whole, 1, 2).reshape(features, width), early
 
 
 def local(img_feat, w_proj, txt_emb, logit_scale, logit_bias):
@@ -102,7 +103,7 @@
     parts = grad_proj.astype(jnp.bfloat16).reshape(members, width, image_rows)
     grad_part = summed(swap(parts, "emb")).astype(jnp.bfloat16)
     local_weight = jnp.dot(grad_part, img_feat, preferred_element_type=jnp.float32)
-    d_weight = sum_over_dp(local_weight)
+    d_weight, sent = sum_over_dp(local_weight, sent)
 
     grad_txt = txt_terms[:text_rows]
     for term in sent:

time: 139 us -> 140 us (level)
  blocking collectives: 73.9 us -> 47 us
  starting transfers between devices: 34.8 us -> 52.9 us
  waiting for transfers between devices: 16.4 us -> 23.9 us
    all_to_all x2 -> x1, blocking collectives: 33.8 us -> 16.6 us  [swap(): return lax.all_to_all(parts, axis, 0, 0, axis_index_groups=groups)]
    all_gather x1, blocking collectives: 40.1 us -> 30.4 us  [sum_over_dp(): lax.all_gather(part, 'dp', axis=0, axis_index_groups=far)]
    all_to_all x2 -> x3, starting transfers between devices: 17.2 us -> 26.7 us  [swap(): return lax.all_to_all(parts, axis, 0, 0, axis_index_groups=groups)]
    ppermute x4, starting transfers between devices: 17.6 us -> 26.2 us  [passed_along(): lax.ppermute(array, axis, [(i, (i + by) % count) for i in range(count)])]
    all_to_all x2 -> x3, waiting for transfers between devices: 1.29 us -> 7.79 us  [swap(): return lax.all_to_all(parts, axis, 0, 0, axis_index_groups=groups)]
  transfers between devices with their start and end apart: 6 -> 7, of which waited for: 3 -> 5; matrix products, arithmetic and copies ran while one was open for 3% -> 3% of each run, Pallas kernels for 0% -> 0%
where the time goes in v3:
time: 140 us; the launch traced here: 139 us
  starting transfers between devices  52.9 us (38%)
  blocking collectives  47 us (34%)
  waiting for transfers between devices  23.9 us (17%)
  matrix products  5.75 us (4%)
  local copies, waits for them, and re-layouts  4.09 us (3%)
  other arithmetic  3.22 us (2%)
  between operations  2.16 us (2%)
    all_gather x1, blocking collectives, sum_over_dp(): lax.all_gather(part, 'dp', axis=0, axis_index_groups=far)  30.4 us
    all_to_all x3, starting transfers between devices, swap(): return lax.all_to_all(parts, axis, 0, 0, axis_index_groups=groups)  26.7 us
    ppermute x4, starting transfers between devices, passed_along(): lax.ppermute(array, axis, [(i, (i + by) % count) for i in range(count)])  26.2 us
    all_to_all x1, blocking collectives, swap(): return lax.all_to_all(parts, axis, 0, 0, axis_index_groups=groups)  16.6 us
    ppermute x4, waiting for transfers between devices, passed_along(): lax.ppermute(array, axis, [(i, (i + by) % count) for i in range(count)])  16.1 us
    all_to_all x3, waiting for transfers between devices, swap(): return lax.all_to_all(parts, axis, 0, 0, axis_index_groups=groups)  7.79 us
  transfers between devices with their start and end apart: 7, of which 5 were waited for; matrix products, arithmetic and copies ran while one was open for 3% of the time, Pallas kernels for 0%

profile of v3, /device:TPU:1, one launch (start us, length us, event | category | flops | bytes accessed | tf_op | source)
XLA Modules:
  0.0 139.0 jit_solution(3195508909840219341)
XLA Ops:
  0.6 1.3 copy-done
  1.9 1.5 %convolution_convert_fusion.1 = bf16[144,512]{1,0:T(8,128)(2,1)S(1)} fusion(bf16[1152,144]{0,1:T(8,128)(2,1)} %param.6, bf16[512,1152]{1,0:T(8,128)(2,1)S(1)} %copy-done), kind=kOutput, calls=%fused_computation.8 | convolution fusion | flops 169943040 | bytes 1658880 | tf_op jit(solution)/shard_map/dot_general | solution.py:73
  3.4 1.1 broadcast_in_dim.12
  4.5 6.1 %all-to-all-start = ((bf16[8,144,512]{2,1,0:T(8,128)(2,1)}), bf16[8,144,512]{2,1,0:T(8,128)(2,1)S(1)}, u32[]{:S(2)}, u32[]{:S(2)}) async-start(bf16[8,144,512]{2,1,0:T(8,128)(2,1)} %broadcast_in_dim.12), calls=%async_computation | async-start | bytes 2359296 | tf_op jit(solution)/shard_map/all_to_all | solution.py:29
  10.6 0.1 fusion.10
  10.7 0.1 fusion.6
  10.9 3.5 %collective-permute-start.1 = (bf16[64,1152]{1,0:T(8,128)(2,1)S(1)}, bf16[64,1152]{1,0:T(8,128)(2,1)S(1)}, u32[]{:S(2)}, u32[]{:S(2)}) collective-permute-start(bf16[64,1152]{1,0:T(8,128)(2,1)S(1)} %fusion.6), channel_id=1, source_target_pairs={{0,16},{8,24},{16,32},{24,40},{32,48},{40,56},{48,64},{56,72},{64,... | collective-permute-start | bytes 442376 | tf_op jit(solution)/shard_map/ppermute | solution.py:14
  14.4 4.7 %collective-permute-start = (bf16[64,1152]{1,0:T(8,128)(2,1)S(1)}, bf16[64,1152]{1,0:T(8,128)(2,1)S(1)}, u32[]{:S(2)}, u32[]{:S(2)}) collective-permute-start(bf16[64,1152]{1,0:T(8,128)(2,1)S(1)} %fusion.6), channel_id=1, source_target_pairs={{0,8},{8,16},{16,24},{24,32},{32,40},{40,48},{48,56},{56,64},{64,7... | collective-permute-start | bytes 442376 | tf_op jit(solution)/shard_map/ppermute | solution.py:14
  20.4 1.3 all-to-all-done
  21.7 0.3 multiply_reduce_fusion
  22.0 0.4 fusion.2
  22.4 12.2 %collective-permute-done.1 = bf16[64,1152]{1,0:T(8,128)(2,1)S(1)} collective-permute-done((bf16[64,1152]{1,0:T(8,128)(2,1)S(1)}, bf16[64,1152]{1,0:T(8,128)(2,1)S(1)}, u32[]{:S(2)}, u32[]{:S(2)}) %collective-permute-start.1) | collective-permute-done | bytes 147488 | tf_op jit(solution)/shard_map/ppermute | solution.py:14
  34.7 0.6 multiply_reduce_fusion.1
  35.3 0.7 fusion.1
  36.0 16.6 %all_to_all.20 = bf16[8,144,512]{2,1,0:T(8,128)(2,1)S(1)} all-to-all(bf16[8,144,512]{2,1,0:T(8,128)(2,1)S(1)} %bitcast.34), channel_id=1, replica_groups=mesh['dp'=128,'emb'=8] {'emb'}, dimensions={0} | all-to-all | bytes 2359296 | tf_op jit(solution)/shard_map/all_to_all | solution.py:29
  52.6 0.2 reduce_sum.75
  52.8 0.4 convolution_convert_fusion
  53.3 0.8 pad.4
  54.1 8.9 %all-to-all-start.2 = ((bf16[8,168,128]{2,1,0:T(8,128)(2,1)}), bf16[8,168,128]{2,1,0:T(8,128)(2,1)S(1)}, u32[]{:S(2)}, u32[]{:S(2)}) async-start(bf16[8,168,128]{2,1,0:T(8,128)(2,1)} %bitcast.4), calls=%async_computation.2 | async-start | bytes 688128 | tf_op jit(solution)/shard_map/all_to_all | solution.py:29
  63.0 2.6 %fusion.16 = (bf16[192,1152]{1,0:T(8,128)(2,1)S(1)}, f32[192,1152]{1,0:T(8,128)}) fusion(bf16[1152,512]{1,0:T(8,128)(2,1)S(1)} %copy-done.3, f32[192,512]{1,0:T(8,128)} %copy-done.5, f32[]{:T(128)} %bitcast.29, f32[]{:T(128)} %bitcast.26, s32[192]{0:T(256)S(1)} %iota_add_fusion, pred[192]{0:T(512)(128)(4,1)S(1)} %iota_compare_fusion.1), kind=kOutput, calls=%fused_computation.45 | convolution fusion | flops 228114432 | bytes 2900936 | tf_op jit(solution)/shard_map/dot_general | solution.py:91
  65.6 15.5 %collective-permute-start.3 = (bf16[64,1152]{1,0:T(8,128)(2,1)S(1)}, bf16[64,1152]{1,0:T(8,128)(2,1)S(1)}, u32[]{:S(2)}, u32[]{:S(2)}) collective-permute-start(bf16[64,1152]{1,0:T(8,128)(2,1)S(1)} %get-tuple-element.10), channel_id=1, source_target_pairs={{0,1008},{8,1016},{16,0},{24,8},{32,16},{40,24},{48,32},{56,40},{6... | collective-permute-start | bytes 442376 | tf_op jit(solution)/shard_map/ppermute | solution.py:14
  81.1 2.5 %collective-permute-start.2 = (bf16[64,1152]{1,0:T(8,128)(2,1)S(1)}, bf16[64,1152]{1,0:T(8,128)(2,1)S(1)}, u32[]{:S(2)}, u32[]{:S(2)}) collective-permute-start(bf16[64,1152]{1,0:T(8,128)(2,1)S(1)} %get-tuple-element.11), channel_id=1, source_target_pairs={{0,1016},{8,0},{16,8},{24,16},{32,24},{40,32},{48,40},{56,48},{64,... | collective-permute-start | bytes 442376 | tf_op jit(solution)/shard_map/ppermute | solution.py:14
  83.7 0.2 collective-permute-done.3
  84.0 3.6 %collective-permute-done.2 = bf16[64,1152]{1,0:T(8,128)(2,1)S(1)} collective-permute-done((bf16[64,1152]{1,0:T(8,128)(2,1)S(1)}, bf16[64,1152]{1,0:T(8,128)(2,1)S(1)}, u32[]{:S(2)}, u32[]{:S(2)}) %collective-permute-start.2) | collective-permute-done | bytes 147488 | tf_op jit(solution)/shard_map/ppermute | solution.py:14
  87.6 30.4 %all-gather = bf16[2688,128]{1,0:T(8,128)(2,1)S(1)} all-gather(bf16[168,128]{1,0:T(8,128)(2,1)S(1)} %reduce_sum.76), channel_id=2, replica_groups={{0,32,64,96,128,160,192,224,256,288,320,352,384,416,448,480},{8,40,72,1..., dimensions={0}, use_global_device_ids=true | all-gather | bytes 731136 | tf_op jit(solution)/shard_map/all_gather | solution.py:52
  118.0 0.1 reduce_sum.77
  118.1 0.8 broadcast_in_dim.15
  118.9 11.7 %all-to-all-start.3 = ((bf16[8,168,128]{2,1,0:T(8,128)(2,1)}), bf16[8,168,128]{2,1,0:T(8,128)(2,1)S(1)}, u32[]{:S(2)}, u32[]{:S(2)}) async-start(bf16[8,168,128]{2,1,0:T(8,128)(2,1)} %broadcast_in_dim.15), calls=%async_computation.3 | async-start | bytes 688128 | tf_op jit(solution)/shard_map/all_to_all | solution.py:29
  130.6 0.2 fusion.7
  130.8 0.8 fusion.9
  131.6 6.5 %all-to-all-done.3 = bf16[8,168,128]{2,1,0:T(8,128)(2,1)S(1)} async-done(((bf16[8,168,128]{2,1,0:T(8,128)(2,1)}), bf16[8,168,128]{2,1,0:T(8,128)(2,1)S(1)}, u32[]{:S(2)}, u32[]{:S(2)}) %all-to-all-start.3) | async-done | bytes 344096 | tf_op jit(solution)/shard_map/all_to_all | solution.py:29
  138.2 0.9 copy_bitcast_fusion
  (29 shorter events, 0.3 us)
Async XLA Ops:
  0.6 1.3 copy-start
  4.5 6.1 %copy-start.1 = (bf16[64,1152]{1,0:T(8,128)(2,1)S(1)}, bf16[64,1152]{1,0:T(8,128)(2,1)}, u32[]{:S(2)}) copy-start(bf16[64,1152]{1,0:T(8,128)(2,1)} %param.7) | copy-start | bytes 442372
  4.5 17.2 %all-to-all-start = ((bf16[8,144,512]{2,1,0:T(8,128)(2,1)}), bf16[8,144,512]{2,1,0:T(8,128)(2,1)S(1)}, u32[]{:S(2)}, u32[]{:S(2)}) async-start(bf16[8,144,512]{2,1,0:T(8,128)(2,1)} %broadcast_in_dim.12), calls=%async_computation | async-start | bytes 2359296 | tf_op jit(solution)/shard_map/all_to_all | solution.py:29
  10.9 23.8 %collective-permute-start.1 = (bf16[64,1152]{1,0:T(8,128)(2,1)S(1)}, bf16[64,1152]{1,0:T(8,128)(2,1)S(1)}, u32[]{:S(2)}, u32[]{:S(2)}) collective-permute-start(bf16[64,1152]{1,0:T(8,128)(2,1)S(1)} %fusion.6), channel_id=1, source_target_pairs={{0,16},{8,24},{16,32},{24,40},{32,48},{40,56},{48,64},{56,72},{64,... | collective-permute-start | bytes 442376 | tf_op jit(solution)/shard_map/ppermute | solution.py:14
  14.4 20.3 %collective-permute-start = (bf16[64,1152]{1,0:T(8,128)(2,1)S(1)}, bf16[64,1152]{1,0:T(8,128)(2,1)S(1)}, u32[]{:S(2)}, u32[]{:S(2)}) collective-permute-start(bf16[64,1152]{1,0:T(8,128)(2,1)S(1)} %fusion.6), channel_id=1, source_target_pairs={{0,8},{8,16},{16,24},{24,32},{32,40},{40,48},{48,56},{56,64},{64,7... | collective-permute-start | bytes 442376 | tf_op jit(solution)/shard_map/ppermute | solution.py:14
  22.4 12.8 %copy-start.2 = (bf16[1152,512]{1,0:T(8,128)(2,1)}, bf16[1152,512]{1,0:T(8,128)(2,1)S(1)}, u32[]{:S(2)}) copy-start(bf16[1152,512]{1,0:T(8,128)(2,1)S(1)} %get-tuple-element.8) | copy-start | bytes 3538948
  35.3 0.7 copy-start.5
  53.2 9.8 %copy-start.3 = (bf16[1152,512]{1,0:T(8,128)(2,1)S(1)}, bf16[1152,512]{1,0:T(8,128)(2,1)}, u32[]{:S(2)}) copy-start(bf16[1152,512]{1,0:T(8,128)(2,1)} %copy-done.2) | copy-start | bytes 3538948
  54.1 29.5 %all-to-all-start.2 = ((bf16[8,168,128]{2,1,0:T(8,128)(2,1)}), bf16[8,168,128]{2,1,0:T(8,128)(2,1)S(1)}, u32[]{:S(2)}, u32[]{:S(2)}) async-start(bf16[8,168,128]{2,1,0:T(8,128)(2,1)} %bitcast.4), calls=%async_computation.2 | async-start | bytes 688128 | tf_op jit(solution)/shard_map/all_to_all | solution.py:29
  65.6 18.3 %collective-permute-start.3 = (bf16[64,1152]{1,0:T(8,128)(2,1)S(1)}, bf16[64,1152]{1,0:T(8,128)(2,1)S(1)}, u32[]{:S(2)}, u32[]{:S(2)}) collective-permute-start(bf16[64,1152]{1,0:T(8,128)(2,1)S(1)} %get-tuple-element.10), channel_id=1, source_target_pairs={{0,1008},{8,1016},{16,0},{24,8},{32,16},{40,24},{48,32},{56,40},{6... | collective-permute-start | bytes 442376 | tf_op jit(solution)/shard_map/ppermute | solution.py:14
  81.1 6.5 %collective-permute-start.2 = (bf16[64,1152]{1,0:T(8,128)(2,1)S(1)}, bf16[64,1152]{1,0:T(8,128)(2,1)S(1)}, u32[]{:S(2)}, u32[]{:S(2)}) collective-permute-start(bf16[64,1152]{1,0:T(8,128)(2,1)S(1)} %get-tuple-element.11), channel_id=1, source_target_pairs={{0,1016},{8,0},{16,8},{24,16},{32,24},{40,32},{48,40},{56,48},{64,... | collective-permute-start | bytes 442376 | tf_op jit(solution)/shard_map/ppermute | solution.py:14
  83.7 46.8 %copy-start.4 = (f32[192,1152]{1,0:T(8,128)S(1)}, f32[192,1152]{1,0:T(8,128)}, u32[]{:S(2)}) copy-start(f32[192,1152]{1,0:T(8,128)} %get-tuple-element.17) | copy-start | bytes 2654212
  118.9 19.3 %all-to-all-start.3 = ((bf16[8,168,128]{2,1,0:T(8,128)(2,1)}), bf16[8,168,128]{2,1,0:T(8,128)(2,1)S(1)}, u32[]{:S(2)}, u32[]{:S(2)}) async-start(bf16[8,168,128]{2,1,0:T(8,128)(2,1)} %broadcast_in_dim.15), calls=%async_computation.3 | async-start | bytes 688128 | tf_op jit(solution)/shard_map/all_to_all | solution.py:29

commit v4 on v3

--- a/solution.py
+++ b/solution.py
@@ -7,11 +7,16 @@
 EPSILON = 1e-06
 LANES = 128
 ROWS = 8
+PAIR = 2
 
 
 def passed_along(array, axis, by):
     count = lax.axis_size(axis)
     return lax.ppermute(array, axis, [(i, (i + by) % count) for i in range(count)])
+
+
+def to_partner(array):
+    return lax.ppermute(array, "emb", [(i, i ^ 1) for i in range(lax.axis_size("emb"))])
 
 
 def dp_groups(count):
@@ -43,10 +48,9 @@
     near, far = dp_groups(lax.axis_size("dp"))
     count = len(near[0])
     share = -(-tiles * width // (count * ROWS)) * ROWS
-    rows = jnp.concatenate(
-        [grad_t[:, LANES * t : LANES * (t + 1)] for t in range(tiles)], axis=0
-    ).astype(jnp.bfloat16)
-    rows = jnp.pad(rows, ((0, count * share - tiles * width), (0, 0)))
+    slabs = [grad_t[:, LANES * t : LANES * (t + 1)].astype(jnp.bfloat16) for t in range(tiles)]
+    slabs.append(jnp.zeros((count * share - tiles * width, LANES), jnp.bfloat16))
+    rows = jnp.concatenate(slabs, axis=0)
     part = summed(swap(rows.reshape(count, share, LANES), "dp", near)).astype(jnp.bfloat16)
     part, early = lax.optimization_barrier((part, early))
     total = summed(lax.all_gather(part, "dp", axis=0, axis_index_groups=far)).astype(jnp.bfloat16)
@@ -61,6 +65,8 @@
     width = w_proj.shape[1]
     members = lax.axis_size("emb")
     member = lax.axis_index("emb")
+    half_rows = image_rows // PAIR
+    half = member % PAIR
     scale = logit_scale[0]
     offset = logit_bias[0]
 
@@ -68,12 +74,15 @@
     inv_txt = lax.rsqrt(jnp.sum(wide_txt * wide_txt, axis=1, keepdims=True) + EPSILON)
     unit_txt = wide_txt * inv_txt
     z_txt = unit_txt.astype(jnp.bfloat16)
-    visitors = [z_txt] + [passed_along(z_txt, "dp", k) for k in range(1, STEPS)]
+    pair_txt = jnp.concatenate([z_txt, to_partner(z_txt)], axis=0)
+    visitors = [pair_txt] + [passed_along(pair_txt, "dp", k) for k in range(1, STEPS)]
 
     local_proj = lax.dot_general(
         w_proj, img_feat, (((0,), (1,)), ((), ())), preferred_element_type=jnp.float32
     ).astype(jnp.bfloat16)
-    projected = gathered(local_proj, members, "emb").reshape(features, image_rows)
+    halves = jnp.stack([local_proj[:, h * half_rows : (h + 1) * half_rows] for h in range(PAIR)])
+    halves = jnp.broadcast_to(halves[None], (members // PAIR,) + halves.shape)
+    projected = swap(halves.reshape(members, width, half_rows), "emb").reshape(features, half_rows)
     wide_img = projected.astype(jnp.float32)
     inv_img = lax.rsqrt(jnp.sum(wide_img * wide_img, axis=0, keepdims=True) + EPSILON)
     unit_img = wide_img * inv_img
@@ -82,30 +91,37 @@
     texts = jnp.concatenate(visitors, axis=0)
     cosines = jnp.dot(texts, z_img, preferred_element_type=jnp.float32)
     text_index = lax.broadcasted_iota(jnp.int32, cosines.shape, 0)
-    image_index = lax.broadcasted_iota(jnp.int32, cosines.shape, 1)
-    own = (text_index < text_rows) & (image_index == member * text_rows + text_index)
-    signs = jnp.where(own, 1.0, -1.0)
+    image_index = lax.broadcasted_iota(jnp.int32, cosines.shape, 1) + half * half_rows
+    partners = (image_index == (member ^ 1) * text_rows + text_index - text_rows) & (
+        (text_index >= text_rows) & (text_index < PAIR * text_rows)
+    )
+    own = (image_index == member * text_rows + text_index) & (text_index < text_rows)
+    signs = jnp.where(own | partners, 1.0, -1.0)
     pair_grad = (-signs * jax.nn.sigmoid(-signs * (scale * cosines + offset))).astype(jnp.bfloat16)
     inner_img = jnp.sum(pair_grad.astype(jnp.float32) * cosines, axis=0, keepdims=True)
 
     txt_terms = scale * lax.dot_general(
         pair_grad, z_img, (((1,), (1,)), ((), ())), preferred_element_type=jnp.float32
     )
-    sent = [
-        passed_along(txt_terms[k * text_rows : (k + 1) * text_rows].astype(jnp.bfloat16), "dp", -k)
-        for k in range(1, STEPS)
-    ]
+    txt_terms = txt_terms.reshape(STEPS, PAIR, text_rows, features)
+    other_terms = to_partner(txt_terms[:, 1].astype(jnp.bfloat16))
 
     grad_img = lax.dot_general(
         texts, pair_grad, (((0,), (0,)), ((), ())), preferred_element_type=jnp.float32
     )
     grad_proj = (scale * inv_img) * (grad_img - unit_img * inner_img)
-    parts = grad_proj.astype(jnp.bfloat16).reshape(members, width, image_rows)
-    grad_part = summed(swap(parts, "emb")).astype(jnp.bfloat16)
+    parts = grad_proj.astype(jnp.bfloat16).reshape(members, width, half_rows)
+    parts = swap(parts, "emb").reshape(members // PAIR, PAIR, width, half_rows)
+    grad_part = summed(parts).astype(jnp.bfloat16)
+    grad_part, other_terms = lax.optimization_barrier((grad_part, other_terms))
+    grad_part = jnp.concatenate([grad_part[h] for h in range(PAIR)], axis=1)
     local_weight = jnp.dot(grad_part, img_feat, preferred_element_type=jnp.float32)
+
+    txt_terms = txt_terms[:, 0] + other_terms.astype(jnp.float32)
+    sent = [passed_along(txt_terms[k].astype(jnp.bfloat16), "dp", -k) for k in range(1, STEPS)]
     d_weight, sent = sum_over_dp(local_weight, sent)
 
-    grad_txt = txt_terms[:text_rows]
+    grad_txt = txt_terms[0]
     for term in sent:
         grad_txt = grad_txt + term.astype(jnp.float32)
     inner_txt = jnp.sum(unit_txt * grad_txt, axis=1, keepdims=True)

time: 140 us -> 157 us (1.12)
  blocking collectives: 47 us -> 28.7 us
  waiting for transfers between devices: 23.9 us -> 37.6 us
  starting transfers between devices: 52.9 us -> 65.2 us
  local copies, waits for them, and re-layouts: 4.09 us -> 10.4 us
  matrix products: 5.75 us -> 7.72 us
    all_to_all x1 -> x0, blocking collectives: 16.6 us -> none  [swap(): return lax.all_to_all(parts, axis, 0, 0, axis_index_groups=groups)]
    ppermute x0 -> x2, waiting for transfers between devices: none -> 10 us  [to_partner(): lax.ppermute(array, 'emb', [(i, i ^ 1) for i in range(lax.axis_size('emb'...]
    all_to_all x3 -> x4, starting transfers between devices: 26.7 us -> 36.2 us  [swap(): return lax.all_to_all(parts, axis, 0, 0, axis_index_groups=groups)]
    ppermute x0 -> x2, starting transfers between devices: none -> 6.72 us  [to_partner(): lax.ppermute(array, 'emb', [(i, i ^ 1) for i in range(lax.axis_size('emb'...]
    unnamed x20 -> x17, local copies, waits for them, and re-layouts: 1.37 us -> 8.02 us
    ppermute x4, starting transfers between devices: 26.2 us -> 22.3 us  [passed_along(): lax.ppermute(array, axis, [(i, (i + by) % count) for i in range(count)])]
    ppermute x4, waiting for transfers between devices: 16.1 us -> 19.3 us  [passed_along(): lax.ppermute(array, axis, [(i, (i + by) % count) for i in range(count)])]
    dot_general x1, matrix products: 0.73 us -> 2.7 us  [local(): lax.dot_general(texts, pair_grad, (((0,), (0,)), ((), ())), preferred_ele...]
  transfers between devices with their start and end apart: 7 -> 10, of which waited for: 5 -> 6; matrix products, arithmetic and copies ran while one was open for 3% -> 3% of each run, Pallas kernels for 0% -> 0%
where the time goes in v4:
time: 157 us; the launch traced here: 156 us
  starting transfers between devices  65.2 us (42%)
  waiting for transfers between devices  37.6 us (24%)
  blocking collectives  28.7 us (18%)
  local copies, waits for them, and re-layouts  10.4 us (7%)
  matrix products  7.72 us (5%)
  other arithmetic  4.09 us (3%)
  between operations  2.18 us (1%)
    all_to_all x4, starting transfers between devices, swap(): return lax.all_to_all(parts, axis, 0, 0, axis_index_groups=groups)  36.2 us
    all_gather x1, blocking collectives, sum_over_dp(): lax.all_gather(part, 'dp', axis=0, axis_index_groups=far)  28.7 us
    ppermute x4, starting transfers between devices, passed_along(): lax.ppermute(array, axis, [(i, (i + by) % count) for i in range(count)])  22.3 us
    ppermute x4, waiting for transfers between devices, passed_along(): lax.ppermute(array, axis, [(i, (i + by) % count) for i in range(count)])  19.3 us
    ppermute x2, waiting for transfers between devices, to_partner(): lax.ppermute(array, 'emb', [(i, i ^ 1) for i in range(lax.axis_size('emb'...  10 us
    all_to_all x4, waiting for transfers between devices, swap(): return lax.all_to_all(parts, axis, 0, 0, axis_index_groups=groups)  8.18 us
    unnamed x17, local copies, waits for them, and re-layouts  8.02 us
    ppermute x2, starting transfers between devices, to_partner(): lax.ppermute(array, 'emb', [(i, i ^ 1) for i in range(lax.axis_size('emb'...  6.72 us
  transfers between devices with their start and end apart: 10, of which 6 were waited for; matrix products, arithmetic and copies ran while one was open for 3% of the time, Pallas kernels for 0%

profile of v4, /device:TPU:1, one launch (start us, length us, event | category | flops | bytes accessed | tf_op | source)
XLA Modules:
  0.0 155.8 jit_solution(6222353014867292787)
XLA Ops:
  0.7 1.3 copy-done
  1.9 1.5 convolution_convert_fusion.1
  3.5 0.9 broadcast_in_dim.14
  4.3 5.9 %all-to-all-start = ((bf16[8,144,256]{2,1,0:T(8,128)(2,1)}), bf16[8,144,256]{2,1,0:T(8,128)(2,1)S(1)}, u32[]{:S(2)}, u32[]{:S(2)}) async-start(bf16[8,144,256]{2,1,0:T(8,128)(2,1)} %bitcast.3), calls=%async_computation | async-start | bytes 1179648 | tf_op jit(solution)/shard_map/all_to_all | solution.py:34
  10.5 3.4 %collective-permute-start = (bf16[64,1152]{1,0:T(8,128)(2,1)S(1)}, bf16[64,1152]{1,0:T(8,128)(2,1)S(1)}, u32[]{:S(2)}, u32[]{:S(2)}) collective-permute-start(bf16[64,1152]{1,0:T(8,128)(2,1)S(1)} %fusion.7), channel_id=1, source_target_pairs={{0,1},{1,0},{2,3},{3,2},{4,5},{5,4},{6,7},{7,6},{8,9},{9,8},{10,11... | collective-permute-start | bytes 442376 | tf_op jit(solution)/shard_map/ppermute | solution.py:19
  15.2 2.4 %collective-permute-done = bf16[64,1152]{1,0:T(8,128)(2,1)S(1)} collective-permute-done((bf16[64,1152]{1,0:T(8,128)(2,1)S(1)}, bf16[64,1152]{1,0:T(8,128)(2,1)S(1)}, u32[]{:S(2)}, u32[]{:S(2)}) %collective-permute-start) | collective-permute-done | bytes 147488 | tf_op jit(solution)/shard_map/ppermute | solution.py:19
  17.6 7.1 %collective-permute-start.2 = (bf16[128,1152]{1,0:T(8,128)(2,1)S(1)}, bf16[128,1152]{1,0:T(8,128)(2,1)S(1)}, u32[]{:S(2)}, u32[]{:S(2)}) collective-permute-start(bf16[128,1152]{1,0:T(8,128)(2,1)S(1)} %pad_maximum_fusion.1), channel_id=1, source_target_pairs={{0,16},{8,24},{16,32},{24,40},{32,48},{40,56},{48,64},{56,72},{64,... | collective-permute-start | bytes 884744 | tf_op jit(solution)/shard_map/ppermute | solution.py:15
  24.8 5.6 %collective-permute-start.1 = (bf16[128,1152]{1,0:T(8,128)(2,1)S(1)}, bf16[128,1152]{1,0:T(8,128)(2,1)}, u32[]{:S(2)}, u32[]{:S(2)}) collective-permute-start(bf16[128,1152]{1,0:T(8,128)(2,1)S(1)} %pad_maximum_fusion.1), channel_id=1, source_target_pairs={{0,8},{8,16},{16,24},{24,32},{32,40},{40,48},{48,56},{56,64},{64,7... | collective-permute-start | bytes 884744 | tf_op jit(solution)/shard_map/ppermute | solution.py:15
  30.7 16.5 %collective-permute-done.2 = bf16[128,1152]{1,0:T(8,128)(2,1)S(1)} collective-permute-done((bf16[128,1152]{1,0:T(8,128)(2,1)S(1)}, bf16[128,1152]{1,0:T(8,128)(2,1)S(1)}, u32[]{:S(2)}, u32[]{:S(2)}) %collective-permute-start.2) | collective-permute-done | bytes 294944 | tf_op jit(solution)/shard_map/ppermute | solution.py:15
  47.2 1.5 multiply_reduce_fusion.1
  48.8 2.7 %fusion.1 = bf16[1152,256]{1,0:T(8,128)(2,1)} fusion(f32[1152,256]{1,0:T(8,128)S(1)} %get-tuple-element.15, f32[256]{0:T(256)S(1)} %get-tuple-element.24, f32[256]{0:T(256)S(1)} %get-tuple-element.22, bf16[128,1152]{1,0:T(8,128)(2,1)S(1)} %collective-permute-done.2, bf16[128,1152]{1,0:T(8,128)(2,1)} %collective-permute-done.1, ...), kind=kOutput, calls=%fused_computation.3 | convolution fusion | flops 232685568 | bytes 3054344 | tf_op jit(solution)/shard_map/dot_general | solution.py:109
  51.5 4.0 %all-to-all-start.1 = ((bf16[8,144,256]{2,1,0:T(8,128)(2,1)}), bf16[8,144,256]{2,1,0:T(8,128)(2,1)S(1)}, u32[]{:S(2)}, u32[]{:S(2)}) async-start(bf16[8,144,256]{2,1,0:T(8,128)(2,1)} %bitcast.6), calls=%async_computation.1 | async-start | bytes 1179648 | tf_op jit(solution)/shard_map/all_to_all | solution.py:34
  55.4 1.6 %convolution_multiply_fusion = f32[384,1152]{1,0:T(8,128)S(1)} fusion(bf16[1152,256]{1,0:T(8,128)(2,1)S(1)} %get-tuple-element.14, f32[]{:T(128)} %bitcast.57, f32[384,256]{1,0:T(8,128)} %copy-done.3, f32[]{:T(128)} %bitcast.60, s32[256]{0:T(256)S(1)} %iota_add_fusion.1, s32[384]{0:T(512)S(1)} %get-tuple-element.26, s32[384]{0:T(512)S(1)} %get-tuple-element.27, ...), kind=kOutput, calls=%fused_computation | convolution fusion | flops 228409344 | bytes 2757384 | tf_op jit(solution)/shard_map/dot_general | solution.py:103
  57.1 1.2 copy-done.2
  58.3 3.4 %collective-permute-start.3 = (bf16[3,64,1152]{2,1,0:T(8,128)(2,1)S(1)}, bf16[3,64,1152]{2,1,0:T(8,128)(2,1)S(1)}, u32[]{:S(2)}, u32[]{:S(2)}) collective-permute-start(bf16[3,64,1152]{2,1,0:T(8,128)(2,1)S(1)} %fusion.4), channel_id=1, source_target_pairs={{0,1},{1,0},{2,3},{3,2},{4,5},{5,4},{6,7},{7,6},{8,9},{9,8},{10,11... | collective-permute-start | bytes 1327112 | tf_op jit(solution)/shard_map/ppermute | solution.py:19
  61.7 1.7 %all-to-all-done.1 = bf16[8,144,256]{2,1,0:T(8,128)(2,1)S(1)} async-done(((bf16[8,144,256]{2,1,0:T(8,128)(2,1)}), bf16[8,144,256]{2,1,0:T(8,128)(2,1)S(1)}, u32[]{:S(2)}, u32[]{:S(2)}) %all-to-all-start.1) | async-done | bytes 589856 | tf_op jit(solution)/shard_map/all_to_all | solution.py:34
  63.4 7.7 %collective-permute-done.3 = bf16[3,64,1152]{2,1,0:T(8,128)(2,1)S(1)} collective-permute-done((bf16[3,64,1152]{2,1,0:T(8,128)(2,1)S(1)}, bf16[3,64,1152]{2,1,0:T(8,128)(2,1)S(1)}, u32[]{:S(2)}, u32[]{:S(2)}) %collective-permute-start.3) | collective-permute-done | bytes 442400 | tf_op jit(solution)/shard_map/ppermute | solution.py:19
  71.5 0.6 slice_dynamic-update-slice_fusion.8
  72.7 0.6 slice_dynamic-update-slice_fusion.6
  74.6 0.6 slice_dynamic-update-slice_fusion.3
  76.4 0.6 slice_dynamic-update-slice_fusion
  77.7 8.2 %all-to-all-start.2 = ((bf16[8,168,128]{2,1,0:T(8,128)(2,1)}), bf16[8,168,128]{2,1,0:T(8,128)(2,1)S(1)}, u32[]{:S(2)}, u32[]{:S(2)}) async-start(bf16[8,168,128]{2,1,0:T(8,128)(2,1)} %bitcast.12), calls=%async_computation.2 | async-start | bytes 688128 | tf_op jit(solution)/shard_map/all_to_all | solution.py:34
  85.8 1.3 fusion.22
  87.1 2.0 %collective-permute-start.4 = (bf16[64,1152]{1,0:T(8,128)(2,1)S(1)}, bf16[64,1152]{1,0:T(8,128)(2,1)S(1)}, u32[]{:S(2)}, u32[]{:S(2)}) collective-permute-start(bf16[64,1152]{1,0:T(8,128)(2,1)S(1)} %get-tuple-element.17), channel_id=1, source_target_pairs={{0,1016},{8,0},{16,8},{24,16},{32,24},{40,32},{48,40},{56,48},{64,... | collective-permute-start | bytes 442376 | tf_op jit(solution)/shard_map/ppermute | solution.py:15
  89.2 7.6 %collective-permute-start.5 = (bf16[64,1152]{1,0:T(8,128)(2,1)S(1)}, bf16[64,1152]{1,0:T(8,128)(2,1)S(1)}, u32[]{:S(2)}, u32[]{:S(2)}) collective-permute-start(bf16[64,1152]{1,0:T(8,128)(2,1)S(1)} %get-tuple-element.16), channel_id=1, source_target_pairs={{0,1008},{8,1016},{16,0},{24,8},{32,16},{40,24},{48,32},{56,40},{6... | collective-permute-start | bytes 442376 | tf_op jit(solution)/shard_map/ppermute | solution.py:15
  96.8 2.8 %collective-permute-done.5 = bf16[64,1152]{1,0:T(8,128)(2,1)S(1)} collective-permute-done((bf16[64,1152]{1,0:T(8,128)(2,1)S(1)}, bf16[64,1152]{1,0:T(8,128)(2,1)S(1)}, u32[]{:S(2)}, u32[]{:S(2)}) %collective-permute-start.5) | collective-permute-done | bytes 147488 | tf_op jit(solution)/shard_map/ppermute | solution.py:15
  99.7 28.7 %all-gather = bf16[2688,128]{1,0:T(8,128)(2,1)S(1)} all-gather(bf16[168,128]{1,0:T(8,128)(2,1)S(1)} %reduce_sum.76), channel_id=2, replica_groups={{0,32,64,96,128,160,192,224,256,288,320,352,384,416,448,480},{8,40,72,1..., dimensions={0}, use_global_device_ids=true | all-gather | bytes 731136 | tf_op jit(solution)/shard_map/all_gather | solution.py:56
  128.5 0.8 broadcast_in_dim.31
  129.2 18.1 %all-to-all-start.3 = ((bf16[8,168,128]{2,1,0:T(8,128)(2,1)}), bf16[8,168,128]{2,1,0:T(8,128)(2,1)S(1)}, u32[]{:S(2)}, u32[]{:S(2)}) async-start(bf16[8,168,128]{2,1,0:T(8,128)(2,1)} %broadcast_in_dim.31), calls=%async_computation.3 | async-start | bytes 688128 | tf_op jit(solution)/shard_map/all_to_all | solution.py:34
  147.5 0.8 fusion.10
  148.4 6.5 %all-to-all-done.3 = bf16[8,168,128]{2,1,0:T(8,128)(2,1)S(1)} async-done(((bf16[8,168,128]{2,1,0:T(8,128)(2,1)}), bf16[8,168,128]{2,1,0:T(8,128)(2,1)S(1)}, u32[]{:S(2)}, u32[]{:S(2)}) %all-to-all-start.3) | async-done | bytes 344096 | tf_op jit(solution)/shard_map/all_to_all | solution.py:34
  154.9 0.9 copy_bitcast_fusion.1
  (37 shorter events, 5.3 us)
Async XLA Ops:
  0.6 1.3 copy-start
  0.6 9.6 %copy-start.1 = (bf16[64,1152]{1,0:T(8,128)(2,1)S(1)}, bf16[64,1152]{1,0:T(8,128)(2,1)}, u32[]{:S(2)}) copy-start(bf16[64,1152]{1,0:T(8,128)(2,1)} %param.7) | copy-start | bytes 442372
  4.3 26.0 %all-to-all-start = ((bf16[8,144,256]{2,1,0:T(8,128)(2,1)}), bf16[8,144,256]{2,1,0:T(8,128)(2,1)S(1)}, u32[]{:S(2)}, u32[]{:S(2)}) async-start(bf16[8,144,256]{2,1,0:T(8,128)(2,1)} %bitcast.3), calls=%async_computation | async-start | bytes 1179648 | tf_op jit(solution)/shard_map/all_to_all | solution.py:34
  10.5 7.1 %collective-permute-start = (bf16[64,1152]{1,0:T(8,128)(2,1)S(1)}, bf16[64,1152]{1,0:T(8,128)(2,1)S(1)}, u32[]{:S(2)}, u32[]{:S(2)}) collective-permute-start(bf16[64,1152]{1,0:T(8,128)(2,1)S(1)} %fusion.7), channel_id=1, source_target_pairs={{0,1},{1,0},{2,3},{3,2},{4,5},{5,4},{6,7},{7,6},{8,9},{9,8},{10,11... | collective-permute-start | bytes 442376 | tf_op jit(solution)/shard_map/ppermute | solution.py:19
  17.6 29.6 %collective-permute-start.2 = (bf16[128,1152]{1,0:T(8,128)(2,1)S(1)}, bf16[128,1152]{1,0:T(8,128)(2,1)S(1)}, u32[]{:S(2)}, u32[]{:S(2)}) collective-permute-start(bf16[128,1152]{1,0:T(8,128)(2,1)S(1)} %pad_maximum_fusion.1), channel_id=1, source_target_pairs={{0,16},{8,24},{16,32},{24,40},{32,48},{40,56},{48,64},{56,72},{64,... | collective-permute-start | bytes 884744 | tf_op jit(solution)/shard_map/ppermute | solution.py:15
  24.8 22.5 %collective-permute-start.1 = (bf16[128,1152]{1,0:T(8,128)(2,1)S(1)}, bf16[128,1152]{1,0:T(8,128)(2,1)}, u32[]{:S(2)}, u32[]{:S(2)}) collective-permute-start(bf16[128,1152]{1,0:T(8,128)(2,1)S(1)} %pad_maximum_fusion.1), channel_id=1, source_target_pairs={{0,8},{8,16},{16,24},{24,32},{32,40},{40,48},{48,56},{56,64},{64,7... | collective-permute-start | bytes 884744 | tf_op jit(solution)/shard_map/ppermute | solution.py:15
  48.8 2.7 %copy-start.3 = (f32[384,256]{1,0:T(8,128)}, f32[384,256]{1,0:T(8,128)S(1)}, u32[]{:S(2)}) copy-start(f32[384,256]{1,0:T(8,128)S(1)} %get-tuple-element.25) | copy-start | bytes 1179652
  51.5 11.9 %all-to-all-start.1 = ((bf16[8,144,256]{2,1,0:T(8,128)(2,1)}), bf16[8,144,256]{2,1,0:T(8,128)(2,1)S(1)}, u32[]{:S(2)}, u32[]{:S(2)}) async-start(bf16[8,144,256]{2,1,0:T(8,128)(2,1)} %bitcast.6), calls=%async_computation.1 | async-start | bytes 1179648 | tf_op jit(solution)/shard_map/all_to_all | solution.py:34
  57.1 1.2 copy-start.2
  58.3 12.8 %collective-permute-start.3 = (bf16[3,64,1152]{2,1,0:T(8,128)(2,1)S(1)}, bf16[3,64,1152]{2,1,0:T(8,128)(2,1)S(1)}, u32[]{:S(2)}, u32[]{:S(2)}) collective-permute-start(bf16[3,64,1152]{2,1,0:T(8,128)(2,1)S(1)} %fusion.4), channel_id=1, source_target_pairs={{0,1},{1,0},{2,3},{3,2},{4,5},{5,4},{6,7},{7,6},{8,9},{9,8},{10,11... | collective-permute-start | bytes 1327112 | tf_op jit(solution)/shard_map/ppermute | solution.py:19
  77.7 19.1 %all-to-all-start.2 = ((bf16[8,168,128]{2,1,0:T(8,128)(2,1)}), bf16[8,168,128]{2,1,0:T(8,128)(2,1)S(1)}, u32[]{:S(2)}, u32[]{:S(2)}) async-start(bf16[8,168,128]{2,1,0:T(8,128)(2,1)} %bitcast.12), calls=%async_computation.2 | async-start | bytes 688128 | tf_op jit(solution)/shard_map/all_to_all | solution.py:34
  87.1 9.7 %collective-permute-start.4 = (bf16[64,1152]{1,0:T(8,128)(2,1)S(1)}, bf16[64,1152]{1,0:T(8,128)(2,1)S(1)}, u32[]{:S(2)}, u32[]{:S(2)}) collective-permute-start(bf16[64,1152]{1,0:T(8,128)(2,1)S(1)} %get-tuple-element.17), channel_id=1, source_target_pairs={{0,1016},{8,0},{16,8},{24,16},{32,24},{40,32},{48,40},{56,48},{64,... | collective-permute-start | bytes 442376 | tf_op jit(solution)/shard_map/ppermute | solution.py:15
  89.2 10.5 %collective-permute-start.5 = (bf16[64,1152]{1,0:T(8,128)(2,1)S(1)}, bf16[64,1152]{1,0:T(8,128)(2,1)S(1)}, u32[]{:S(2)}, u32[]{:S(2)}) collective-permute-start(bf16[64,1152]{1,0:T(8,128)(2,1)S(1)} %get-tuple-element.16), channel_id=1, source_target_pairs={{0,1008},{8,1016},{16,0},{24,8},{32,16},{40,24},{48,32},{56,40},{6... | collective-permute-start | bytes 442376 | tf_op jit(solution)/shard_map/ppermute | solution.py:15
  129.2 25.7 %all-to-all-start.3 = ((bf16[8,168,128]{2,1,0:T(8,128)(2,1)}), bf16[8,168,128]{2,1,0:T(8,128)(2,1)S(1)}, u32[]{:S(2)}, u32[]{:S(2)}) async-start(bf16[8,168,128]{2,1,0:T(8,128)(2,1)} %broadcast_in_dim.31), calls=%async_computation.3 | async-start | bytes 688128 | tf_op jit(solution)/shard_map/all_to_all | solution.py:34

commit v5 on v2

--- a/solution.py
+++ b/solution.py
@@ -101,6 +101,7 @@
     grad_proj = (scale * inv_img) * (grad_img - unit_img * inner_img)
     parts = grad_proj.astype(jnp.bfloat16).reshape(members, width, image_rows)
     grad_part = summed(swap(parts, "emb")).astype(jnp.bfloat16)
+    grad_part, sent = lax.optimization_barrier((grad_part, sent))
     local_weight = jnp.dot(grad_part, img_feat, preferred_element_type=jnp.float32)
     d_weight = sum_over_dp(local_weight)
 

time: 139 us -> 138 us (level)
  blocking collectives: 73.9 us -> 51.7 us
  starting transfers between devices: 34.8 us -> 47.5 us
  waiting for transfers between devices: 16.4 us -> 22.5 us
  matrix products: 4.83 us -> 7.04 us
    all_to_all x2 -> x1, blocking collectives: 33.8 us -> 10.9 us  [swap(): return lax.all_to_all(parts, axis, 0, 0, axis_index_groups=groups)]
    ppermute x4, starting transfers between devices: 17.6 us -> 25.6 us  [passed_along(): lax.ppermute(array, axis, [(i, (i + by) % count) for i in range(count)])]
    all_to_all x2 -> x3, waiting for transfers between devices: 1.29 us -> 7.82 us  [swap(): return lax.all_to_all(parts, axis, 0, 0, axis_index_groups=groups)]
    all_to_all x2 -> x3, starting transfers between devices: 17.2 us -> 21.9 us  [swap(): return lax.all_to_all(parts, axis, 0, 0, axis_index_groups=groups)]
  transfers between devices with their start and end apart: 6 -> 7, of which waited for: 3 -> 4; matrix products, arithmetic and copies ran while one was open for 3% -> 4% of each run, Pallas kernels for 0% -> 0%
where the time goes in v5:
time: 138 us; the launch traced here: 137 us
  blocking collectives  51.7 us (37%)
  starting transfers between devices  47.5 us (34%)
  waiting for transfers between devices  22.5 us (16%)
  matrix products  7.04 us (5%)
  local copies, waits for them, and re-layouts  3.33 us (2%)
  other arithmetic  3.22 us (2%)
  between operations  2.14 us (2%)
    all_gather x1, blocking collectives, sum_over_dp(): lax.all_gather(part, 'dp', axis=0, axis_index_groups=far)  40.8 us
    ppermute x4, starting transfers between devices, passed_along(): lax.ppermute(array, axis, [(i, (i + by) % count) for i in range(count)])  25.6 us
    all_to_all x3, starting transfers between devices, swap(): return lax.all_to_all(parts, axis, 0, 0, axis_index_groups=groups)  21.9 us
    ppermute x4, waiting for transfers between devices, passed_along(): lax.ppermute(array, axis, [(i, (i + by) % count) for i in range(count)])  14.6 us
    all_to_all x1, blocking collectives, swap(): return lax.all_to_all(parts, axis, 0, 0, axis_index_groups=groups)  10.9 us
    all_to_all x3, waiting for transfers between devices, swap(): return lax.all_to_all(parts, axis, 0, 0, axis_index_groups=groups)  7.82 us
    dot_general x1, matrix products, local(): lax.dot_general(pair_grad, z_img, (((1,), (1,)), ((), ())), preferred_ele...  2.85 us
  transfers between devices with their start and end apart: 7, of which 4 were waited for; matrix products, arithmetic and copies ran while one was open for 4% of the time, Pallas kernels for 0%

profile of v5, /device:TPU:1, one launch (start us, length us, event | category | flops | bytes accessed | tf_op | source)
XLA Modules:
  0.0 137.4 jit_solution(9770015287677592224)
XLA Ops:
  0.6 0.0 copy-start
  0.6 1.3 copy-done
  1.9 1.5 %convolution_convert_fusion.1 = bf16[144,512]{1,0:T(8,128)(2,1)S(1)} fusion(bf16[1152,144]{0,1:T(8,128)(2,1)} %param.6, bf16[512,1152]{1,0:T(8,128)(2,1)S(1)} %copy-done), kind=kOutput, calls=%fused_computation.8 | convolution fusion | flops 169943040 | bytes 1658880 | tf_op jit(solution)/shard_map/dot_general | solution.py:72
  3.4 1.1 broadcast_in_dim.12
  4.5 6.1 %all-to-all-start = ((bf16[8,144,512]{2,1,0:T(8,128)(2,1)}), bf16[8,144,512]{2,1,0:T(8,128)(2,1)S(1)}, u32[]{:S(2)}, u32[]{:S(2)}) async-start(bf16[8,144,512]{2,1,0:T(8,128)(2,1)} %broadcast_in_dim.12), calls=%async_computation | async-start | bytes 2359296 | tf_op jit(solution)/shard_map/all_to_all | solution.py:29
  10.6 0.1 fusion.10
  10.7 0.1 fusion.6
  10.9 3.5 %collective-permute-start.1 = (bf16[64,1152]{1,0:T(8,128)(2,1)S(1)}, bf16[64,1152]{1,0:T(8,128)(2,1)S(1)}, u32[]{:S(2)}, u32[]{:S(2)}) collective-permute-start(bf16[64,1152]{1,0:T(8,128)(2,1)S(1)} %fusion.6), channel_id=1, source_target_pairs={{0,16},{8,24},{16,32},{24,40},{32,48},{40,56},{48,64},{56,72},{64,... | collective-permute-start | bytes 442376 | tf_op jit(solution)/shard_map/ppermute | solution.py:14
  14.4 4.7 %collective-permute-start = (bf16[64,1152]{1,0:T(8,128)(2,1)S(1)}, bf16[64,1152]{1,0:T(8,128)(2,1)S(1)}, u32[]{:S(2)}, u32[]{:S(2)}) collective-permute-start(bf16[64,1152]{1,0:T(8,128)(2,1)S(1)} %fusion.6), channel_id=1, source_target_pairs={{0,8},{8,16},{16,24},{24,32},{32,40},{40,48},{48,56},{56,64},{64,7... | collective-permute-start | bytes 442376 | tf_op jit(solution)/shard_map/ppermute | solution.py:14
  20.4 1.3 all-to-all-done
  21.7 0.3 multiply_reduce_fusion
  22.0 0.4 fusion.2
  22.4 12.2 %collective-permute-done.1 = bf16[64,1152]{1,0:T(8,128)(2,1)S(1)} collective-permute-done((bf16[64,1152]{1,0:T(8,128)(2,1)S(1)}, bf16[64,1152]{1,0:T(8,128)(2,1)S(1)}, u32[]{:S(2)}, u32[]{:S(2)}) %collective-permute-start.1) | collective-permute-done | bytes 147488 | tf_op jit(solution)/shard_map/ppermute | solution.py:14
  34.7 0.6 multiply_reduce_fusion.1
  35.3 1.7 %fusion.1 = bf16[1152,512]{1,0:T(8,128)(2,1)} fusion(f32[1152,512]{1,0:T(8,128)S(1)} %get-tuple-element.9, f32[512]{0:T(512)S(1)} %get-tuple-element.14, f32[512]{0:T(512)S(1)} %get-tuple-element.12, bf16[64,1152]{1,0:T(8,128)(2,1)S(1)} %collective-permute-done.1, bf16[64,1152]{1,0:T(8,128)(2,1)S(1)} %collective-permute-done, ...), kind=kOutput, calls=%fused_computation.2 | convolution fusion | flops 231358464 | bytes 4379592 | tf_op jit(solution)/shard_map/dot_general | solution.py:98
  37.0 4.2 %all-to-all-start.1 = ((bf16[8,144,512]{2,1,0:T(8,128)(2,1)}), bf16[8,144,512]{2,1,0:T(8,128)(2,1)S(1)}, u32[]{:S(2)}, u32[]{:S(2)}) async-start(bf16[8,144,512]{2,1,0:T(8,128)(2,1)} %bitcast.35), calls=%async_computation.1 | async-start | bytes 2359296 | tf_op jit(solution)/shard_map/all_to_all | solution.py:29
  41.2 2.9 %fusion.16 = (bf16[192,1152]{1,0:T(8,128)(2,1)S(1)}, f32[192,1152]{1,0:T(8,128)}) fusion(bf16[1152,512]{1,0:T(8,128)(2,1)} %copy-done.2, f32[192,512]{1,0:T(8,128)S(1)} %get-tuple-element.15, f32[]{:T(128)} %bitcast.29, f32[]{:T(128)} %bitcast.26, s32[192]{0:T(256)S(1)} %iota_add_fusion, pred[192]{0:T(512)(128)(4,1)S(1)} %iota_compare_fusion.1), kind=kOutput, calls=%fused_computation.45 | convolution fusion | flops 228114432 | bytes 2900936 | tf_op jit(solution)/shard_map/dot_general | solution.py:90
  44.1 13.5 %collective-permute-start.3 = (bf16[64,1152]{1,0:T(8,128)(2,1)S(1)}, bf16[64,1152]{1,0:T(8,128)(2,1)S(1)}, u32[]{:S(2)}, u32[]{:S(2)}) collective-permute-start(bf16[64,1152]{1,0:T(8,128)(2,1)S(1)} %get-tuple-element.10), channel_id=1, source_target_pairs={{0,1008},{8,1016},{16,0},{24,8},{32,16},{40,24},{48,32},{56,40},{6... | collective-permute-start | bytes 442376 | tf_op jit(solution)/shard_map/ppermute | solution.py:14
  57.6 3.8 %collective-permute-start.2 = (bf16[64,1152]{1,0:T(8,128)(2,1)S(1)}, bf16[64,1152]{1,0:T(8,128)(2,1)S(1)}, u32[]{:S(2)}, u32[]{:S(2)}) collective-permute-start(bf16[64,1152]{1,0:T(8,128)(2,1)S(1)} %get-tuple-element.11), channel_id=1, source_target_pairs={{0,1016},{8,0},{16,8},{24,16},{32,24},{40,32},{48,40},{56,48},{64,... | collective-permute-start | bytes 442376 | tf_op jit(solution)/shard_map/ppermute | solution.py:14
  61.5 0.2 reduce_sum.75
  61.6 2.4 %collective-permute-done.2 = bf16[64,1152]{1,0:T(8,128)(2,1)S(1)} collective-permute-done((bf16[64,1152]{1,0:T(8,128)(2,1)S(1)}, bf16[64,1152]{1,0:T(8,128)(2,1)S(1)}, u32[]{:S(2)}, u32[]{:S(2)}) %collective-permute-start.2) | collective-permute-done | bytes 147488 | tf_op jit(solution)/shard_map/ppermute | solution.py:14
  64.1 0.4 convolution_convert_fusion
  64.6 10.9 %all_to_all.20 = bf16[8,168,128]{2,1,0:T(8,128)(2,1)S(1)} all-to-all(bf16[8,168,128]{2,1,0:T(8,128)(2,1)S(1)} %bitcast.32), channel_id=1, replica_groups={{0,8,16,24,512,520,528,536},{32,40,48,56,544,552,560,568},{64,72,80,88,..., dimensions={0} | all-to-all | bytes 688128 | tf_op jit(solution)/shard_map/all_to_all | solution.py:29
  75.5 0.1 reduce_sum.76
  75.6 40.8 %all-gather = bf16[2688,128]{1,0:T(8,128)(2,1)S(1)} all-gather(bf16[168,128]{1,0:T(8,128)(2,1)S(1)} %reduce_sum.76), channel_id=2, replica_groups={{0,32,64,96,128,160,192,224,256,288,320,352,384,416,448,480},{8,40,72,1..., dimensions={0}, use_global_device_ids=true | all-gather | bytes 731136 | tf_op jit(solution)/shard_map/all_gather | solution.py:51
  116.4 0.1 reduce_sum.77
  116.5 0.8 broadcast_in_dim.15
  117.3 11.6 %all-to-all-start.3 = ((bf16[8,168,128]{2,1,0:T(8,128)(2,1)}), bf16[8,168,128]{2,1,0:T(8,128)(2,1)S(1)}, u32[]{:S(2)}, u32[]{:S(2)}) async-start(bf16[8,168,128]{2,1,0:T(8,128)(2,1)} %broadcast_in_dim.15), calls=%async_computation.3 | async-start | bytes 688128 | tf_op jit(solution)/shard_map/all_to_all | solution.py:29
  128.9 0.2 fusion.7
  129.1 0.8 fusion.9
  129.9 6.5 %all-to-all-done.3 = bf16[8,168,128]{2,1,0:T(8,128)(2,1)S(1)} async-done(((bf16[8,168,128]{2,1,0:T(8,128)(2,1)}), bf16[8,168,128]{2,1,0:T(8,128)(2,1)S(1)}, u32[]{:S(2)}, u32[]{:S(2)}) %all-to-all-start.3) | async-done | bytes 344096 | tf_op jit(solution)/shard_map/all_to_all | solution.py:29
  136.5 0.9 copy_bitcast_fusion
  (25 shorter events, 0.2 us)
Async XLA Ops:
  0.6 1.3 copy-start
  4.5 6.1 %copy-start.1 = (bf16[64,1152]{1,0:T(8,128)(2,1)S(1)}, bf16[64,1152]{1,0:T(8,128)(2,1)}, u32[]{:S(2)}) copy-start(bf16[64,1152]{1,0:T(8,128)(2,1)} %param.7) | copy-start | bytes 442372
  4.5 17.2 %all-to-all-start = ((bf16[8,144,512]{2,1,0:T(8,128)(2,1)}), bf16[8,144,512]{2,1,0:T(8,128)(2,1)S(1)}, u32[]{:S(2)}, u32[]{:S(2)}) async-start(bf16[8,144,512]{2,1,0:T(8,128)(2,1)} %broadcast_in_dim.12), calls=%async_computation | async-start | bytes 2359296 | tf_op jit(solution)/shard_map/all_to_all | solution.py:29
  10.9 23.8 %collective-permute-start.1 = (bf16[64,1152]{1,0:T(8,128)(2,1)S(1)}, bf16[64,1152]{1,0:T(8,128)(2,1)S(1)}, u32[]{:S(2)}, u32[]{:S(2)}) collective-permute-start(bf16[64,1152]{1,0:T(8,128)(2,1)S(1)} %fusion.6), channel_id=1, source_target_pairs={{0,16},{8,24},{16,32},{24,40},{32,48},{40,56},{48,64},{56,72},{64,... | collective-permute-start | bytes 442376 | tf_op jit(solution)/shard_map/ppermute | solution.py:14
  14.4 20.3 %collective-permute-start = (bf16[64,1152]{1,0:T(8,128)(2,1)S(1)}, bf16[64,1152]{1,0:T(8,128)(2,1)S(1)}, u32[]{:S(2)}, u32[]{:S(2)}) collective-permute-start(bf16[64,1152]{1,0:T(8,128)(2,1)S(1)} %fusion.6), channel_id=1, source_target_pairs={{0,8},{8,16},{16,24},{24,32},{32,40},{40,48},{48,56},{56,64},{64,7... | collective-permute-start | bytes 442376 | tf_op jit(solution)/shard_map/ppermute | solution.py:14
  22.4 12.8 %copy-start.2 = (bf16[1152,512]{1,0:T(8,128)(2,1)}, bf16[1152,512]{1,0:T(8,128)(2,1)S(1)}, u32[]{:S(2)}) copy-start(bf16[1152,512]{1,0:T(8,128)(2,1)S(1)} %get-tuple-element.8) | copy-start | bytes 3538948
  37.0 24.4 %all-to-all-start.1 = ((bf16[8,144,512]{2,1,0:T(8,128)(2,1)}), bf16[8,144,512]{2,1,0:T(8,128)(2,1)S(1)}, u32[]{:S(2)}, u32[]{:S(2)}) async-start(bf16[8,144,512]{2,1,0:T(8,128)(2,1)} %bitcast.35), calls=%async_computation.1 | async-start | bytes 2359296 | tf_op jit(solution)/shard_map/all_to_all | solution.py:29
  44.1 17.5 %collective-permute-start.3 = (bf16[64,1152]{1,0:T(8,128)(2,1)S(1)}, bf16[64,1152]{1,0:T(8,128)(2,1)S(1)}, u32[]{:S(2)}, u32[]{:S(2)}) collective-permute-start(bf16[64,1152]{1,0:T(8,128)(2,1)S(1)} %get-tuple-element.10), channel_id=1, source_target_pairs={{0,1008},{8,1016},{16,0},{24,8},{32,16},{40,24},{48,32},{56,40},{6... | collective-permute-start | bytes 442376 | tf_op jit(solution)/shard_map/ppermute | solution.py:14
  57.6 6.5 %collective-permute-start.2 = (bf16[64,1152]{1,0:T(8,128)(2,1)S(1)}, bf16[64,1152]{1,0:T(8,128)(2,1)S(1)}, u32[]{:S(2)}, u32[]{:S(2)}) collective-permute-start(bf16[64,1152]{1,0:T(8,128)(2,1)S(1)} %get-tuple-element.11), channel_id=1, source_target_pairs={{0,1016},{8,0},{16,8},{24,16},{32,24},{40,32},{48,40},{56,48},{64,... | collective-permute-start | bytes 442376 | tf_op jit(solution)/shard_map/ppermute | solution.py:14
  75.6 53.3 %copy-start.3 = (f32[192,1152]{1,0:T(8,128)S(1)}, f32[192,1152]{1,0:T(8,128)}, u32[]{:S(2)}) copy-start(f32[192,1152]{1,0:T(8,128)} %get-tuple-element.17) | copy-start | bytes 2654212
  117.3 19.2 %all-to-all-start.3 = ((bf16[8,168,128]{2,1,0:T(8,128)(2,1)}), bf16[8,168,128]{2,1,0:T(8,128)(2,1)S(1)}, u32[]{:S(2)}, u32[]{:S(2)}) async-start(bf16[8,168,128]{2,1,0:T(8,128)(2,1)} %broadcast_in_dim.15), calls=%async_computation.3 | async-start | bytes 688128 | tf_op jit(solution)/shard_map/all_to_all | solution.py:29

commit v6 on v4

--- a/solution.py
+++ b/solution.py
@@ -48,9 +48,10 @@
     near, far = dp_groups(lax.axis_size("dp"))
     count = len(near[0])
     share = -(-tiles * width // (count * ROWS)) * ROWS
-    slabs = [grad_t[:, LANES * t : LANES * (t + 1)].astype(jnp.bfloat16) for t in range(tiles)]
-    slabs.append(jnp.zeros((count * share - tiles * width, LANES), jnp.bfloat16))
-    rows = jnp.concatenate(slabs, axis=0)
+    rows = jnp.concatenate(
+        [grad_t[:, LANES * t : LANES * (t + 1)] for t in range(tiles)], axis=0
+    ).astype(jnp.bfloat16)
+    rows = jnp.pad(rows, ((0, count * share - tiles * width), (0, 0)))
     part = summed(swap(rows.reshape(count, share, LANES), "dp", near)).astype(jnp.bfloat16)
     part, early = lax.optimization_barrier((part, early))
     total = summed(lax.all_gather(part, "dp", axis=0, axis_index_groups=far)).astype(jnp.bfloat16)
@@ -75,20 +76,21 @@
     unit_txt = wide_txt * inv_txt
     z_txt = unit_txt.astype(jnp.bfloat16)
     pair_txt = jnp.concatenate([z_txt, to_partner(z_txt)], axis=0)
-    visitors = [pair_txt] + [passed_along(pair_txt, "dp", k) for k in range(1, STEPS)]
 
     local_proj = lax.dot_general(
         w_proj, img_feat, (((0,), (1,)), ((), ())), preferred_element_type=jnp.float32
     ).astype(jnp.bfloat16)
     halves = jnp.stack([local_proj[:, h * half_rows : (h + 1) * half_rows] for h in range(PAIR)])
     halves = jnp.broadcast_to(halves[None], (members // PAIR,) + halves.shape)
+    halves, pair_txt = lax.optimization_barrier((halves, pair_txt))
+    visitors = [pair_txt] + [passed_along(pair_txt, "dp", k) for k in range(1, STEPS)]
     projected = swap(halves.reshape(members, width, half_rows), "emb").reshape(features, half_rows)
     wide_img = projected.astype(jnp.float32)
     inv_img = lax.rsqrt(jnp.sum(wide_img * wide_img, axis=0, keepdims=True) + EPSILON)
     unit_img = wide_img * inv_img
     z_img = unit_img.astype(jnp.bfloat16)
 
-    texts = jnp.concatenate(visitors, axis=0)
+    texts = lax.optimization_barrier(jnp.concatenate(visitors, axis=0))
     cosines = jnp.dot(texts, z_img, preferred_element_type=jnp.float32)
     text_index = lax.broadcasted_iota(jnp.int32, cosines.shape, 0)
     image_index = lax.broadcasted_iota(jnp.int32, cosines.shape, 1) + half * half_rows
@@ -113,7 +115,6 @@
     parts = grad_proj.astype(jnp.bfloat16).reshape(members, width, half_rows)
     parts = swap(parts, "emb").reshape(members // PAIR, PAIR, width, half_rows)
     grad_part = summed(parts).astype(jnp.bfloat16)
-    grad_part, other_terms = lax.optimization_barrier((grad_part, other_terms))
     grad_part = jnp.concatenate([grad_part[h] for h in range(PAIR)], axis=1)
     local_weight = jnp.dot(grad_part, img_feat, preferred_element_type=jnp.float32)
 

time: 157 us -> 149 us (0.949)
  blocking collectives: 28.7 us -> 42 us
  local copies, waits for them, and re-layouts: 10.4 us -> 3.18 us
  starting transfers between devices: 65.2 us -> 58 us
  matrix products: 7.72 us -> 3.82 us
  waiting for transfers between devices: 37.6 us -> 34 us
    all_to_all x0 -> x1, blocking collectives: none -> 12 us  [swap(): return lax.all_to_all(parts, axis, 0, 0, axis_index_groups=groups)]
    unnamed x17 -> x20, local copies, waits for them, and re-layouts: 8.02 us -> 0.66 us
    all_to_all x4 -> x3, starting transfers between devices: 36.2 us -> 30.2 us  [swap(): return lax.all_to_all(parts, axis, 0, 0, axis_index_groups=groups)]
    ppermute x4, waiting for transfers between devices: 19.3 us -> 14 us  [passed_along(): lax.ppermute(array, axis, [(i, (i + by) % count) for i in range(count)])]
    ppermute x2, waiting for transfers between devices: 10 us -> 13.5 us  [to_partner(): lax.ppermute(array, 'emb', [(i, i ^ 1) for i in range(lax.axis_size('emb'...]
    dot_general x1, matrix products: 2.7 us -> 0.77 us  [local(): lax.dot_general(texts, pair_grad, (((0,), (0,)), ((), ())), preferred_ele...]
    all_to_all x4 -> x3, waiting for transfers between devices: 8.18 us -> 6.51 us  [swap(): return lax.all_to_all(parts, axis, 0, 0, axis_index_groups=groups)]
  transfers between devices with their start and end apart: 10 -> 9, of which waited for: 6 -> 5; matrix products, arithmetic and copies ran while one was open for 3% -> 3% of each run, Pallas kernels for 0% -> 0%
where the time goes in v6:
time: 149 us
  starting transfers between devices  58 us (39%)
  blocking collectives  42 us (28%)
  waiting for transfers between devices  34 us (23%)
  other arithmetic  5.47 us (4%)
  matrix products  3.82 us (3%)
  local copies, waits for them, and re-layouts  3.18 us (2%)
  between operations  2.26 us (2%)
    all_to_all x3, starting transfers between devices, swap(): return lax.all_to_all(parts, axis, 0, 0, axis_index_groups=groups)  30.2 us
    all_gather x1, blocking collectives, sum_over_dp(): lax.all_gather(part, 'dp', axis=0, axis_index_groups=far)  29.9 us
    ppermute x4, starting transfers between devices, passed_along(): lax.ppermute(array, axis, [(i, (i + by) % count) for i in range(count)])  21.9 us
    ppermute x4, waiting for transfers between devices, passed_along(): lax.ppermute(array, axis, [(i, (i + by) % count) for i in range(count)])  14 us
    ppermute x2, waiting for transfers between devices, to_partner(): lax.ppermute(array, 'emb', [(i, i ^ 1) for i in range(lax.axis_size('emb'...  13.5 us
    all_to_all x1, blocking collectives, swap(): return lax.all_to_all(parts, axis, 0, 0, axis_index_groups=groups)  12 us
    all_to_all x3, waiting for transfers between devices, swap(): return lax.all_to_all(parts, axis, 0, 0, axis_index_groups=groups)  6.51 us
    ppermute x2, starting transfers between devices, to_partner(): lax.ppermute(array, 'emb', [(i, i ^ 1) for i in range(lax.axis_size('emb'...  5.87 us
  transfers between devices with their start and end apart: 9, of which 5 were waited for; matrix products, arithmetic and copies ran while one was open for 3% of the time, Pallas kernels for 0%

profile of v6, /device:TPU:1, one launch (start us, length us, event | category | flops | bytes accessed | tf_op | source)
XLA Modules:
  0.0 148.8 jit_solution(14331931446312200375)
XLA Ops:
  0.6 1.1 fusion.11
  1.8 1.0 fusion.7
  2.8 3.9 %collective-permute-start = (bf16[64,1152]{1,0:T(8,128)(2,1)S(1)}, bf16[64,1152]{1,0:T(8,128)(2,1)S(1)}, u32[]{:S(2)}, u32[]{:S(2)}) collective-permute-start(bf16[64,1152]{1,0:T(8,128)(2,1)S(1)} %fusion.7), channel_id=1, source_target_pairs={{0,1},{1,0},{2,3},{3,2},{4,5},{5,4},{6,7},{7,6},{8,9},{9,8},{10,11... | collective-permute-start | bytes 442376 | tf_op jit(solution)/shard_map/ppermute | solution.py:19
  6.8 1.5 %convolution_convert_fusion.1 = bf16[144,512]{1,0:T(8,128)(2,1)S(1)} fusion(bf16[1152,144]{0,1:T(8,128)(2,1)} %param.6, bf16[512,1152]{1,0:T(8,128)(2,1)S(1)} %copy-done), kind=kOutput, calls=%fused_computation.7 | convolution fusion | flops 169943040 | bytes 1658880 | tf_op jit(solution)/shard_map/dot_general | solution.py:80
  8.3 1.0 collective-permute-done
  9.3 0.9 broadcast_in_dim.12
  10.2 4.5 %collective-permute-start.2 = (bf16[128,1152]{1,0:T(8,128)(2,1)S(1)}, bf16[128,1152]{1,0:T(8,128)(2,1)S(1)}, u32[]{:S(2)}, u32[]{:S(2)}) collective-permute-start(bf16[128,1152]{1,0:T(8,128)(2,1)S(1)} %pad_maximum_fusion.1), channel_id=1, source_target_pairs={{0,16},{8,24},{16,32},{24,40},{32,48},{40,56},{48,64},{56,72},{64,... | collective-permute-start | bytes 884744 | tf_op jit(solution)/shard_map/ppermute | solution.py:15
  14.7 5.3 %collective-permute-start.1 = (bf16[128,1152]{1,0:T(8,128)(2,1)S(1)}, bf16[128,1152]{1,0:T(8,128)(2,1)S(1)}, u32[]{:S(2)}, u32[]{:S(2)}) collective-permute-start(bf16[128,1152]{1,0:T(8,128)(2,1)S(1)} %pad_maximum_fusion.1), channel_id=1, source_target_pairs={{0,8},{8,16},{16,24},{24,32},{32,40},{40,48},{48,56},{56,64},{64,7... | collective-permute-start | bytes 884744 | tf_op jit(solution)/shard_map/ppermute | solution.py:15
  19.9 5.1 %all-to-all-start = ((bf16[8,144,256]{2,1,0:T(8,128)(2,1)}), bf16[8,144,256]{2,1,0:T(8,128)(2,1)S(1)}, u32[]{:S(2)}, u32[]{:S(2)}) async-start(bf16[8,144,256]{2,1,0:T(8,128)(2,1)} %bitcast.3), calls=%async_computation | async-start | bytes 1179648 | tf_op jit(solution)/shard_map/all_to_all | solution.py:34
  25.1 0.6 iota_compare_fusion.2
  27.0 10.8 %collective-permute-done.2 = bf16[128,1152]{1,0:T(8,128)(2,1)S(1)} collective-permute-done((bf16[128,1152]{1,0:T(8,128)(2,1)S(1)}, bf16[128,1152]{1,0:T(8,128)(2,1)S(1)}, u32[]{:S(2)}, u32[]{:S(2)}) %collective-permute-start.2) | collective-permute-done | bytes 294944 | tf_op jit(solution)/shard_map/ppermute | solution.py:15
  37.9 0.2 multiply_reduce_fusion
  38.2 0.5 copy-done.2
  38.8 0.6 multiply_reduce_fusion.1
  39.3 0.8 fusion.1
  40.1 12.0 %all_to_all.20 = bf16[8,144,256]{2,1,0:T(8,128)(2,1)S(1)} all-to-all(bf16[8,144,256]{2,1,0:T(8,128)(2,1)S(1)} %bitcast.70), channel_id=1, replica_groups=mesh['dp'=128,'emb'=8] {'emb'}, dimensions={0} | all-to-all | bytes 1179648 | tf_op jit(solution)/shard_map/all_to_all | solution.py:34
  52.3 0.4 convolution_convert_fusion
  52.8 0.8 pad.4
  53.6 13.2 %all-to-all-start.2 = ((bf16[8,168,128]{2,1,0:T(8,128)(2,1)}), bf16[8,168,128]{2,1,0:T(8,128)(2,1)S(1)}, u32[]{:S(2)}, u32[]{:S(2)}) async-start(bf16[8,168,128]{2,1,0:T(8,128)(2,1)} %bitcast.10), calls=%async_computation.2 | async-start | bytes 688128 | tf_op jit(solution)/shard_map/all_to_all | solution.py:34
  66.8 0.6 convolution_multiply_fusion
  67.5 1.9 %collective-permute-start.3 = (bf16[3,64,1152]{2,1,0:T(8,128)(2,1)S(1)}, bf16[3,64,1152]{2,1,0:T(8,128)(2,1)S(1)}, u32[]{:S(2)}, u32[]{:S(2)}) collective-permute-start(bf16[3,64,1152]{2,1,0:T(8,128)(2,1)S(1)} %fusion.4), channel_id=1, source_target_pairs={{0,1},{1,0},{2,3},{3,2},{4,5},{5,4},{6,7},{7,6},{8,9},{9,8},{10,11... | collective-permute-start | bytes 1327112 | tf_op jit(solution)/shard_map/ppermute | solution.py:19
  69.4 12.6 %collective-permute-done.3 = bf16[3,64,1152]{2,1,0:T(8,128)(2,1)S(1)} collective-permute-done((bf16[3,64,1152]{2,1,0:T(8,128)(2,1)S(1)}, bf16[3,64,1152]{2,1,0:T(8,128)(2,1)S(1)}, u32[]{:S(2)}, u32[]{:S(2)}) %collective-permute-start.3) | collective-permute-done | bytes 442400 | tf_op jit(solution)/shard_map/ppermute | solution.py:19
  82.1 9.0 %collective-permute-start.5 = (bf16[64,1152]{1,0:T(8,128)(2,1)S(1)}, bf16[64,1152]{1,0:T(8,128)(2,1)S(1)}, u32[]{:S(2)}, u32[]{:S(2)}) collective-permute-start(bf16[64,1152]{1,0:T(8,128)(2,1)S(1)} %get-tuple-element.16), channel_id=1, source_target_pairs={{0,1008},{8,1016},{16,0},{24,8},{32,16},{40,24},{48,32},{56,40},{6... | collective-permute-start | bytes 442376 | tf_op jit(solution)/shard_map/ppermute | solution.py:15
  91.1 3.2 %collective-permute-start.4 = (bf16[64,1152]{1,0:T(8,128)(2,1)S(1)}, bf16[64,1152]{1,0:T(8,128)(2,1)S(1)}, u32[]{:S(2)}, u32[]{:S(2)}) collective-permute-start(bf16[64,1152]{1,0:T(8,128)(2,1)S(1)} %get-tuple-element.17), channel_id=1, source_target_pairs={{0,1016},{8,0},{16,8},{24,16},{32,24},{40,32},{48,40},{56,48},{64,... | collective-permute-start | bytes 442376 | tf_op jit(solution)/shard_map/ppermute | solution.py:15
  94.4 3.2 %collective-permute-done.4 = bf16[64,1152]{1,0:T(8,128)(2,1)S(1)} collective-permute-done((bf16[64,1152]{1,0:T(8,128)(2,1)S(1)}, bf16[64,1152]{1,0:T(8,128)(2,1)S(1)}, u32[]{:S(2)}, u32[]{:S(2)}) %collective-permute-start.4) | collective-permute-done | bytes 147488 | tf_op jit(solution)/shard_map/ppermute | solution.py:15
  97.6 29.9 %all-gather = bf16[2688,128]{1,0:T(8,128)(2,1)S(1)} all-gather(bf16[168,128]{1,0:T(8,128)(2,1)S(1)} %reduce_sum.76), channel_id=2, replica_groups={{0,32,64,96,128,160,192,224,256,288,320,352,384,416,448,480},{8,40,72,1..., dimensions={0}, use_global_device_ids=true | all-gather | bytes 731136 | tf_op jit(solution)/shard_map/all_gather | solution.py:57
  127.6 0.8 broadcast_in_dim.15
  128.4 11.9 %all-to-all-start.3 = ((bf16[8,168,128]{2,1,0:T(8,128)(2,1)}), bf16[8,168,128]{2,1,0:T(8,128)(2,1)S(1)}, u32[]{:S(2)}, u32[]{:S(2)}) async-start(bf16[8,168,128]{2,1,0:T(8,128)(2,1)} %broadcast_in_dim.15), calls=%async_computation.3 | async-start | bytes 688128 | tf_op jit(solution)/shard_map/all_to_all | solution.py:34
  140.3 0.2 fusion.8
  140.5 0.8 fusion.10
  141.3 6.5 %all-to-all-done.3 = bf16[8,168,128]{2,1,0:T(8,128)(2,1)S(1)} async-done(((bf16[8,168,128]{2,1,0:T(8,128)(2,1)}), bf16[8,168,128]{2,1,0:T(8,128)(2,1)S(1)}, u32[]{:S(2)}, u32[]{:S(2)}) %all-to-all-start.3) | async-done | bytes 344096 | tf_op jit(solution)/shard_map/all_to_all | solution.py:34
  147.9 0.9 copy_bitcast_fusion.1
  (41 shorter events, 0.9 us)
Async XLA Ops:
  0.6 6.1 %copy-start = (bf16[512,1152]{1,0:T(8,128)(2,1)S(1)}, bf16[512,1152]{1,0:T(8,128)(2,1)}, u32[]{:S(2)}) copy-start(bf16[512,1152]{1,0:T(8,128)(2,1)} %param.5) | copy-start | bytes 3538948
  2.8 6.5 %collective-permute-start = (bf16[64,1152]{1,0:T(8,128)(2,1)S(1)}, bf16[64,1152]{1,0:T(8,128)(2,1)S(1)}, u32[]{:S(2)}, u32[]{:S(2)}) collective-permute-start(bf16[64,1152]{1,0:T(8,128)(2,1)S(1)} %fusion.7), channel_id=1, source_target_pairs={{0,1},{1,0},{2,3},{3,2},{4,5},{5,4},{6,7},{7,6},{8,9},{9,8},{10,11... | collective-permute-start | bytes 442376 | tf_op jit(solution)/shard_map/ppermute | solution.py:19
  10.2 27.6 %collective-permute-start.2 = (bf16[128,1152]{1,0:T(8,128)(2,1)S(1)}, bf16[128,1152]{1,0:T(8,128)(2,1)S(1)}, u32[]{:S(2)}, u32[]{:S(2)}) collective-permute-start(bf16[128,1152]{1,0:T(8,128)(2,1)S(1)} %pad_maximum_fusion.1), channel_id=1, source_target_pairs={{0,16},{8,24},{16,32},{24,40},{32,48},{40,56},{48,64},{56,72},{64,... | collective-permute-start | bytes 884744 | tf_op jit(solution)/shard_map/ppermute | solution.py:15
  14.7 23.1 %collective-permute-start.1 = (bf16[128,1152]{1,0:T(8,128)(2,1)S(1)}, bf16[128,1152]{1,0:T(8,128)(2,1)S(1)}, u32[]{:S(2)}, u32[]{:S(2)}) collective-permute-start(bf16[128,1152]{1,0:T(8,128)(2,1)S(1)} %pad_maximum_fusion.1), channel_id=1, source_target_pairs={{0,8},{8,16},{16,24},{24,32},{32,40},{40,48},{48,56},{56,64},{64,7... | collective-permute-start | bytes 884744 | tf_op jit(solution)/shard_map/ppermute | solution.py:15
  19.9 17.9 %all-to-all-start = ((bf16[8,144,256]{2,1,0:T(8,128)(2,1)}), bf16[8,144,256]{2,1,0:T(8,128)(2,1)S(1)}, u32[]{:S(2)}, u32[]{:S(2)}) async-start(bf16[8,144,256]{2,1,0:T(8,128)(2,1)} %bitcast.3), calls=%async_computation | async-start | bytes 1179648 | tf_op jit(solution)/shard_map/all_to_all | solution.py:34
  38.1 0.7 copy-start.2
  38.1 0.7 copy-start.3
  39.3 0.8 copy-start.4
  52.6 14.1 %copy-start.5 = (f32[384,256]{1,0:T(8,128)S(1)}, f32[384,256]{1,0:T(8,128)}, u32[]{:S(2)}) copy-start(f32[384,256]{1,0:T(8,128)} %copy-done.4) | copy-start | bytes 1179652
  53.6 40.7 %all-to-all-start.2 = ((bf16[8,168,128]{2,1,0:T(8,128)(2,1)}), bf16[8,168,128]{2,1,0:T(8,128)(2,1)S(1)}, u32[]{:S(2)}, u32[]{:S(2)}) async-start(bf16[8,168,128]{2,1,0:T(8,128)(2,1)} %bitcast.10), calls=%async_computation.2 | async-start | bytes 688128 | tf_op jit(solution)/shard_map/all_to_all | solution.py:34
  67.5 14.5 %collective-permute-start.3 = (bf16[3,64,1152]{2,1,0:T(8,128)(2,1)S(1)}, bf16[3,64,1152]{2,1,0:T(8,128)(2,1)S(1)}, u32[]{:S(2)}, u32[]{:S(2)}) collective-permute-start(bf16[3,64,1152]{2,1,0:T(8,128)(2,1)S(1)} %fusion.4), channel_id=1, source_target_pairs={{0,1},{1,0},{2,3},{3,2},{4,5},{5,4},{6,7},{7,6},{8,9},{9,8},{10,11... | collective-permute-start | bytes 1327112 | tf_op jit(solution)/shard_map/ppermute | solution.py:19
  82.1 12.3 %collective-permute-start.5 = (bf16[64,1152]{1,0:T(8,128)(2,1)S(1)}, bf16[64,1152]{1,0:T(8,128)(2,1)S(1)}, u32[]{:S(2)}, u32[]{:S(2)}) collective-permute-start(bf16[64,1152]{1,0:T(8,128)(2,1)S(1)} %get-tuple-element.16), channel_id=1, source_target_pairs={{0,1008},{8,1016},{16,0},{24,8},{32,16},{40,24},{48,32},{56,40},{6... | collective-permute-start | bytes 442376 | tf_op jit(solution)/shard_map/ppermute | solution.py:15
  91.1 6.5 %collective-permute-start.4 = (bf16[64,1152]{1,0:T(8,128)(2,1)S(1)}, bf16[64,1152]{1,0:T(8,128)(2,1)S(1)}, u32[]{:S(2)}, u32[]{:S(2)}) collective-permute-start(bf16[64,1152]{1,0:T(8,128)(2,1)S(1)} %get-tuple-element.17), channel_id=1, source_target_pairs={{0,1016},{8,0},{16,8},{24,16},{32,24},{40,32},{48,40},{56,48},{64,... | collective-permute-start | bytes 442376 | tf_op jit(solution)/shard_map/ppermute | solution.py:15
  94.4 45.9 %copy-start.1 = (bf16[64,1152]{1,0:T(8,128)(2,1)S(1)}, bf16[64,1152]{1,0:T(8,128)(2,1)}, u32[]{:S(2)}) copy-start(bf16[64,1152]{1,0:T(8,128)(2,1)} %param.7) | copy-start | bytes 442372
  128.4 19.5 %all-to-all-start.3 = ((bf16[8,168,128]{2,1,0:T(8,128)(2,1)}), bf16[8,168,128]{2,1,0:T(8,128)(2,1)S(1)}, u32[]{:S(2)}, u32[]{:S(2)}) async-start(bf16[8,168,128]{2,1,0:T(8,128)(2,1)} %broadcast_in_dim.15), calls=%async_computation.3 | async-start | bytes 688128 | tf_op jit(solution)/shard_map/all_to_all | solution.py:34

commit v7 on v6

v7 whole, which is shorter than its diff:
```python
import jax
import jax.numpy as jnp
from jax import lax
from jax.sharding import PartitionSpec as P

STEPS = 3
EPSILON = 1e-06
LANES = 128
ROWS = 8
PAIR = 2


def passed_along(array, axis, by):
    count = lax.axis_size(axis)
    return lax.ppermute(array, axis, [(i, (i + by) % count) for i in range(count)])


def to_partner(array):
    return lax.ppermute(array, "emb", [(i, i ^ 1) for i in range(lax.axis_size("emb"))])


def dp_groups(count):
    z_len = count // 4
    index = lambda hi, z, core: (hi * z_len + z) * 2 + core
    near = [
        [index(hi, z + dz, c) for hi in range(2) for dz in range(2) for c in range(2)]
        for z in range(0, z_len, 2)
    ]
    far = [list(members) for members in zip(*near)]
    return near, far


def swap(parts, axis, groups=None):
    return lax.all_to_all(parts, axis, 0, 0, axis_index_groups=groups)


def gathered(part, count, axis, groups=None):
    return swap(jnp.broadcast_to(part[None], (count,) + part.shape), axis, groups)


def summed(parts):
    return jnp.sum(parts.astype(jnp.float32), axis=0)


def sum_over_dp(grad_t, early):
    width, features = grad_t.shape
    tiles = features // LANES
    near, far = dp_groups(lax.axis_size("dp"))
    count = len(near[0])
    share = -(-tiles * width // (count * ROWS)) * ROWS
    rows = jnp.concatenate(
        [grad_t[:, LANES * t : LANES * (t + 1)] for t in range(tiles)], axis=0
    ).astype(jnp.bfloat16)
    rows = jnp.pad(rows, ((0, count * share - tiles * width), (0, 0)))
    part = summed(swap(rows.reshape(count, share, LANES), "dp", near)).astype(jnp.bfloat16)
    total = summed(lax.all_gather(part, "dp", axis=0, axis_index_groups=far)).astype(jnp.bfloat16)
    total, early = lax.optimization_barrier((total, early))
    whole = gathered(total, count, "dp", near).reshape(count * share, LANES)[: tiles * width]
    whole = whole.astype(jnp.float32).reshape(tiles, width, LANES)
    return jnp.swapaxes(whole, 1, 2).reshape(features, width), early


def unit_columns(values):
    wide = values.astype(jnp.float32)
    inverse = lax.rsqrt(jnp.sum(wide * wide, axis=0, keepdims=True) + EPSILON)
    return wide * inverse, inverse


def unit_rows(values):
    wide = values.astype(jnp.float32)
    inverse = lax.rsqrt(jnp.sum(wide * wide, axis=1, keepdims=True) + EPSILON)
    return wide * inverse, inverse


def local(img_feat, w_proj, txt_emb, logit_scale, logit_bias):
    image_rows, features = img_feat.shape
    text_rows = txt_emb.shape[0]
    width = w_proj.shape[1]
    members = lax.axis_size("emb")
    member = lax.axis_index("emb")
    half_rows = image_rows // PAIR
    first_row = (member % PAIR) * half_rows
    scale = logit_scale[0]
    offset = logit_bias[0]

    def slopes(texts, images, matches):
        cosines = jnp.dot(texts, images, preferred_element_type=jnp.float32)
        text = lax.broadcasted_iota(jnp.int32, cosines.shape, 0)
        image = lax.broadcasted_iota(jnp.int32, cosines.shape, 1)
        signs = jnp.where(matches(text, image), 1.0, -1.0)
        grads = -signs * jax.nn.sigmoid(-signs * (scale * cosines + offset))
        return cosines, grads.astype(jnp.bfloat16)

    partner_txt = to_partner(txt_emb)
    local_proj = lax.dot_general(
        w_proj, img_feat, (((0,), (1,)), ((), ())), preferred_element_type=jnp.float32
    ).astype(jnp.bfloat16)
    copies = jnp.broadcast_to(local_proj[None], (members,) + local_proj.shape)
    copies, partner_txt = lax.optimization_barrier((copies, partner_txt))
    unit_txt, inv_txt = unit_rows(txt_emb)
    pair_txt = jnp.concatenate([unit_txt, unit_rows(partner_txt)[0]], axis=0).astype(jnp.bfloat16)
    visitors = [pair_txt] + [passed_along(pair_txt, "dp", k) for k in range(1, STEPS)]
    projected = swap(copies, "emb").reshape(features, image_rows)

    mine = lax.dynamic_slice_in_dim(projected, first_row, half_rows, 1)
    unit_img, inv_img = unit_columns(mine)
    texts = lax.optimization_barrier(jnp.concatenate(visitors, axis=0))

    def pair_matches(text, image):
        row = image + first_row
        own = (text < text_rows) & (row == member * text_rows + text)
        other = (text >= text_rows) & (text < PAIR * text_rows)
        return own | (other & (row == (member ^ 1) * text_rows + text - text_rows))

    cosines, pair_grad = slopes(texts, unit_img.astype(jnp.bfloat16), pair_matches)
    inner_img = jnp.sum(pair_grad.astype(jnp.float32) * cosines, axis=0, keepdims=True)
    grad_img = lax.dot_general(
        texts, pair_grad, (((0,), (0,)), ((), ())), preferred_element_type=jnp.float32
    )
    grad_proj = (scale * inv_img) * (grad_img - unit_img * inner_img)
    parts = grad_proj.astype(jnp.bfloat16).reshape(members, width, half_rows)
    parts = swap(parts, "emb").reshape(members // PAIR, PAIR, width, half_rows)
    grad_part = summed(parts).astype(jnp.bfloat16)
    grad_part = jnp.concatenate([grad_part[h] for h in range(PAIR)], axis=1)
    local_weight = jnp.dot(grad_part, img_feat, preferred_element_type=jnp.float32)

    own_texts = jnp.concatenate([visitor[:text_rows] for visitor in visitors], axis=0)
    z_img = unit_columns(projected)[0].astype(jnp.bfloat16)
    own_grad = slopes(
        own_texts,
        z_img,
        lambda text, image: (text < text_rows) & (image == member * text_rows + text),
    )[1]
    txt_terms = scale * lax.dot_general(
        own_grad, z_img, (((1,), (1,)), ((), ())), preferred_element_type=jnp.float32
    )
    sent = [
        passed_along(txt_terms[k * text_rows : (k + 1) * text_rows].astype(jnp.bfloat16), "dp", -k)
        for k in range(1, STEPS)
    ]
    d_weight, sent = sum_over_dp(local_weight, sent)

    grad_txt = txt_terms[:text_rows]
    for term in sent:
        grad_txt = grad_txt + term.astype(jnp.float32)
    inner_txt = jnp.sum(unit_txt * grad_txt, axis=1, keepdims=True)
    d_text = inv_txt * (grad_txt - unit_txt * inner_txt)
    return (d_weight, d_text)


def solution(mesh):
    in_specs = (P("dp", None), P(None, "emb"), P(("dp", "emb"), None), P(), P())
    out_specs = (P(None, "emb"), P(("dp", "emb"), None))
    return jax.shard_map(local, mesh=mesh, in_specs=in_specs, out_specs=out_specs, check_vma=False)
```

time: 149 us -> 134 us (0.90)
  waiting for transfers between devices: 34 us -> 24.6 us
  starting transfers between devices: 58 us -> 49.9 us
  local copies, waits for them, and re-layouts: 3.18 us -> 5.22 us
    ppermute x2 -> x1, waiting for transfers between devices: 13.5 us -> 0.01 us  [to_partner(): lax.ppermute(array, 'emb', [(i, i ^ 1) for i in range(lax.axis_size('emb'...]
    ppermute x4, waiting for transfers between devices: 14 us -> 18.1 us  [passed_along(): lax.ppermute(array, axis, [(i, (i + by) % count) for i in range(count)])]
    all_to_all x3, starting transfers between devices: 30.2 us -> 26.7 us  [swap(): return lax.all_to_all(parts, axis, 0, 0, axis_index_groups=groups)]
    ppermute x4, starting transfers between devices: 21.9 us -> 19.1 us  [passed_along(): lax.ppermute(array, axis, [(i, (i + by) % count) for i in range(count)])]
    ppermute x2 -> x1, starting transfers between devices: 5.87 us -> 4.08 us  [to_partner(): lax.ppermute(array, 'emb', [(i, i ^ 1) for i in range(lax.axis_size('emb'...]
  transfers between devices with their start and end apart: 9 -> 8, of which waited for: 5 -> 2; matrix products, arithmetic and copies ran while one was open for 3% -> 6% of each run, Pallas kernels for 0% -> 0%
where the time goes in v7:
time: 134 us; the launch traced here: 133 us
  starting transfers between devices  49.9 us (37%)
  blocking collectives  41.2 us (31%)
  waiting for transfers between devices  24.6 us (18%)
  matrix products  5.26 us (4%)
  local copies, waits for them, and re-layouts  5.22 us (4%)
  other arithmetic  5.1 us (4%)
  between operations  2.24 us (2%)
    all_gather x1, blocking collectives, sum_over_dp(): lax.all_gather(part, 'dp', axis=0, axis_index_groups=far)  29.1 us
    all_to_all x3, starting transfers between devices, swap(): return lax.all_to_all(parts, axis, 0, 0, axis_index_groups=groups)  26.7 us
    ppermute x4, starting transfers between devices, passed_along(): lax.ppermute(array, axis, [(i, (i + by) % count) for i in range(count)])  19.1 us
    ppermute x4, waiting for transfers between devices, passed_along(): lax.ppermute(array, axis, [(i, (i + by) % count) for i in range(count)])  18.1 us
    all_to_all x1, blocking collectives, swap(): return lax.all_to_all(parts, axis, 0, 0, axis_index_groups=groups)  12.1 us
    all_to_all x3, waiting for transfers between devices, swap(): return lax.all_to_all(parts, axis, 0, 0, axis_index_groups=groups)  6.53 us
    ppermute x1, starting transfers between devices, to_partner(): lax.ppermute(array, 'emb', [(i, i ^ 1) for i in range(lax.axis_size('emb'...  4.08 us
  transfers between devices with their start and end apart: 8, of which 2 were waited for; matrix products, arithmetic and copies ran while one was open for 6% of the time, Pallas kernels for 0%

profile of v7, /device:TPU:1, one launch (start us, length us, event | category | flops | bytes accessed | tf_op | source)
XLA Modules:
  0.0 133.4 jit_solution(12426136374074730598)
XLA Ops:
  0.6 4.1 %collective-permute-start = (bf16[64,1152]{1,0:T(8,128)(2,1)}, bf16[64,1152]{1,0:T(8,128)(2,1)S(1)}, u32[]{:S(2)}, u32[]{:S(2)}) collective-permute-start(bf16[64,1152]{1,0:T(8,128)(2,1)} %param.7), channel_id=1, source_target_pairs={{0,1},{1,0},{2,3},{3,2},{4,5},{5,4},{6,7},{7,6},{8,9},{9,8},{10,11... | collective-permute-start | bytes 442376 | tf_op jit(solution)/shard_map/ppermute | solution.py:19
  4.7 1.0 fusion.37
  7.1 1.0 fusion.33
  8.1 1.5 %convolution_convert_fusion.1 = bf16[144,512]{1,0:T(8,128)(2,1)S(1)} fusion(bf16[1152,144]{0,1:T(8,128)(2,1)} %param.6, bf16[512,1152]{1,0:T(8,128)(2,1)S(1)} %copy-done), kind=kOutput, calls=%fused_computation.21 | convolution fusion | flops 169943040 | bytes 1658880 | tf_op jit(solution)/shard_map/dot_general | solution.py:95
  9.7 1.1 broadcast_in_dim.20
  10.8 0.1 fusion.38
  10.9 4.2 %all-to-all-start = ((bf16[8,144,512]{2,1,0:T(8,128)(2,1)}), bf16[8,144,512]{2,1,0:T(8,128)(2,1)S(1)}, u32[]{:S(2)}, u32[]{:S(2)}) async-start(bf16[8,144,512]{2,1,0:T(8,128)(2,1)} %broadcast_in_dim.20), calls=%async_computation | async-start | bytes 2359296 | tf_op jit(solution)/shard_map/all_to_all | solution.py:34
  15.2 3.5 %collective-permute-start.2 = (bf16[128,1152]{1,0:T(8,128)(2,1)S(1)}, bf16[128,1152]{1,0:T(8,128)(2,1)S(1)}, u32[]{:S(2)}, u32[]{:S(2)}) collective-permute-start(bf16[128,1152]{1,0:T(8,128)(2,1)S(1)} %pad_maximum_fusion.1), channel_id=1, source_target_pairs={{0,16},{8,24},{16,32},{24,40},{32,48},{40,56},{48,64},{56,72},{64,... | collective-permute-start | bytes 884744 | tf_op jit(solution)/shard_map/ppermute | solution.py:15
  18.8 5.2 %collective-permute-start.1 = (bf16[128,1152]{1,0:T(8,128)(2,1)S(1)}, bf16[128,1152]{1,0:T(8,128)(2,1)S(1)}, u32[]{:S(2)}, u32[]{:S(2)}) collective-permute-start(bf16[128,1152]{1,0:T(8,128)(2,1)S(1)} %pad_maximum_fusion.1), channel_id=1, source_target_pairs={{0,8},{8,16},{16,24},{24,32},{32,40},{40,48},{48,56},{56,64},{64,7... | collective-permute-start | bytes 884744 | tf_op jit(solution)/shard_map/ppermute | solution.py:15
  24.1 18.0 %collective-permute-done.2 = bf16[128,1152]{1,0:T(8,128)(2,1)S(1)} collective-permute-done((bf16[128,1152]{1,0:T(8,128)(2,1)S(1)}, bf16[128,1152]{1,0:T(8,128)(2,1)S(1)}, u32[]{:S(2)}, u32[]{:S(2)}) %collective-permute-start.2) | collective-permute-done | bytes 294944 | tf_op jit(solution)/shard_map/ppermute | solution.py:15
  42.1 0.7 copy-done.2
  42.8 0.7 copy-done.3
  43.6 0.2 fusion.11
  43.8 0.6 multiply_reduce_fusion.1
  44.4 0.8 fusion.1
  45.2 12.1 %all_to_all.20 = bf16[8,144,256]{2,1,0:T(8,128)(2,1)S(1)} all-to-all(bf16[8,144,256]{2,1,0:T(8,128)(2,1)S(1)} %bitcast.40), channel_id=1, replica_groups=mesh['dp'=128,'emb'=8] {'emb'}, dimensions={0} | all-to-all | bytes 1179648 | tf_op jit(solution)/shard_map/all_to_all | solution.py:34
  57.4 0.4 convolution_convert_fusion
  57.9 0.8 pad.4
  58.6 9.6 %all-to-all-start.2 = ((bf16[8,168,128]{2,1,0:T(8,128)(2,1)}), bf16[8,168,128]{2,1,0:T(8,128)(2,1)S(1)}, u32[]{:S(2)}, u32[]{:S(2)}) async-start(bf16[8,168,128]{2,1,0:T(8,128)(2,1)} %bitcast.7), calls=%async_computation.2 | async-start | bytes 688128 | tf_op jit(solution)/shard_map/all_to_all | solution.py:34
  68.3 0.3 multiply_reduce_fusion
  68.6 2.0 %fusion.58 = (bf16[192,1152]{1,0:T(8,128)(2,1)}, f32[192,1152]{1,0:T(8,128)}) fusion(bf16[1152,512]{1,0:T(8,128)(2,1)S(1)} %bitcast.35, f32[512]{0:T(512)S(1)} %add_rsqrt_fusion, bf16[64,1152]{1,0:T(8,128)(2,1)S(1)} %slice-done, bf16[64,1152]{1,0:T(8,128)(2,1)S(1)} %slice-done.1, bf16[64,1152]{1,0:T(8,128)(2,1)S(1)} %fusion.33, f32[]{:T(128)} %bitcast.30, ...), kind=kOutput, calls=%fused_computation.95 | convolution fusion | flops 459472896 | bytes 2952136 | tf_op jit(solution)/shard_map/dot_general | solution.py:134
  70.6 1.0 fusion.57
  71.7 7.7 %collective-permute-start.4 = (bf16[64,1152]{1,0:T(8,128)(2,1)S(1)}, bf16[64,1152]{1,0:T(8,128)(2,1)S(1)}, u32[]{:S(2)}, u32[]{:S(2)}) collective-permute-start(bf16[64,1152]{1,0:T(8,128)(2,1)S(1)} %get-tuple-element.12), channel_id=1, source_target_pairs={{0,1008},{8,1016},{16,0},{24,8},{32,16},{40,24},{48,32},{56,40},{6... | collective-permute-start | bytes 442376 | tf_op jit(solution)/shard_map/ppermute | solution.py:15
  79.4 2.5 %collective-permute-start.3 = (bf16[64,1152]{1,0:T(8,128)(2,1)S(1)}, bf16[64,1152]{1,0:T(8,128)(2,1)S(1)}, u32[]{:S(2)}, u32[]{:S(2)}) collective-permute-start(bf16[64,1152]{1,0:T(8,128)(2,1)S(1)} %get-tuple-element.13), channel_id=1, source_target_pairs={{0,1016},{8,0},{16,8},{24,16},{32,24},{40,32},{48,40},{56,48},{64,... | collective-permute-start | bytes 442376 | tf_op jit(solution)/shard_map/ppermute | solution.py:15
  82.0 29.1 %all-gather = bf16[2688,128]{1,0:T(8,128)(2,1)S(1)} all-gather(bf16[168,128]{1,0:T(8,128)(2,1)S(1)} %reduce_sum.95), channel_id=2, replica_groups={{0,32,64,96,128,160,192,224,256,288,320,352,384,416,448,480},{8,40,72,1..., dimensions={0}, use_global_device_ids=true | all-gather | bytes 731136 | tf_op jit(solution)/shard_map/all_gather | solution.py:56
  111.1 0.1 reduce_sum.96
  111.3 0.8 broadcast_in_dim.39
  112.0 12.9 %all-to-all-start.3 = ((bf16[8,168,128]{2,1,0:T(8,128)(2,1)}), bf16[8,168,128]{2,1,0:T(8,128)(2,1)S(1)}, u32[]{:S(2)}, u32[]{:S(2)}) async-start(bf16[8,168,128]{2,1,0:T(8,128)(2,1)} %broadcast_in_dim.39), calls=%async_computation.3 | async-start | bytes 688128 | tf_op jit(solution)/shard_map/all_to_all | solution.py:34
  124.9 0.2 fusion.34
  125.1 0.8 fusion.36
  126.0 6.5 %all-to-all-done.3 = bf16[8,168,128]{2,1,0:T(8,128)(2,1)S(1)} async-done(((bf16[8,168,128]{2,1,0:T(8,128)(2,1)}), bf16[8,168,128]{2,1,0:T(8,128)(2,1)S(1)}, u32[]{:S(2)}, u32[]{:S(2)}) %all-to-all-start.3) | async-done | bytes 344096 | tf_op jit(solution)/shard_map/all_to_all | solution.py:34
  132.5 0.9 copy_bitcast_fusion
  (43 shorter events, 0.6 us)
Async XLA Ops:
  0.6 7.5 %copy-start = (bf16[512,1152]{1,0:T(8,128)(2,1)S(1)}, bf16[512,1152]{1,0:T(8,128)(2,1)}, u32[]{:S(2)}) copy-start(bf16[512,1152]{1,0:T(8,128)(2,1)} %param.5) | copy-start | bytes 3538948
  0.6 9.0 %collective-permute-start = (bf16[64,1152]{1,0:T(8,128)(2,1)}, bf16[64,1152]{1,0:T(8,128)(2,1)S(1)}, u32[]{:S(2)}, u32[]{:S(2)}) collective-permute-start(bf16[64,1152]{1,0:T(8,128)(2,1)} %param.7), channel_id=1, source_target_pairs={{0,1},{1,0},{2,3},{3,2},{4,5},{5,4},{6,7},{7,6},{8,9},{9,8},{10,11... | collective-permute-start | bytes 442376 | tf_op jit(solution)/shard_map/ppermute | solution.py:19
  10.9 32.7 %all-to-all-start = ((bf16[8,144,512]{2,1,0:T(8,128)(2,1)}), bf16[8,144,512]{2,1,0:T(8,128)(2,1)S(1)}, u32[]{:S(2)}, u32[]{:S(2)}) async-start(bf16[8,144,512]{2,1,0:T(8,128)(2,1)} %broadcast_in_dim.20), calls=%async_computation | async-start | bytes 2359296 | tf_op jit(solution)/shard_map/all_to_all | solution.py:34
  15.2 26.9 %collective-permute-start.2 = (bf16[128,1152]{1,0:T(8,128)(2,1)S(1)}, bf16[128,1152]{1,0:T(8,128)(2,1)S(1)}, u32[]{:S(2)}, u32[]{:S(2)}) collective-permute-start(bf16[128,1152]{1,0:T(8,128)(2,1)S(1)} %pad_maximum_fusion.1), channel_id=1, source_target_pairs={{0,16},{8,24},{16,32},{24,40},{32,48},{40,56},{48,64},{56,72},{64,... | collective-permute-start | bytes 884744 | tf_op jit(solution)/shard_map/ppermute | solution.py:15
  18.8 23.3 %collective-permute-start.1 = (bf16[128,1152]{1,0:T(8,128)(2,1)S(1)}, bf16[128,1152]{1,0:T(8,128)(2,1)S(1)}, u32[]{:S(2)}, u32[]{:S(2)}) collective-permute-start(bf16[128,1152]{1,0:T(8,128)(2,1)S(1)} %pad_maximum_fusion.1), channel_id=1, source_target_pairs={{0,8},{8,16},{16,24},{24,32},{32,40},{40,48},{48,56},{56,64},{64,7... | collective-permute-start | bytes 884744 | tf_op jit(solution)/shard_map/ppermute | solution.py:15
  42.1 0.7 copy-start.2
  42.8 0.7 copy-start.3
  58.6 10.0 %slice-start = ((bf16[128,1152]{1,0:T(8,128)(2,1)}), bf16[64,1152]{1,0:T(8,128)(2,1)S(1)}, s32[]{:S(2)}) async-start(bf16[128,1152]{1,0:T(8,128)(2,1)} %copy-done.2), calls=%async_computation.4 | async-start | bytes 294912 | tf_op jit(solution)/shard_map/slice | solution.py:127
  58.6 10.0 %slice-start.1 = ((bf16[128,1152]{1,0:T(8,128)(2,1)}), bf16[64,1152]{1,0:T(8,128)(2,1)S(1)}, s32[]{:S(2)}) async-start(bf16[128,1152]{1,0:T(8,128)(2,1)} %copy-done.3), calls=%async_computation.5 | async-start | bytes 294912 | tf_op jit(solution)/shard_map/slice | solution.py:127
  58.6 23.3 %all-to-all-start.2 = ((bf16[8,168,128]{2,1,0:T(8,128)(2,1)}), bf16[8,168,128]{2,1,0:T(8,128)(2,1)S(1)}, u32[]{:S(2)}, u32[]{:S(2)}) async-start(bf16[8,168,128]{2,1,0:T(8,128)(2,1)} %bitcast.7), calls=%async_computation.2 | async-start | bytes 688128 | tf_op jit(solution)/shard_map/all_to_all | solution.py:34
  71.7 39.6 %collective-permute-start.4 = (bf16[64,1152]{1,0:T(8,128)(2,1)S(1)}, bf16[64,1152]{1,0:T(8,128)(2,1)S(1)}, u32[]{:S(2)}, u32[]{:S(2)}) collective-permute-start(bf16[64,1152]{1,0:T(8,128)(2,1)S(1)} %get-tuple-element.12), channel_id=1, source_target_pairs={{0,1008},{8,1016},{16,0},{24,8},{32,16},{40,24},{48,32},{56,40},{6... | collective-permute-start | bytes 442376 | tf_op jit(solution)/shard_map/ppermute | solution.py:15
  79.4 31.9 %collective-permute-start.3 = (bf16[64,1152]{1,0:T(8,128)(2,1)S(1)}, bf16[64,1152]{1,0:T(8,128)(2,1)S(1)}, u32[]{:S(2)}, u32[]{:S(2)}) collective-permute-start(bf16[64,1152]{1,0:T(8,128)(2,1)S(1)} %get-tuple-element.13), channel_id=1, source_target_pairs={{0,1016},{8,0},{16,8},{24,16},{32,24},{40,32},{48,40},{56,48},{64,... | collective-permute-start | bytes 442376 | tf_op jit(solution)/shard_map/ppermute | solution.py:15
  82.0 42.9 %copy-start.1 = (bf16[64,1152]{1,0:T(8,128)(2,1)S(1)}, bf16[64,1152]{1,0:T(8,128)(2,1)}, u32[]{:S(2)}) copy-start(bf16[64,1152]{1,0:T(8,128)(2,1)} %param.7) | copy-start | bytes 442372
  82.0 42.9 %copy-start.4 = (f32[192,1152]{1,0:T(8,128)S(1)}, f32[192,1152]{1,0:T(8,128)}, u32[]{:S(2)}) copy-start(f32[192,1152]{1,0:T(8,128)} %get-tuple-element.21) | copy-start | bytes 2654212
  112.0 20.5 %all-to-all-start.3 = ((bf16[8,168,128]{2,1,0:T(8,128)(2,1)}), bf16[8,168,128]{2,1,0:T(8,128)(2,1)S(1)}, u32[]{:S(2)}, u32[]{:S(2)}) async-start(bf16[8,168,128]{2,1,0:T(8,128)(2,1)} %broadcast_in_dim.39), calls=%async_computation.3 | async-start | bytes 688128 | tf_op jit(solution)/shard_map/all_to_all | solution.py:34

commit v8 on v7

--- a/solution.py
+++ b/solution.py
@@ -96,7 +96,7 @@
         w_proj, img_feat, (((0,), (1,)), ((), ())), preferred_element_type=jnp.float32
     ).astype(jnp.bfloat16)
     copies = jnp.broadcast_to(local_proj[None], (members,) + local_proj.shape)
-    copies, partner_txt = lax.optimization_barrier((copies, partner_txt))
+    copies, txt_emb, partner_txt = lax.optimization_barrier((copies, txt_emb, partner_txt))
     unit_txt, inv_txt = unit_rows(txt_emb)
     pair_txt = jnp.concatenate([unit_txt, unit_rows(partner_txt)[0]], axis=0).astype(jnp.bfloat16)
     visitors = [pair_txt] + [passed_along(pair_txt, "dp", k) for k in range(1, STEPS)]
@@ -121,9 +121,6 @@
     parts = grad_proj.astype(jnp.bfloat16).reshape(members, width, half_rows)
     parts = swap(parts, "emb").reshape(members // PAIR, PAIR, width, half_rows)
     grad_part = summed(parts).astype(jnp.bfloat16)
-    grad_part = jnp.concatenate([grad_part[h] for h in range(PAIR)], axis=1)
-    local_weight = jnp.dot(grad_part, img_feat, preferred_element_type=jnp.float32)
-
     own_texts = jnp.concatenate([visitor[:text_rows] for visitor in visitors], axis=0)
     z_img = unit_columns(projected)[0].astype(jnp.bfloat16)
     own_grad = slopes(
@@ -134,6 +131,10 @@
     txt_terms = scale * lax.dot_general(
         own_grad, z_img, (((1,), (1,)), ((), ())), preferred_element_type=jnp.float32
     )
+    grad_part, txt_terms = lax.optimization_barrier((grad_part, txt_terms))
+    grad_part = jnp.concatenate([grad_part[h] for h in range(PAIR)], axis=1)
+    local_weight = jnp.dot(grad_part, img_feat, preferred_element_type=jnp.float32)
+
     sent = [
         passed_along(txt_terms[k * text_rows : (k + 1) * text_rows].astype(jnp.bfloat16), "dp", -k)
         for k in range(1, STEPS)

time: 134 us -> 134 us (level)
  blocking collectives: 41.2 us -> 29.2 us
  starting transfers between devices: 49.9 us -> 55 us
  waiting for transfers between devices: 24.6 us -> 28 us
  other arithmetic: 5.1 us -> 7.03 us
  matrix products: 5.26 us -> 6.78 us
    all_to_all x1 -> x0, blocking collectives: 12.1 us -> none  [swap(): return lax.all_to_all(parts, axis, 0, 0, axis_index_groups=groups)]
    all_to_all x3 -> x4, starting transfers between devices: 26.7 us -> 33.7 us  [swap(): return lax.all_to_all(parts, axis, 0, 0, axis_index_groups=groups)]
    all_to_all x3 -> x4, waiting for transfers between devices: 6.53 us -> 12.2 us  [swap(): return lax.all_to_all(parts, axis, 0, 0, axis_index_groups=groups)]
    ppermute x4, waiting for transfers between devices: 18.1 us -> 15.8 us  [passed_along(): lax.ppermute(array, axis, [(i, (i + by) % count) for i in range(count)])]
    ppermute x4, starting transfers between devices: 19.1 us -> 17.2 us  [passed_along(): lax.ppermute(array, axis, [(i, (i + by) % count) for i in range(count)])]
    unnamed x18 -> x22, local copies, waits for them, and re-layouts: 1.52 us -> 0.12 us
    slice x4 -> x2, local copies, waits for them, and re-layouts: 0.01 us -> 1.35 us  [local(): visitor[:text_rows]]
  transfers between devices with their start and end apart: 8 -> 9, of which waited for: 2 -> 3; matrix products, arithmetic and copies ran while one was open for 6% -> 8% of each run, Pallas kernels for 0% -> 0%
where the time goes in v8:
time: 134 us; the launch traced here: 133 us
  starting transfers between devices  55 us (41%)
  blocking collectives  29.2 us (22%)
  waiting for transfers between devices  28 us (21%)
  other arithmetic  7.03 us (5%)
  matrix products  6.78 us (5%)
  local copies, waits for them, and re-layouts  4.84 us (4%)
  between operations  2.22 us (2%)
    all_to_all x4, starting transfers between devices, swap(): return lax.all_to_all(parts, axis, 0, 0, axis_index_groups=groups)  33.7 us
    all_gather x1, blocking collectives, sum_over_dp(): lax.all_gather(part, 'dp', axis=0, axis_index_groups=far)  29.2 us
    ppermute x4, starting transfers between devices, passed_along(): lax.ppermute(array, axis, [(i, (i + by) % count) for i in range(count)])  17.2 us
    ppermute x4, waiting for transfers between devices, passed_along(): lax.ppermute(array, axis, [(i, (i + by) % count) for i in range(count)])  15.8 us
    all_to_all x4, waiting for transfers between devices, swap(): return lax.all_to_all(parts, axis, 0, 0, axis_index_groups=groups)  12.2 us
    ppermute x1, starting transfers between devices, to_partner(): lax.ppermute(array, 'emb', [(i, i ^ 1) for i in range(lax.axis_size('emb'...  4.08 us
  transfers between devices with their start and end apart: 9, of which 3 were waited for; matrix products, arithmetic and copies ran while one was open for 8% of the time, Pallas kernels for 0%

profile of v8, /device:TPU:1, one launch (start us, length us, event | category | flops | bytes accessed | tf_op | source)
XLA Modules:
  0.0 133.1 jit_solution(6892878064804225578)
XLA Ops:
  0.6 4.1 %collective-permute-start = (bf16[64,1152]{1,0:T(8,128)(2,1)}, bf16[64,1152]{1,0:T(8,128)(2,1)S(1)}, u32[]{:S(2)}, u32[]{:S(2)}) collective-permute-start(bf16[64,1152]{1,0:T(8,128)(2,1)} %param.7), channel_id=1, source_target_pairs={{0,1},{1,0},{2,3},{3,2},{4,5},{5,4},{6,7},{7,6},{8,9},{9,8},{10,11... | collective-permute-start | bytes 442376 | tf_op jit(solution)/shard_map/ppermute | solution.py:19
  4.8 1.5 %convolution_convert_fusion.1 = bf16[144,512]{1,0:T(8,128)(2,1)S(1)} fusion(bf16[1152,144]{0,1:T(8,128)(2,1)} %param.6, bf16[512,1152]{1,0:T(8,128)(2,1)S(1)} %copy-done), kind=kOutput, calls=%fused_computation.21 | convolution fusion | flops 169943040 | bytes 1658880 | tf_op jit(solution)/shard_map/dot_general | solution.py:95
  7.6 0.6 iota_compare_fusion.3
  8.2 1.1 broadcast_in_dim.20
  9.5 5.3 %all-to-all-start = ((bf16[8,144,512]{2,1,0:T(8,128)(2,1)}), bf16[8,144,512]{2,1,0:T(8,128)(2,1)S(1)}, u32[]{:S(2)}, u32[]{:S(2)}) async-start(bf16[8,144,512]{2,1,0:T(8,128)(2,1)} %broadcast_in_dim.20), calls=%async_computation | async-start | bytes 2359296 | tf_op jit(solution)/shard_map/all_to_all | solution.py:34
  15.1 3.5 %collective-permute-start.2 = (bf16[128,1152]{1,0:T(8,128)(2,1)S(1)}, bf16[128,1152]{1,0:T(8,128)(2,1)S(1)}, u32[]{:S(2)}, u32[]{:S(2)}) collective-permute-start(bf16[128,1152]{1,0:T(8,128)(2,1)S(1)} %pad_maximum_fusion.1), channel_id=1, source_target_pairs={{0,16},{8,24},{16,32},{24,40},{32,48},{40,56},{48,64},{56,72},{64,... | collective-permute-start | bytes 884744 | tf_op jit(solution)/shard_map/ppermute | solution.py:15
  18.6 5.5 %collective-permute-start.1 = (bf16[128,1152]{1,0:T(8,128)(2,1)S(1)}, bf16[128,1152]{1,0:T(8,128)(2,1)S(1)}, u32[]{:S(2)}, u32[]{:S(2)}) collective-permute-start(bf16[128,1152]{1,0:T(8,128)(2,1)S(1)} %pad_maximum_fusion.1), channel_id=1, source_target_pairs={{0,8},{8,16},{16,24},{24,32},{32,40},{40,48},{48,56},{56,64},{64,7... | collective-permute-start | bytes 884744 | tf_op jit(solution)/shard_map/ppermute | solution.py:15
  24.2 0.6 iota_compare_fusion.4
  24.8 0.6 iota_add_fusion.1
  25.4 15.8 %collective-permute-done.2 = bf16[128,1152]{1,0:T(8,128)(2,1)S(1)} collective-permute-done((bf16[128,1152]{1,0:T(8,128)(2,1)S(1)}, bf16[128,1152]{1,0:T(8,128)(2,1)S(1)}, u32[]{:S(2)}, u32[]{:S(2)}) %collective-permute-start.2) | collective-permute-done | bytes 294944 | tf_op jit(solution)/shard_map/ppermute | solution.py:15
  41.1 1.1 pad_maximum_fusion
  42.2 0.7 slice.84
  42.9 0.7 slice.83
  43.8 1.3 multiply_reduce_fusion.1
  45.1 1.6 %fusion.1 = bf16[1152,256]{1,0:T(8,128)(2,1)} fusion(bf16[384,1152]{1,0:T(8,128)(2,1)S(1)} %copy-done.2, f32[256]{0:T(256)S(1)} %get-tuple-element.24, f32[256]{0:T(256)S(1)} %get-tuple-element.23, f32[256]{0:T(256)S(1)} %get-tuple-element.22, bf16[1152,512]{1,0:T(8,128)(2,1)S(1)} %bitcast.34, s32[]{:T(128)S(6)} %select_n.19, ...), kind=kOutput, calls=%fused_computation.3 | convolution fusion | flops 229736448 | bytes 2465548 | tf_op jit(solution)/shard_map/dot_general | solution.py:117
  46.7 4.4 %all-to-all-start.1 = ((bf16[8,144,256]{2,1,0:T(8,128)(2,1)}), bf16[8,144,256]{2,1,0:T(8,128)(2,1)}, u32[]{:S(2)}, u32[]{:S(2)}) async-start(bf16[8,144,256]{2,1,0:T(8,128)(2,1)} %bitcast.39), calls=%async_computation.1 | async-start | bytes 1179648 | tf_op jit(solution)/shard_map/all_to_all | solution.py:34
  51.1 0.3 multiply_reduce_fusion
  51.4 2.0 %convolution_multiply_fusion = f32[192,1152]{1,0:T(8,128)S(1)} fusion(bf16[1152,512]{1,0:T(8,128)(2,1)S(1)} %bitcast.35, f32[512]{0:T(512)S(1)} %add_rsqrt_fusion, bf16[64,1152]{1,0:T(8,128)(2,1)} %slice.84, bf16[64,1152]{1,0:T(8,128)(2,1)} %slice.83, bf16[64,1152]{1,0:T(8,128)(2,1)S(1)} %get-tuple-element.26, f32[]{:T(128)} %bitcast.27, f32[]{:T(128)} %bitcast.30, ...), kind=kOutput, calls=%fused_computation.2 | convolution fusion | flops 459251712 | bytes 2509768 | tf_op jit(solution)/shard_map/dot_general | solution.py:131
  53.4 5.7 %all-to-all-done.1 = bf16[8,144,256]{2,1,0:T(8,128)(2,1)} async-done(((bf16[8,144,256]{2,1,0:T(8,128)(2,1)}), bf16[8,144,256]{2,1,0:T(8,128)(2,1)}, u32[]{:S(2)}, u32[]{:S(2)}) %all-to-all-start.1) | async-done | bytes 589856 | tf_op jit(solution)/shard_map/all_to_all | solution.py:34
  59.1 1.2 reduce_sum.94
  60.3 0.4 convolution_convert_fusion
  60.8 0.8 pad.4
  61.5 11.1 %all-to-all-start.2 = ((bf16[8,168,128]{2,1,0:T(8,128)(2,1)}), bf16[8,168,128]{2,1,0:T(8,128)(2,1)S(1)}, u32[]{:S(2)}, u32[]{:S(2)}) async-start(bf16[8,168,128]{2,1,0:T(8,128)(2,1)} %bitcast.7), calls=%async_computation.2 | async-start | bytes 688128 | tf_op jit(solution)/shard_map/all_to_all | solution.py:34
  72.7 0.7 fusion.56
  73.4 5.6 %collective-permute-start.4 = (bf16[64,1152]{1,0:T(8,128)(2,1)}, bf16[64,1152]{1,0:T(8,128)(2,1)S(1)}, u32[]{:S(2)}, u32[]{:S(2)}) collective-permute-start(bf16[64,1152]{1,0:T(8,128)(2,1)} %get-tuple-element.18), channel_id=1, source_target_pairs={{0,1008},{8,1016},{16,0},{24,8},{32,16},{40,24},{48,32},{56,40},{6... | collective-permute-start | bytes 442376 | tf_op jit(solution)/shard_map/ppermute | solution.py:15
  79.1 2.5 %collective-permute-start.3 = (bf16[64,1152]{1,0:T(8,128)(2,1)S(1)}, bf16[64,1152]{1,0:T(8,128)(2,1)S(1)}, u32[]{:S(2)}, u32[]{:S(2)}) collective-permute-start(bf16[64,1152]{1,0:T(8,128)(2,1)S(1)} %get-tuple-element.19), channel_id=1, source_target_pairs={{0,1016},{8,0},{16,8},{24,16},{32,24},{40,32},{48,40},{56,48},{64,... | collective-permute-start | bytes 442376 | tf_op jit(solution)/shard_map/ppermute | solution.py:15
  81.7 29.2 %all-gather = bf16[2688,128]{1,0:T(8,128)(2,1)S(1)} all-gather(bf16[168,128]{1,0:T(8,128)(2,1)S(1)} %reduce_sum.96), channel_id=2, replica_groups={{0,32,64,96,128,160,192,224,256,288,320,352,384,416,448,480},{8,40,72,1..., dimensions={0}, use_global_device_ids=true | all-gather | bytes 731136 | tf_op jit(solution)/shard_map/all_gather | solution.py:56
  111.0 0.8 broadcast_in_dim.39
  111.8 12.8 %all-to-all-start.3 = ((bf16[8,168,128]{2,1,0:T(8,128)(2,1)}), bf16[8,168,128]{2,1,0:T(8,128)(2,1)S(1)}, u32[]{:S(2)}, u32[]{:S(2)}) async-start(bf16[8,168,128]{2,1,0:T(8,128)(2,1)} %broadcast_in_dim.39), calls=%async_computation.3 | async-start | bytes 688128 | tf_op jit(solution)/shard_map/all_to_all | solution.py:34
  124.8 0.8 fusion.36
  125.6 6.5 %all-to-all-done.3 = bf16[8,168,128]{2,1,0:T(8,128)(2,1)S(1)} async-done(((bf16[8,168,128]{2,1,0:T(8,128)(2,1)}), bf16[8,168,128]{2,1,0:T(8,128)(2,1)S(1)}, u32[]{:S(2)}, u32[]{:S(2)}) %all-to-all-start.3) | async-done | bytes 344096 | tf_op jit(solution)/shard_map/all_to_all | solution.py:34
  132.2 0.9 copy_bitcast_fusion
  (46 shorter events, 1.2 us)
Async XLA Ops:
  0.6 4.1 %copy-start = (bf16[512,1152]{1,0:T(8,128)(2,1)S(1)}, bf16[512,1152]{1,0:T(8,128)(2,1)}, u32[]{:S(2)}) copy-start(bf16[512,1152]{1,0:T(8,128)(2,1)} %param.5) | copy-start | bytes 3538948
  0.6 7.6 %collective-permute-start = (bf16[64,1152]{1,0:T(8,128)(2,1)}, bf16[64,1152]{1,0:T(8,128)(2,1)S(1)}, u32[]{:S(2)}, u32[]{:S(2)}) collective-permute-start(bf16[64,1152]{1,0:T(8,128)(2,1)} %param.7), channel_id=1, source_target_pairs={{0,1},{1,0},{2,3},{3,2},{4,5},{5,4},{6,7},{7,6},{8,9},{9,8},{10,11... | collective-permute-start | bytes 442376 | tf_op jit(solution)/shard_map/ppermute | solution.py:19
  4.8 4.6 %copy-start.1 = (bf16[64,1152]{1,0:T(8,128)(2,1)S(1)}, bf16[64,1152]{1,0:T(8,128)(2,1)}, u32[]{:S(2)}) copy-start(bf16[64,1152]{1,0:T(8,128)(2,1)} %param.7) | copy-start | bytes 442372
  9.5 34.1 %all-to-all-start = ((bf16[8,144,512]{2,1,0:T(8,128)(2,1)}), bf16[8,144,512]{2,1,0:T(8,128)(2,1)S(1)}, u32[]{:S(2)}, u32[]{:S(2)}) async-start(bf16[8,144,512]{2,1,0:T(8,128)(2,1)} %broadcast_in_dim.20), calls=%async_computation | async-start | bytes 2359296 | tf_op jit(solution)/shard_map/all_to_all | solution.py:34
  15.1 26.1 %collective-permute-start.2 = (bf16[128,1152]{1,0:T(8,128)(2,1)S(1)}, bf16[128,1152]{1,0:T(8,128)(2,1)S(1)}, u32[]{:S(2)}, u32[]{:S(2)}) collective-permute-start(bf16[128,1152]{1,0:T(8,128)(2,1)S(1)} %pad_maximum_fusion.1), channel_id=1, source_target_pairs={{0,16},{8,24},{16,32},{24,40},{32,48},{40,56},{48,64},{56,72},{64,... | collective-permute-start | bytes 884744 | tf_op jit(solution)/shard_map/ppermute | solution.py:15
  18.6 22.5 %collective-permute-start.1 = (bf16[128,1152]{1,0:T(8,128)(2,1)S(1)}, bf16[128,1152]{1,0:T(8,128)(2,1)S(1)}, u32[]{:S(2)}, u32[]{:S(2)}) collective-permute-start(bf16[128,1152]{1,0:T(8,128)(2,1)S(1)} %pad_maximum_fusion.1), channel_id=1, source_target_pairs={{0,8},{8,16},{16,24},{24,32},{32,40},{40,48},{48,56},{56,64},{64,7... | collective-permute-start | bytes 884744 | tf_op jit(solution)/shard_map/ppermute | solution.py:15
  42.2 1.6 %copy-start.2 = (bf16[384,1152]{1,0:T(8,128)(2,1)S(1)}, bf16[384,1152]{1,0:T(8,128)(2,1)}, u32[]{:S(2)}) copy-start(bf16[384,1152]{1,0:T(8,128)(2,1)} %pad_maximum_fusion) | copy-start | bytes 2654212
  43.8 1.3 copy-start.4
  43.8 1.3 copy-start.5
  46.7 4.7 %copy-start.3 = (s32[192]{0:T(256)S(1)}, s32[192]{0:T(256)}, u32[]{:S(2)}) copy-start(s32[192]{0:T(256)} %iota_add_fusion.1) | copy-start | bytes 2308
  46.7 4.7 %copy-start.6 = (pred[192]{0:T(512)(128)(4,1)S(1)}, pred[192]{0:T(512)(128)(4,1)}, u32[]{:S(2)}) copy-start(pred[192]{0:T(512)(128)(4,1)} %iota_compare_fusion.4) | copy-start | bytes 580
  46.7 12.4 %all-to-all-start.1 = ((bf16[8,144,256]{2,1,0:T(8,128)(2,1)}), bf16[8,144,256]{2,1,0:T(8,128)(2,1)}, u32[]{:S(2)}, u32[]{:S(2)}) async-start(bf16[8,144,256]{2,1,0:T(8,128)(2,1)} %bitcast.39), calls=%async_computation.1 | async-start | bytes 1179648 | tf_op jit(solution)/shard_map/all_to_all | solution.py:34
  61.5 20.1 %all-to-all-start.2 = ((bf16[8,168,128]{2,1,0:T(8,128)(2,1)}), bf16[8,168,128]{2,1,0:T(8,128)(2,1)S(1)}, u32[]{:S(2)}, u32[]{:S(2)}) async-start(bf16[8,168,128]{2,1,0:T(8,128)(2,1)} %bitcast.7), calls=%async_computation.2 | async-start | bytes 688128 | tf_op jit(solution)/shard_map/all_to_all | solution.py:34
  73.4 37.5 %collective-permute-start.4 = (bf16[64,1152]{1,0:T(8,128)(2,1)}, bf16[64,1152]{1,0:T(8,128)(2,1)S(1)}, u32[]{:S(2)}, u32[]{:S(2)}) collective-permute-start(bf16[64,1152]{1,0:T(8,128)(2,1)} %get-tuple-element.18), channel_id=1, source_target_pairs={{0,1008},{8,1016},{16,0},{24,8},{32,16},{40,24},{48,32},{56,40},{6... | collective-permute-start | bytes 442376 | tf_op jit(solution)/shard_map/ppermute | solution.py:15
  79.1 31.9 %collective-permute-start.3 = (bf16[64,1152]{1,0:T(8,128)(2,1)S(1)}, bf16[64,1152]{1,0:T(8,128)(2,1)S(1)}, u32[]{:S(2)}, u32[]{:S(2)}) collective-permute-start(bf16[64,1152]{1,0:T(8,128)(2,1)S(1)} %get-tuple-element.19), channel_id=1, source_target_pairs={{0,1016},{8,0},{16,8},{24,16},{32,24},{40,32},{48,40},{56,48},{64,... | collective-permute-start | bytes 442376 | tf_op jit(solution)/shard_map/ppermute | solution.py:15
  111.8 20.4 %all-to-all-start.3 = ((bf16[8,168,128]{2,1,0:T(8,128)(2,1)}), bf16[8,168,128]{2,1,0:T(8,128)(2,1)S(1)}, u32[]{:S(2)}, u32[]{:S(2)}) async-start(bf16[8,168,128]{2,1,0:T(8,128)(2,1)} %broadcast_in_dim.39), calls=%async_computation.3 | async-start | bytes 688128 | tf_op jit(solution)/shard_map/all_to_all | solution.py:34

commit v9 on v7

--- a/solution.py
+++ b/solution.py
@@ -36,6 +36,11 @@
 
 def gathered(part, count, axis, groups=None):
     return swap(jnp.broadcast_to(part[None], (count,) + part.shape), axis, groups)
+
+
+def repeated(blocks, times):
+    copies = jnp.broadcast_to(blocks[None], (times,) + blocks.shape)
+    return copies.reshape((times * blocks.shape[0],) + blocks.shape[1:])
 
 
 def summed(parts):
@@ -91,20 +96,20 @@
         grads = -signs * jax.nn.sigmoid(-signs * (scale * cosines + offset))
         return cosines, grads.astype(jnp.bfloat16)
 
-    partner_txt = to_partner(txt_emb)
+    pair_txt = jnp.concatenate([txt_emb, to_partner(txt_emb)], axis=0)
     local_proj = lax.dot_general(
         w_proj, img_feat, (((0,), (1,)), ((), ())), preferred_element_type=jnp.float32
     ).astype(jnp.bfloat16)
-    copies = jnp.broadcast_to(local_proj[None], (members,) + local_proj.shape)
-    copies, partner_txt = lax.optimization_barrier((copies, partner_txt))
-    unit_txt, inv_txt = unit_rows(txt_emb)
-    pair_txt = jnp.concatenate([unit_txt, unit_rows(partner_txt)[0]], axis=0).astype(jnp.bfloat16)
+    halves = [local_proj[:, h * half_rows : (h + 1) * half_rows] for h in range(PAIR)]
+    wanted = repeated(jnp.stack(halves), members // PAIR)
+    others = repeated(jnp.stack(halves[::-1]), members // PAIR)
+    wanted, pair_txt = lax.optimization_barrier((wanted, pair_txt))
     visitors = [pair_txt] + [passed_along(pair_txt, "dp", k) for k in range(1, STEPS)]
-    projected = swap(copies, "emb").reshape(features, image_rows)
+    mine = swap(wanted, "emb").reshape(features, half_rows)
 
-    mine = lax.dynamic_slice_in_dim(projected, first_row, half_rows, 1)
     unit_img, inv_img = unit_columns(mine)
-    texts = lax.optimization_barrier(jnp.concatenate(visitors, axis=0))
+    z_img = unit_img.astype(jnp.bfloat16)
+    texts = unit_rows(jnp.concatenate(visitors, axis=0))[0].astype(jnp.bfloat16)
 
     def pair_matches(text, image):
         row = image + first_row
@@ -112,32 +117,37 @@
         other = (text >= text_rows) & (text < PAIR * text_rows)
         return own | (other & (row == (member ^ 1) * text_rows + text - text_rows))
 
-    cosines, pair_grad = slopes(texts, unit_img.astype(jnp.bfloat16), pair_matches)
+    cosines, pair_grad = slopes(texts, z_img, pair_matches)
     inner_img = jnp.sum(pair_grad.astype(jnp.float32) * cosines, axis=0, keepdims=True)
     grad_img = lax.dot_general(
         texts, pair_grad, (((0,), (0,)), ((), ())), preferred_element_type=jnp.float32
     )
     grad_proj = (scale * inv_img) * (grad_img - unit_img * inner_img)
     parts = grad_proj.astype(jnp.bfloat16).reshape(members, width, half_rows)
+    parts, others = lax.optimization_barrier((parts, others))
     parts = swap(parts, "emb").reshape(members // PAIR, PAIR, width, half_rows)
     grad_part = summed(parts).astype(jnp.bfloat16)
     grad_part = jnp.concatenate([grad_part[h] for h in range(PAIR)], axis=1)
     local_weight = jnp.dot(grad_part, img_feat, preferred_element_type=jnp.float32)
 
-    own_texts = jnp.concatenate([visitor[:text_rows] for visitor in visitors], axis=0)
-    z_img = unit_columns(projected)[0].astype(jnp.bfloat16)
-    own_grad = slopes(
-        own_texts,
-        z_img,
-        lambda text, image: (text < text_rows) & (image == member * text_rows + text),
+    z_other = unit_columns(swap(others, "emb").reshape(features, half_rows))[0].astype(jnp.bfloat16)
+    starts = [k * PAIR * text_rows for k in range(STEPS)]
+    own_rows = lambda array: jnp.concatenate([array[i : i + text_rows] for i in starts], axis=0)
+    other_row = half_rows - first_row
+    other_grad = slopes(
+        own_rows(texts),
+        z_other,
+        lambda text, image: (text < text_rows) & (image + other_row == member * text_rows + text),
     )[1]
-    txt_terms = scale * lax.dot_general(
-        own_grad, z_img, (((1,), (1,)), ((), ())), preferred_element_type=jnp.float32
+    over_images = lambda grads, images: lax.dot_general(
+        grads, images, (((1,), (1,)), ((), ())), preferred_element_type=jnp.float32
     )
+    txt_terms = scale * (over_images(own_rows(pair_grad), z_img) + over_images(other_grad, z_other))
     sent = [
         passed_along(txt_terms[k * text_rows : (k + 1) * text_rows].astype(jnp.bfloat16), "dp", -k)
         for k in range(1, STEPS)
     ]
+    unit_txt, inv_txt = unit_rows(txt_emb)
     d_weight, sent = sum_over_dp(local_weight, sent)
 
     grad_txt = txt_terms[:text_rows]

time: 134 us -> 151 us (1.13)
  starting transfers between devices: 49.9 us -> 62.7 us
  waiting for transfers between devices: 24.6 us -> 32.9 us
  blocking collectives: 41.2 us -> 33.1 us
  matrix products: 5.26 us -> 6.82 us
    all_to_all x3 -> x5, waiting for transfers between devices: 6.53 us -> 20.6 us  [swap(): return lax.all_to_all(parts, axis, 0, 0, axis_index_groups=groups)]
    all_to_all x3 -> x5, starting transfers between devices: 26.7 us -> 39.8 us  [swap(): return lax.all_to_all(parts, axis, 0, 0, axis_index_groups=groups)]
    all_to_all x1 -> x0, blocking collectives: 12.1 us -> none  [swap(): return lax.all_to_all(parts, axis, 0, 0, axis_index_groups=groups)]
    ppermute x4, waiting for transfers between devices: 18.1 us -> 12.2 us  [passed_along(): lax.ppermute(array, axis, [(i, (i + by) % count) for i in range(count)])]
    all_gather x1, blocking collectives: 29.1 us -> 33.1 us  [sum_over_dp(): lax.all_gather(part, 'dp', axis=0, axis_index_groups=far)]
    slice x4 -> x2, local copies, waits for them, and re-layouts: 0.01 us -> 1.55 us  [local(): array[i:i + text_rows]]
    dot_general x1 -> x2, matrix products: 2.05 us -> 3.06 us  [local(): lax.dot_general(grads, images, (((1,), (1,)), ((), ())), preferred_elemen...]
  transfers between devices with their start and end apart: 8 -> 10, of which waited for: 2 -> 4; matrix products, arithmetic and copies ran while one was open for 6% -> 8% of each run, Pallas kernels for 0% -> 0%
where the time goes in v9:
time: 151 us; the launch traced here: 150 us
  starting transfers between devices  62.7 us (42%)
  blocking collectives  33.1 us (22%)
  waiting for transfers between devices  32.9 us (22%)
  matrix products  6.82 us (5%)
  other arithmetic  5.96 us (4%)
  local copies, waits for them, and re-layouts  5.92 us (4%)
  between operations  2.27 us (2%)
    all_to_all x5, starting transfers between devices, swap(): return lax.all_to_all(parts, axis, 0, 0, axis_index_groups=groups)  39.8 us
    all_gather x1, blocking collectives, sum_over_dp(): lax.all_gather(part, 'dp', axis=0, axis_index_groups=far)  33.1 us
    all_to_all x5, waiting for transfers between devices, swap(): return lax.all_to_all(parts, axis, 0, 0, axis_index_groups=groups)  20.6 us
    ppermute x4, starting transfers between devices, passed_along(): lax.ppermute(array, axis, [(i, (i + by) % count) for i in range(count)])  18.9 us
    ppermute x4, waiting for transfers between devices, passed_along(): lax.ppermute(array, axis, [(i, (i + by) % count) for i in range(count)])  12.2 us
    ppermute x1, starting transfers between devices, to_partner(): lax.ppermute(array, 'emb', [(i, i ^ 1) for i in range(lax.axis_size('emb'...  4.08 us
    dot_general x2, matrix products, local(): lax.dot_general(grads, images, (((1,), (1,)), ((), ())), preferred_elemen...  3.06 us
  transfers between devices with their start and end apart: 10, of which 4 were waited for; matrix products, arithmetic and copies ran while one was open for 8% of the time, Pallas kernels for 0%

profile of v9, /device:TPU:1, one launch (start us, length us, event | category | flops | bytes accessed | tf_op | source)
XLA Modules:
  0.0 149.6 jit_solution(4799402691595897480)
XLA Ops:
  0.7 4.1 %collective-permute-start = (bf16[64,1152]{1,0:T(8,128)(2,1)}, bf16[64,1152]{1,0:T(8,128)(2,1)S(1)}, u32[]{:S(2)}, u32[]{:S(2)}) collective-permute-start(bf16[64,1152]{1,0:T(8,128)(2,1)} %param.7), channel_id=1, source_target_pairs={{0,1},{1,0},{2,3},{3,2},{4,5},{5,4},{6,7},{7,6},{8,9},{9,8},{10,11... | collective-permute-start | bytes 442376 | tf_op jit(solution)/shard_map/ppermute | solution.py:19
  4.8 1.5 %convolution_convert_fusion.1 = bf16[144,512]{1,0:T(8,128)(2,1)S(1)} fusion(bf16[1152,144]{0,1:T(8,128)(2,1)} %param.6, bf16[512,1152]{1,0:T(8,128)(2,1)S(1)} %copy-done), kind=kOutput, calls=%fused_computation.15 | convolution fusion | flops 169943040 | bytes 1658880 | tf_op jit(solution)/shard_map/dot_general | solution.py:100
  7.7 0.9 broadcast_in_dim.22
  8.5 4.3 %collective-permute-start.2 = (bf16[128,1152]{1,0:T(8,128)(2,1)S(1)}, bf16[128,1152]{1,0:T(8,128)(2,1)S(1)}, u32[]{:S(2)}, u32[]{:S(2)}) collective-permute-start(bf16[128,1152]{1,0:T(8,128)(2,1)S(1)} %pad_maximum_fusion.1), channel_id=1, source_target_pairs={{0,16},{8,24},{16,32},{24,40},{32,48},{40,56},{48,64},{56,72},{64,... | collective-permute-start | bytes 884744 | tf_op jit(solution)/shard_map/ppermute | solution.py:15
  12.9 5.3 %collective-permute-start.1 = (bf16[128,1152]{1,0:T(8,128)(2,1)S(1)}, bf16[128,1152]{1,0:T(8,128)(2,1)S(1)}, u32[]{:S(2)}, u32[]{:S(2)}) collective-permute-start(bf16[128,1152]{1,0:T(8,128)(2,1)S(1)} %pad_maximum_fusion.1), channel_id=1, source_target_pairs={{0,8},{8,16},{16,24},{24,32},{32,40},{40,48},{48,56},{56,64},{64,7... | collective-permute-start | bytes 884744 | tf_op jit(solution)/shard_map/ppermute | solution.py:15
  18.1 0.5 iota_compare_fusion.2
  18.7 5.1 %all-to-all-start = ((bf16[8,144,256]{2,1,0:T(8,128)(2,1)}), bf16[8,144,256]{2,1,0:T(8,128)(2,1)S(1)}, u32[]{:S(2)}, u32[]{:S(2)}) async-start(bf16[8,144,256]{2,1,0:T(8,128)(2,1)} %bitcast.3), calls=%async_computation | async-start | bytes 1179648 | tf_op jit(solution)/shard_map/all_to_all | solution.py:34
  23.8 12.2 %collective-permute-done.2 = bf16[128,1152]{1,0:T(8,128)(2,1)S(1)} collective-permute-done((bf16[128,1152]{1,0:T(8,128)(2,1)S(1)}, bf16[128,1152]{1,0:T(8,128)(2,1)S(1)}, u32[]{:S(2)}, u32[]{:S(2)}) %collective-permute-start.2) | collective-permute-done | bytes 294944 | tf_op jit(solution)/shard_map/ppermute | solution.py:15
  36.2 0.5 copy-done.4
  36.7 1.2 fusion.4
  38.2 0.5 copy-done.7
  38.7 0.6 multiply_reduce_fusion.2
  39.3 1.3 fusion.2
  40.6 0.9 broadcast_in_dim.25
  41.5 4.2 %all-to-all-start.1 = ((bf16[8,144,256]{2,1,0:T(8,128)(2,1)}), bf16[8,144,256]{2,1,0:T(8,128)(2,1)S(1)}, u32[]{:S(2)}, u32[]{:S(2)}) async-start(bf16[8,144,256]{2,1,0:T(8,128)(2,1)} %bitcast.6), calls=%async_computation.1 | async-start | bytes 1179648 | tf_op jit(solution)/shard_map/all_to_all | solution.py:34
  45.7 7.9 %all-to-all-done.1 = bf16[8,144,256]{2,1,0:T(8,128)(2,1)S(1)} async-done(((bf16[8,144,256]{2,1,0:T(8,128)(2,1)}), bf16[8,144,256]{2,1,0:T(8,128)(2,1)S(1)}, u32[]{:S(2)}, u32[]{:S(2)}) %all-to-all-start.1) | async-done | bytes 589856 | tf_op jit(solution)/shard_map/all_to_all | solution.py:34
  53.6 3.5 %all-to-all-start.3 = ((bf16[8,144,256]{2,1,0:T(8,128)(2,1)}), bf16[8,144,256]{2,1,0:T(8,128)(2,1)S(1)}, u32[]{:S(2)}, u32[]{:S(2)}) async-start(bf16[8,144,256]{2,1,0:T(8,128)(2,1)} %bitcast.7), calls=%async_computation.3 | async-start | bytes 1179648 | tf_op jit(solution)/shard_map/all_to_all | solution.py:34
  57.8 0.8 pad.4
  58.5 6.4 %all-to-all-done.3 = bf16[8,144,256]{2,1,0:T(8,128)(2,1)S(1)} async-done(((bf16[8,144,256]{2,1,0:T(8,128)(2,1)}), bf16[8,144,256]{2,1,0:T(8,128)(2,1)S(1)}, u32[]{:S(2)}, u32[]{:S(2)}) %all-to-all-start.3) | async-done | bytes 589856 | tf_op jit(solution)/shard_map/all_to_all | solution.py:34
  65.0 15.9 %all-to-all-start.2 = ((bf16[8,168,128]{2,1,0:T(8,128)(2,1)}), bf16[8,168,128]{2,1,0:T(8,128)(2,1)}, u32[]{:S(2)}, u32[]{:S(2)}) async-start(bf16[8,168,128]{2,1,0:T(8,128)(2,1)} %bitcast.50), calls=%async_computation.2 | async-start | bytes 688128 | tf_op jit(solution)/shard_map/all_to_all | solution.py:34
  80.9 0.8 fusion.59
  81.6 0.8 fusion.61
  83.1 2.7 %fusion.62 = (bf16[192,1152]{1,0:T(8,128)(2,1)S(1)}, f32[192,1152]{1,0:T(8,128)}) fusion(f32[192,1152]{1,0:T(8,128)S(1)} %fusion.39, bf16[1152,256]{1,0:T(8,128)(2,1)S(1)} %fusion.5, bf16[64,1152]{1,0:T(8,128)(2,1)} %get-tuple-element.19, bf16[64,1152]{1,0:T(8,128)(2,1)} %get-tuple-element.20, bf16[64,1152]{1,0:T(8,128)(2,1)S(1)} %get-tuple-element.18, ...), kind=kOutput, calls=%fused_computation.105 | convolution fusion | flops 229072896 | bytes 3246024 | tf_op jit(solution)/shard_map/dot_general | solution.py:142
  85.8 1.9 %collective-permute-start.3 = (bf16[64,1152]{1,0:T(8,128)(2,1)S(1)}, bf16[64,1152]{1,0:T(8,128)(2,1)S(1)}, u32[]{:S(2)}, u32[]{:S(2)}) collective-permute-start(bf16[64,1152]{1,0:T(8,128)(2,1)S(1)} %get-tuple-element.24), channel_id=1, source_target_pairs={{0,1016},{8,0},{16,8},{24,16},{32,24},{40,32},{48,40},{56,48},{64,... | collective-permute-start | bytes 442376 | tf_op jit(solution)/shard_map/ppermute | solution.py:15
  87.8 7.4 %collective-permute-start.4 = (bf16[64,1152]{1,0:T(8,128)(2,1)S(1)}, bf16[64,1152]{1,0:T(8,128)(2,1)S(1)}, u32[]{:S(2)}, u32[]{:S(2)}) collective-permute-start(bf16[64,1152]{1,0:T(8,128)(2,1)S(1)} %get-tuple-element.23), channel_id=1, source_target_pairs={{0,1008},{8,1016},{16,0},{24,8},{32,16},{40,24},{48,32},{56,40},{6... | collective-permute-start | bytes 442376 | tf_op jit(solution)/shard_map/ppermute | solution.py:15
  95.2 1.0 reduce_sum.94
  96.2 33.1 %all-gather = bf16[2688,128]{1,0:T(8,128)(2,1)S(1)} all-gather(bf16[168,128]{1,0:T(8,128)(2,1)S(1)} %reduce_sum.94), channel_id=2, replica_groups={{0,32,64,96,128,160,192,224,256,288,320,352,384,416,448,480},{8,40,72,1..., dimensions={0}, use_global_device_ids=true | all-gather | bytes 731136 | tf_op jit(solution)/shard_map/all_gather | solution.py:61
  129.4 0.8 broadcast_in_dim.46
  130.2 11.0 %all-to-all-start.4 = ((bf16[8,168,128]{2,1,0:T(8,128)(2,1)}), bf16[8,168,128]{2,1,0:T(8,128)(2,1)S(1)}, u32[]{:S(2)}, u32[]{:S(2)}) async-start(bf16[8,168,128]{2,1,0:T(8,128)(2,1)} %broadcast_in_dim.46), calls=%async_computation.4 | async-start | bytes 688128 | tf_op jit(solution)/shard_map/all_to_all | solution.py:34
  141.5 0.8 fusion.29
  142.4 6.4 %all-to-all-done.4 = bf16[8,168,128]{2,1,0:T(8,128)(2,1)S(1)} async-done(((bf16[8,168,128]{2,1,0:T(8,128)(2,1)}), bf16[8,168,128]{2,1,0:T(8,128)(2,1)S(1)}, u32[]{:S(2)}, u32[]{:S(2)}) %all-to-all-start.4) | async-done | bytes 344096 | tf_op jit(solution)/shard_map/all_to_all | solution.py:34
  148.8 0.9 copy_bitcast_fusion
  (55 shorter events, 2.4 us)
Async XLA Ops:
  0.6 4.1 %copy-start = (bf16[512,1152]{1,0:T(8,128)(2,1)S(1)}, bf16[512,1152]{1,0:T(8,128)(2,1)}, u32[]{:S(2)}) copy-start(bf16[512,1152]{1,0:T(8,128)(2,1)} %param.5) | copy-start | bytes 3538948
  0.6 7.0 %copy-start.1 = (bf16[64,1152]{1,0:T(8,128)(2,1)S(1)}, bf16[64,1152]{1,0:T(8,128)(2,1)}, u32[]{:S(2)}) copy-start(bf16[64,1152]{1,0:T(8,128)(2,1)} %param.7) | copy-start | bytes 442372
  0.7 7.0 %collective-permute-start = (bf16[64,1152]{1,0:T(8,128)(2,1)}, bf16[64,1152]{1,0:T(8,128)(2,1)S(1)}, u32[]{:S(2)}, u32[]{:S(2)}) collective-permute-start(bf16[64,1152]{1,0:T(8,128)(2,1)} %param.7), channel_id=1, source_target_pairs={{0,1},{1,0},{2,3},{3,2},{4,5},{5,4},{6,7},{7,6},{8,9},{9,8},{10,11... | collective-permute-start | bytes 442376 | tf_op jit(solution)/shard_map/ppermute | solution.py:19
  8.5 27.5 %collective-permute-start.2 = (bf16[128,1152]{1,0:T(8,128)(2,1)S(1)}, bf16[128,1152]{1,0:T(8,128)(2,1)S(1)}, u32[]{:S(2)}, u32[]{:S(2)}) collective-permute-start(bf16[128,1152]{1,0:T(8,128)(2,1)S(1)} %pad_maximum_fusion.1), channel_id=1, source_target_pairs={{0,16},{8,24},{16,32},{24,40},{32,48},{40,56},{48,64},{56,72},{64,... | collective-permute-start | bytes 884744 | tf_op jit(solution)/shard_map/ppermute | solution.py:15
  12.9 23.1 %collective-permute-start.1 = (bf16[128,1152]{1,0:T(8,128)(2,1)S(1)}, bf16[128,1152]{1,0:T(8,128)(2,1)S(1)}, u32[]{:S(2)}, u32[]{:S(2)}) collective-permute-start(bf16[128,1152]{1,0:T(8,128)(2,1)S(1)} %pad_maximum_fusion.1), channel_id=1, source_target_pairs={{0,8},{8,16},{16,24},{24,32},{32,40},{40,48},{48,56},{56,64},{64,7... | collective-permute-start | bytes 884744 | tf_op jit(solution)/shard_map/ppermute | solution.py:15
  18.7 19.2 %all-to-all-start = ((bf16[8,144,256]{2,1,0:T(8,128)(2,1)}), bf16[8,144,256]{2,1,0:T(8,128)(2,1)S(1)}, u32[]{:S(2)}, u32[]{:S(2)}) async-start(bf16[8,144,256]{2,1,0:T(8,128)(2,1)} %bitcast.3), calls=%async_computation | async-start | bytes 1179648 | tf_op jit(solution)/shard_map/all_to_all | solution.py:34
  36.0 0.7 copy-start.4
  38.1 0.6 copy-start.7
  38.2 1.1 copy-start.2
  39.3 1.3 copy-start.5
  41.5 12.1 %all-to-all-start.1 = ((bf16[8,144,256]{2,1,0:T(8,128)(2,1)}), bf16[8,144,256]{2,1,0:T(8,128)(2,1)S(1)}, u32[]{:S(2)}, u32[]{:S(2)}) async-start(bf16[8,144,256]{2,1,0:T(8,128)(2,1)} %bitcast.6), calls=%async_computation.1 | async-start | bytes 1179648 | tf_op jit(solution)/shard_map/all_to_all | solution.py:34
  53.6 11.4 %all-to-all-start.3 = ((bf16[8,144,256]{2,1,0:T(8,128)(2,1)}), bf16[8,144,256]{2,1,0:T(8,128)(2,1)S(1)}, u32[]{:S(2)}, u32[]{:S(2)}) async-start(bf16[8,144,256]{2,1,0:T(8,128)(2,1)} %bitcast.7), calls=%async_computation.3 | async-start | bytes 1179648 | tf_op jit(solution)/shard_map/all_to_all | solution.py:34
  57.8 24.6 %copy-start.3 = (bf16[1152,256]{1,0:T(8,128)(2,1)S(1)}, bf16[1152,256]{1,0:T(8,128)(2,1)}, u32[]{:S(2)}) copy-start(bf16[1152,256]{1,0:T(8,128)(2,1)} %copy-done.2) | copy-start | bytes 1769476
  65.0 30.2 %all-to-all-start.2 = ((bf16[8,168,128]{2,1,0:T(8,128)(2,1)}), bf16[8,168,128]{2,1,0:T(8,128)(2,1)}, u32[]{:S(2)}, u32[]{:S(2)}) async-start(bf16[8,168,128]{2,1,0:T(8,128)(2,1)} %bitcast.50), calls=%async_computation.2 | async-start | bytes 688128 | tf_op jit(solution)/shard_map/all_to_all | solution.py:34
  85.8 43.5 %collective-permute-start.3 = (bf16[64,1152]{1,0:T(8,128)(2,1)S(1)}, bf16[64,1152]{1,0:T(8,128)(2,1)S(1)}, u32[]{:S(2)}, u32[]{:S(2)}) collective-permute-start(bf16[64,1152]{1,0:T(8,128)(2,1)S(1)} %get-tuple-element.24), channel_id=1, source_target_pairs={{0,1016},{8,0},{16,8},{24,16},{32,24},{40,32},{48,40},{56,48},{64,... | collective-permute-start | bytes 442376 | tf_op jit(solution)/shard_map/ppermute | solution.py:15
  87.8 41.6 %collective-permute-start.4 = (bf16[64,1152]{1,0:T(8,128)(2,1)S(1)}, bf16[64,1152]{1,0:T(8,128)(2,1)S(1)}, u32[]{:S(2)}, u32[]{:S(2)}) collective-permute-start(bf16[64,1152]{1,0:T(8,128)(2,1)S(1)} %get-tuple-element.23), channel_id=1, source_target_pairs={{0,1008},{8,1016},{16,0},{24,8},{32,16},{40,24},{48,32},{56,40},{6... | collective-permute-start | bytes 442376 | tf_op jit(solution)/shard_map/ppermute | solution.py:15
  96.2 45.1 %copy-start.6 = (f32[192,1152]{1,0:T(8,128)S(1)}, f32[192,1152]{1,0:T(8,128)}, u32[]{:S(2)}) copy-start(f32[192,1152]{1,0:T(8,128)} %get-tuple-element.37) | copy-start | bytes 2654212
  130.2 18.6 %all-to-all-start.4 = ((bf16[8,168,128]{2,1,0:T(8,128)(2,1)}), bf16[8,168,128]{2,1,0:T(8,128)(2,1)S(1)}, u32[]{:S(2)}, u32[]{:S(2)}) async-start(bf16[8,168,128]{2,1,0:T(8,128)(2,1)} %broadcast_in_dim.46), calls=%async_computation.4 | async-start | bytes 688128 | tf_op jit(solution)/shard_map/all_to_all | solution.py:34

commit v10 on v3

--- a/solution.py
+++ b/solution.py
@@ -48,8 +48,8 @@
     ).astype(jnp.bfloat16)
     rows = jnp.pad(rows, ((0, count * share - tiles * width), (0, 0)))
     part = summed(swap(rows.reshape(count, share, LANES), "dp", near)).astype(jnp.bfloat16)
-    part, early = lax.optimization_barrier((part, early))
     total = summed(lax.all_gather(part, "dp", axis=0, axis_index_groups=far)).astype(jnp.bfloat16)
+    total, early = lax.optimization_barrier((total, early))
     whole = gathered(total, count, "dp", near).reshape(count * share, LANES)[: tiles * width]
     whole = whole.astype(jnp.float32).reshape(tiles, width, LANES)
     return jnp.swapaxes(whole, 1, 2).reshape(features, width), early
@@ -64,22 +64,24 @@
     scale = logit_scale[0]
     offset = logit_bias[0]
 
-    wide_txt = txt_emb.astype(jnp.float32)
-    inv_txt = lax.rsqrt(jnp.sum(wide_txt * wide_txt, axis=1, keepdims=True) + EPSILON)
-    unit_txt = wide_txt * inv_txt
-    z_txt = unit_txt.astype(jnp.bfloat16)
-    visitors = [z_txt] + [passed_along(z_txt, "dp", k) for k in range(1, STEPS)]
-
+    visitors = [txt_emb] + [passed_along(txt_emb, "dp", k) for k in range(1, STEPS)]
     local_proj = lax.dot_general(
         w_proj, img_feat, (((0,), (1,)), ((), ())), preferred_element_type=jnp.float32
     ).astype(jnp.bfloat16)
-    projected = gathered(local_proj, members, "emb").reshape(features, image_rows)
+    copies = jnp.broadcast_to(local_proj[None], (members,) + local_proj.shape)
+    copies, visitors = lax.optimization_barrier((copies, visitors))
+    projected = swap(copies, "emb").reshape(features, image_rows)
+
+    wide_txt = jnp.concatenate(visitors, axis=0).astype(jnp.float32)
+    inverse_txt = lax.rsqrt(jnp.sum(wide_txt * wide_txt, axis=1, keepdims=True) + EPSILON)
+    texts = (wide_txt * inverse_txt).astype(jnp.bfloat16)
+    inv_txt = inverse_txt[:text_rows]
+    unit_txt = txt_emb.astype(jnp.float32) * inv_txt
     wide_img = projected.astype(jnp.float32)
     inv_img = lax.rsqrt(jnp.sum(wide_img * wide_img, axis=0, keepdims=True) + EPSILON)
     unit_img = wide_img * inv_img
     z_img = unit_img.astype(jnp.bfloat16)
 
-    texts = jnp.concatenate(visitors, axis=0)
     cosines = jnp.dot(texts, z_img, preferred_element_type=jnp.float32)
     text_index = lax.broadcasted_iota(jnp.int32, cosines.shape, 0)
     image_index = lax.broadcasted_iota(jnp.int32, cosines.shape, 1)

time: 140 us -> 143 us (1.021)
  waiting for transfers between devices: 23.9 us -> 37.7 us
  starting transfers between devices: 52.9 us -> 40.7 us
  blocking collectives: 47 us -> 50.2 us
    all_to_all x3, waiting for transfers between devices: 7.79 us -> 20.4 us  [swap(): return lax.all_to_all(parts, axis, 0, 0, axis_index_groups=groups)]
    ppermute x4, starting transfers between devices: 26.2 us -> 18.6 us  [passed_along(): lax.ppermute(array, axis, [(i, (i + by) % count) for i in range(count)])]
    all_to_all x3, starting transfers between devices: 26.7 us -> 22.1 us  [swap(): return lax.all_to_all(parts, axis, 0, 0, axis_index_groups=groups)]
    all_to_all x1, blocking collectives: 16.6 us -> 20 us  [swap(): return lax.all_to_all(parts, axis, 0, 0, axis_index_groups=groups)]
  transfers between devices with their start and end apart: 7 -> 7, of which waited for: 5 -> 4; matrix products, arithmetic and copies ran while one was open for 3% -> 3% of each run, Pallas kernels for 0% -> 0%
where the time goes in v10:
time: 143 us; the launch traced here: 142 us
  blocking collectives  50.2 us (35%)
  starting transfers between devices  40.7 us (28%)
  waiting for transfers between devices  37.7 us (26%)
  matrix products  4.83 us (3%)
  local copies, waits for them, and re-layouts  3.18 us (2%)
  other arithmetic  3.16 us (2%)
  between operations  2.16 us (2%)
    all_gather x1, blocking collectives, sum_over_dp(): lax.all_gather(part, 'dp', axis=0, axis_index_groups=far)  30.3 us
    all_to_all x3, starting transfers between devices, swap(): return lax.all_to_all(parts, axis, 0, 0, axis_index_groups=groups)  22.1 us
    all_to_all x3, waiting for transfers between devices, swap(): return lax.all_to_all(parts, axis, 0, 0, axis_index_groups=groups)  20.4 us
    all_to_all x1, blocking collectives, swap(): return lax.all_to_all(parts, axis, 0, 0, axis_index_groups=groups)  20 us
    ppermute x4, starting transfers between devices, passed_along(): lax.ppermute(array, axis, [(i, (i + by) % count) for i in range(count)])  18.6 us
    ppermute x4, waiting for transfers between devices, passed_along(): lax.ppermute(array, axis, [(i, (i + by) % count) for i in range(count)])  17.4 us
  transfers between devices with their start and end apart: 7, of which 4 were waited for; matrix products, arithmetic and copies ran while one was open for 3% of the time, Pallas kernels for 0%

profile of v10, /device:TPU:1, one launch (start us, length us, event | category | flops | bytes accessed | tf_op | source)
XLA Modules:
  0.0 142.0 jit_solution(9161056609922535060)
XLA Ops:
  0.6 0.0 copy-start
  0.6 5.1 %collective-permute-start = (bf16[64,1152]{1,0:T(8,128)(2,1)}, bf16[64,1152]{1,0:T(8,128)(2,1)S(1)}, u32[]{:S(2)}, u32[]{:S(2)}) collective-permute-start(bf16[64,1152]{1,0:T(8,128)(2,1)} %param.7), channel_id=1, source_target_pairs={{0,8},{8,16},{16,24},{24,32},{32,40},{40,48},{48,56},{56,64},{64,7... | collective-permute-start | bytes 442376 | tf_op jit(solution)/shard_map/ppermute | solution.py:14
  5.7 3.5 %collective-permute-start.1 = (bf16[64,1152]{1,0:T(8,128)(2,1)}, bf16[64,1152]{1,0:T(8,128)(2,1)S(1)}, u32[]{:S(2)}, u32[]{:S(2)}) collective-permute-start(bf16[64,1152]{1,0:T(8,128)(2,1)} %param.7), channel_id=1, source_target_pairs={{0,16},{8,24},{16,32},{24,40},{32,48},{40,56},{48,64},{56,72},{64,... | collective-permute-start | bytes 442376 | tf_op jit(solution)/shard_map/ppermute | solution.py:14
  9.3 1.5 %convolution_convert_fusion.1 = bf16[144,512]{1,0:T(8,128)(2,1)S(1)} fusion(bf16[1152,144]{0,1:T(8,128)(2,1)} %param.6, bf16[512,1152]{1,0:T(8,128)(2,1)S(1)} %copy-done), kind=kOutput, calls=%fused_computation.8 | convolution fusion | flops 169943040 | bytes 1658880 | tf_op jit(solution)/shard_map/dot_general | solution.py:68
  10.8 7.1 %collective-permute-done = bf16[64,1152]{1,0:T(8,128)(2,1)S(1)} collective-permute-done((bf16[64,1152]{1,0:T(8,128)(2,1)}, bf16[64,1152]{1,0:T(8,128)(2,1)S(1)}, u32[]{:S(2)}, u32[]{:S(2)}) %collective-permute-start) | collective-permute-done | bytes 147488 | tf_op jit(solution)/shard_map/ppermute | solution.py:14
  17.9 10.3 %collective-permute-done.1 = bf16[64,1152]{1,0:T(8,128)(2,1)S(1)} collective-permute-done((bf16[64,1152]{1,0:T(8,128)(2,1)}, bf16[64,1152]{1,0:T(8,128)(2,1)S(1)}, u32[]{:S(2)}, u32[]{:S(2)}) %collective-permute-start.1) | collective-permute-done | bytes 147488 | tf_op jit(solution)/shard_map/ppermute | solution.py:14
  28.2 1.1 broadcast_in_dim.12
  29.3 4.4 %all-to-all-start = ((bf16[8,144,512]{2,1,0:T(8,128)(2,1)}), bf16[8,144,512]{2,1,0:T(8,128)(2,1)S(1)}, u32[]{:S(2)}, u32[]{:S(2)}) async-start(bf16[8,144,512]{2,1,0:T(8,128)(2,1)} %broadcast_in_dim.12), calls=%async_computation | async-start | bytes 2359296 | tf_op jit(solution)/shard_map/all_to_all | solution.py:29
  35.0 0.2 fusion.3
  35.1 13.8 %all-to-all-done = bf16[8,144,512]{2,1,0:T(8,128)(2,1)S(1)} async-done(((bf16[8,144,512]{2,1,0:T(8,128)(2,1)}), bf16[8,144,512]{2,1,0:T(8,128)(2,1)S(1)}, u32[]{:S(2)}, u32[]{:S(2)}) %all-to-all-start) | async-done | bytes 1179680 | tf_op jit(solution)/shard_map/all_to_all | solution.py:29
  49.0 0.3 multiply_reduce_fusion
  49.3 0.4 fusion.2
  49.7 0.6 multiply_reduce_fusion.1
  50.3 0.4 copy-done.2
  50.7 0.8 fusion.1
  51.5 20.0 %all_to_all.20 = bf16[8,144,512]{2,1,0:T(8,128)(2,1)S(1)} all-to-all(bf16[8,144,512]{2,1,0:T(8,128)(2,1)S(1)} %bitcast.34), channel_id=1, replica_groups=mesh['dp'=128,'emb'=8] {'emb'}, dimensions={0} | all-to-all | bytes 2359296 | tf_op jit(solution)/shard_map/all_to_all | solution.py:29
  71.4 0.2 reduce_sum.75
  71.6 0.4 convolution_convert_fusion
  72.1 0.8 pad.4
  72.9 5.7 %all-to-all-start.2 = ((bf16[8,168,128]{2,1,0:T(8,128)(2,1)}), bf16[8,168,128]{2,1,0:T(8,128)(2,1)S(1)}, u32[]{:S(2)}, u32[]{:S(2)}) async-start(bf16[8,168,128]{2,1,0:T(8,128)(2,1)} %bitcast.4), calls=%async_computation.2 | async-start | bytes 688128 | tf_op jit(solution)/shard_map/all_to_all | solution.py:29
  78.6 1.6 %fusion.11 = (bf16[192,1152]{1,0:T(8,128)(2,1)S(1)}, f32[192,1152]{1,0:T(8,128)}) fusion(bf16[1152,512]{1,0:T(8,128)(2,1)S(1)} %copy-done.3, f32[192,512]{1,0:T(8,128)S(1)} %get-tuple-element.23, f32[]{:T(128)} %bitcast.29, f32[]{:T(128)} %bitcast.26, s32[192]{0:T(256)S(1)} %iota_add_fusion, pred[192]{0:T(512)(128)(4,1)S(1)} %iota_compare_fusion.1), kind=kOutput, calls=%fused_computation.41 | convolution fusion | flops 228114432 | bytes 2900936 | tf_op jit(solution)/shard_map/dot_general | solution.py:93
  80.2 2.0 %collective-permute-start.2 = (bf16[64,1152]{1,0:T(8,128)(2,1)S(1)}, bf16[64,1152]{1,0:T(8,128)(2,1)S(1)}, u32[]{:S(2)}, u32[]{:S(2)}) collective-permute-start(bf16[64,1152]{1,0:T(8,128)(2,1)S(1)} %get-tuple-element.19), channel_id=1, source_target_pairs={{0,1016},{8,0},{16,8},{24,16},{32,24},{40,32},{48,40},{56,48},{64,... | collective-permute-start | bytes 442376 | tf_op jit(solution)/shard_map/ppermute | solution.py:14
  82.2 7.9 %collective-permute-start.3 = (bf16[64,1152]{1,0:T(8,128)(2,1)S(1)}, bf16[64,1152]{1,0:T(8,128)(2,1)S(1)}, u32[]{:S(2)}, u32[]{:S(2)}) collective-permute-start(bf16[64,1152]{1,0:T(8,128)(2,1)S(1)} %get-tuple-element.18), channel_id=1, source_target_pairs={{0,1008},{8,1016},{16,0},{24,8},{32,16},{40,24},{48,32},{56,40},{6... | collective-permute-start | bytes 442376 | tf_op jit(solution)/shard_map/ppermute | solution.py:14
  90.2 0.1 reduce_sum.76
  90.3 30.3 %all-gather = bf16[2688,128]{1,0:T(8,128)(2,1)S(1)} all-gather(bf16[168,128]{1,0:T(8,128)(2,1)S(1)} %reduce_sum.76), channel_id=2, replica_groups={{0,32,64,96,128,160,192,224,256,288,320,352,384,416,448,480},{8,40,72,1..., dimensions={0}, use_global_device_ids=true | all-gather | bytes 731136 | tf_op jit(solution)/shard_map/all_gather | solution.py:51
  120.5 0.1 reduce_sum.77
  120.6 0.8 broadcast_in_dim.15
  121.4 12.0 %all-to-all-start.3 = ((bf16[8,168,128]{2,1,0:T(8,128)(2,1)}), bf16[8,168,128]{2,1,0:T(8,128)(2,1)S(1)}, u32[]{:S(2)}, u32[]{:S(2)}) async-start(bf16[8,168,128]{2,1,0:T(8,128)(2,1)} %broadcast_in_dim.15), calls=%async_computation.3 | async-start | bytes 688128 | tf_op jit(solution)/shard_map/all_to_all | solution.py:29
  133.5 0.2 multiply_reduce_fusion.2
  133.7 0.8 subtract_multiply_fusion
  134.5 6.5 %all-to-all-done.3 = bf16[8,168,128]{2,1,0:T(8,128)(2,1)S(1)} async-done(((bf16[8,168,128]{2,1,0:T(8,128)(2,1)}), bf16[8,168,128]{2,1,0:T(8,128)(2,1)S(1)}, u32[]{:S(2)}, u32[]{:S(2)}) %all-to-all-start.3) | async-done | bytes 344096 | tf_op jit(solution)/shard_map/all_to_all | solution.py:29
  141.1 0.9 copy_bitcast_fusion
  (27 shorter events, 0.2 us)
Async XLA Ops:
  0.6 8.7 %copy-start = (bf16[512,1152]{1,0:T(8,128)(2,1)S(1)}, bf16[512,1152]{1,0:T(8,128)(2,1)}, u32[]{:S(2)}) copy-start(bf16[512,1152]{1,0:T(8,128)(2,1)} %param.5) | copy-start | bytes 3538948
  0.6 17.3 %collective-permute-start = (bf16[64,1152]{1,0:T(8,128)(2,1)}, bf16[64,1152]{1,0:T(8,128)(2,1)S(1)}, u32[]{:S(2)}, u32[]{:S(2)}) collective-permute-start(bf16[64,1152]{1,0:T(8,128)(2,1)} %param.7), channel_id=1, source_target_pairs={{0,8},{8,16},{16,24},{24,32},{32,40},{40,48},{48,56},{56,64},{64,7... | collective-permute-start | bytes 442376 | tf_op jit(solution)/shard_map/ppermute | solution.py:14
  5.7 22.5 %collective-permute-start.1 = (bf16[64,1152]{1,0:T(8,128)(2,1)}, bf16[64,1152]{1,0:T(8,128)(2,1)S(1)}, u32[]{:S(2)}, u32[]{:S(2)}) collective-permute-start(bf16[64,1152]{1,0:T(8,128)(2,1)} %param.7), channel_id=1, source_target_pairs={{0,16},{8,24},{16,32},{24,40},{32,48},{40,56},{48,64},{56,72},{64,... | collective-permute-start | bytes 442376 | tf_op jit(solution)/shard_map/ppermute | solution.py:14
  29.3 5.7 %copy-start.1 = (bf16[64,1152]{1,0:T(8,128)(2,1)S(1)}, bf16[64,1152]{1,0:T(8,128)(2,1)}, u32[]{:S(2)}) copy-start(bf16[64,1152]{1,0:T(8,128)(2,1)} %param.7) | copy-start | bytes 442372
  29.3 19.7 %all-to-all-start = ((bf16[8,144,512]{2,1,0:T(8,128)(2,1)}), bf16[8,144,512]{2,1,0:T(8,128)(2,1)S(1)}, u32[]{:S(2)}, u32[]{:S(2)}) async-start(bf16[8,144,512]{2,1,0:T(8,128)(2,1)} %broadcast_in_dim.12), calls=%async_computation | async-start | bytes 2359296 | tf_op jit(solution)/shard_map/all_to_all | solution.py:29
  49.7 1.0 copy-start.2
  72.0 6.6 %copy-start.3 = (bf16[1152,512]{1,0:T(8,128)(2,1)S(1)}, bf16[1152,512]{1,0:T(8,128)(2,1)}, u32[]{:S(2)}) copy-start(bf16[1152,512]{1,0:T(8,128)(2,1)} %copy-done.2) | copy-start | bytes 3538948
  72.9 17.3 %all-to-all-start.2 = ((bf16[8,168,128]{2,1,0:T(8,128)(2,1)}), bf16[8,168,128]{2,1,0:T(8,128)(2,1)S(1)}, u32[]{:S(2)}, u32[]{:S(2)}) async-start(bf16[8,168,128]{2,1,0:T(8,128)(2,1)} %bitcast.4), calls=%async_computation.2 | async-start | bytes 688128 | tf_op jit(solution)/shard_map/all_to_all | solution.py:29
  80.2 40.4 %collective-permute-start.2 = (bf16[64,1152]{1,0:T(8,128)(2,1)S(1)}, bf16[64,1152]{1,0:T(8,128)(2,1)S(1)}, u32[]{:S(2)}, u32[]{:S(2)}) collective-permute-start(bf16[64,1152]{1,0:T(8,128)(2,1)S(1)} %get-tuple-element.19), channel_id=1, source_target_pairs={{0,1016},{8,0},{16,8},{24,16},{32,24},{40,32},{48,40},{56,48},{64,... | collective-permute-start | bytes 442376 | tf_op jit(solution)/shard_map/ppermute | solution.py:14
  82.2 38.4 %collective-permute-start.3 = (bf16[64,1152]{1,0:T(8,128)(2,1)S(1)}, bf16[64,1152]{1,0:T(8,128)(2,1)S(1)}, u32[]{:S(2)}, u32[]{:S(2)}) collective-permute-start(bf16[64,1152]{1,0:T(8,128)(2,1)S(1)} %get-tuple-element.18), channel_id=1, source_target_pairs={{0,1008},{8,1016},{16,0},{24,8},{32,16},{40,24},{48,32},{56,40},{6... | collective-permute-start | bytes 442376 | tf_op jit(solution)/shard_map/ppermute | solution.py:14
  90.2 43.2 %copy-start.4 = (f32[192,1152]{1,0:T(8,128)S(1)}, f32[192,1152]{1,0:T(8,128)}, u32[]{:S(2)}) copy-start(f32[192,1152]{1,0:T(8,128)} %get-tuple-element.25) | copy-start | bytes 2654212
  121.4 19.6 %all-to-all-start.3 = ((bf16[8,168,128]{2,1,0:T(8,128)(2,1)}), bf16[8,168,128]{2,1,0:T(8,128)(2,1)S(1)}, u32[]{:S(2)}, u32[]{:S(2)}) async-start(bf16[8,168,128]{2,1,0:T(8,128)(2,1)} %broadcast_in_dim.15), calls=%async_computation.3 | async-start | bytes 688128 | tf_op jit(solution)/shard_map/all_to_all | solution.py:29

commit v11 on v7

--- a/solution.py
+++ b/solution.py
@@ -96,7 +96,7 @@
         w_proj, img_feat, (((0,), (1,)), ((), ())), preferred_element_type=jnp.float32
     ).astype(jnp.bfloat16)
     copies = jnp.broadcast_to(local_proj[None], (members,) + local_proj.shape)
-    copies, partner_txt = lax.optimization_barrier((copies, partner_txt))
+    copies, txt_emb, partner_txt = lax.optimization_barrier((copies, txt_emb, partner_txt))
     unit_txt, inv_txt = unit_rows(txt_emb)
     pair_txt = jnp.concatenate([unit_txt, unit_rows(partner_txt)[0]], axis=0).astype(jnp.bfloat16)
     visitors = [pair_txt] + [passed_along(pair_txt, "dp", k) for k in range(1, STEPS)]
@@ -112,7 +112,8 @@
         other = (text >= text_rows) & (text < PAIR * text_rows)
         return own | (other & (row == (member ^ 1) * text_rows + text - text_rows))
 
-    cosines, pair_grad = slopes(texts, unit_img.astype(jnp.bfloat16), pair_matches)
+    z_img = unit_img.astype(jnp.bfloat16)
+    cosines, pair_grad = slopes(texts, z_img, pair_matches)
     inner_img = jnp.sum(pair_grad.astype(jnp.float32) * cosines, axis=0, keepdims=True)
     grad_img = lax.dot_general(
         texts, pair_grad, (((0,), (0,)), ((), ())), preferred_element_type=jnp.float32
@@ -124,16 +125,21 @@
     grad_part = jnp.concatenate([grad_part[h] for h in range(PAIR)], axis=1)
     local_weight = jnp.dot(grad_part, img_feat, preferred_element_type=jnp.float32)
 
-    own_texts = jnp.concatenate([visitor[:text_rows] for visitor in visitors], axis=0)
-    z_img = unit_columns(projected)[0].astype(jnp.bfloat16)
-    own_grad = slopes(
-        own_texts,
-        z_img,
-        lambda text, image: (text < text_rows) & (image == member * text_rows + text),
+    own_rows = lambda array: jnp.concatenate(
+        [array[k * PAIR * text_rows :][:text_rows] for k in range(STEPS)], axis=0
+    )
+    over_images = lambda grads, images: lax.dot_general(
+        grads, images, (((1,), (1,)), ((), ())), preferred_element_type=jnp.float32
+    )
+    other_row = half_rows - first_row
+    other = lax.dynamic_slice_in_dim(projected, other_row, half_rows, 1)
+    z_other = unit_columns(other)[0].astype(jnp.bfloat16)
+    other_grad = slopes(
+        own_rows(texts),
+        z_other,
+        lambda text, image: (text < text_rows) & (image + other_row == member * text_rows + text),
     )[1]
-    txt_terms = scale * lax.dot_general(
-        own_grad, z_img, (((1,), (1,)), ((), ())), preferred_element_type=jnp.float32
-    )
+    txt_terms = scale * (over_images(own_rows(pair_grad), z_img) + over_images(other_grad, z_other))
     sent = [
         passed_along(txt_terms[k * text_rows : (k + 1) * text_rows].astype(jnp.bfloat16), "dp", -k)
         for k in range(1, STEPS)

time: 134 us -> 136 us (1.015)
  starting transfers between devices: 49.9 us -> 51.3 us
    all_to_all x3, starting transfers between devices: 26.7 us -> 29.7 us  [swap(): return lax.all_to_all(parts, axis, 0, 0, axis_index_groups=groups)]
    ppermute x4, starting transfers between devices: 19.1 us -> 17.5 us  [passed_along(): lax.ppermute(array, axis, [(i, (i + by) % count) for i in range(count)])]
    slice x4 -> x2, local copies, waits for them, and re-layouts: 0.01 us -> 1.55 us  [local(): array[k * PAIR * text_rows:][:text_rows]]
    dot_general x1 -> x2, matrix products: 2.05 us -> 3.21 us  [local(): lax.dot_general(grads, images, (((1,), (1,)), ((), ())), preferred_elemen...]
  transfers between devices with their start and end apart: 8 -> 8, of which waited for: 2 -> 2; matrix products, arithmetic and copies ran while one was open for 6% -> 9% of each run, Pallas kernels for 0% -> 0%
where the time goes in v11:
time: 136 us; the launch traced here: 135 us
  starting transfers between devices  51.3 us (38%)
  blocking collectives  41.2 us (30%)
  waiting for transfers between devices  23.4 us (17%)
  matrix products  6.19 us (5%)
  other arithmetic  5.62 us (4%)
  local copies, waits for them, and re-layouts  5.53 us (4%)
  between operations  2.24 us (2%)
    all_to_all x3, starting transfers between devices, swap(): return lax.all_to_all(parts, axis, 0, 0, axis_index_groups=groups)  29.7 us
    all_gather x1, blocking collectives, sum_over_dp(): lax.all_gather(part, 'dp', axis=0, axis_index_groups=far)  29.1 us
    ppermute x4, starting transfers between devices, passed_along(): lax.ppermute(array, axis, [(i, (i + by) % count) for i in range(count)])  17.5 us
    ppermute x4, waiting for transfers between devices, passed_along(): lax.ppermute(array, axis, [(i, (i + by) % count) for i in range(count)])  16.9 us
    all_to_all x1, blocking collectives, swap(): return lax.all_to_all(parts, axis, 0, 0, axis_index_groups=groups)  12 us
    all_to_all x3, waiting for transfers between devices, swap(): return lax.all_to_all(parts, axis, 0, 0, axis_index_groups=groups)  6.51 us
    ppermute x1, starting transfers between devices, to_partner(): lax.ppermute(array, 'emb', [(i, i ^ 1) for i in range(lax.axis_size('emb'...  4.08 us
    dot_general x2, matrix products, local(): lax.dot_general(grads, images, (((1,), (1,)), ((), ())), preferred_elemen...  3.21 us
  transfers between devices with their start and end apart: 8, of which 2 were waited for; matrix products, arithmetic and copies ran while one was open for 9% of the time, Pallas kernels for 0%

profile of v11, /device:TPU:1, one launch (start us, length us, event | category | flops | bytes accessed | tf_op | source)
XLA Modules:
  0.0 135.5 jit_solution(1523093836154401970)
XLA Ops:
  0.6 4.1 %collective-permute-start = (bf16[64,1152]{1,0:T(8,128)(2,1)}, bf16[64,1152]{1,0:T(8,128)(2,1)S(1)}, u32[]{:S(2)}, u32[]{:S(2)}) collective-permute-start(bf16[64,1152]{1,0:T(8,128)(2,1)} %param.7), channel_id=1, source_target_pairs={{0,1},{1,0},{2,3},{3,2},{4,5},{5,4},{6,7},{7,6},{8,9},{9,8},{10,11... | collective-permute-start | bytes 442376 | tf_op jit(solution)/shard_map/ppermute | solution.py:19
  6.1 1.5 %convolution_convert_fusion.1 = bf16[144,512]{1,0:T(8,128)(2,1)S(1)} fusion(bf16[1152,144]{0,1:T(8,128)(2,1)} %param.6, bf16[512,1152]{1,0:T(8,128)(2,1)S(1)} %copy-done), kind=kOutput, calls=%fused_computation.15 | convolution fusion | flops 169943040 | bytes 1658880 | tf_op jit(solution)/shard_map/dot_general | solution.py:95
  7.6 1.1 broadcast_in_dim.20
  8.9 5.9 %all-to-all-start = ((bf16[8,144,512]{2,1,0:T(8,128)(2,1)}), bf16[8,144,512]{2,1,0:T(8,128)(2,1)S(1)}, u32[]{:S(2)}, u32[]{:S(2)}) async-start(bf16[8,144,512]{2,1,0:T(8,128)(2,1)} %broadcast_in_dim.20), calls=%async_computation | async-start | bytes 2359296 | tf_op jit(solution)/shard_map/all_to_all | solution.py:34
  15.1 3.5 %collective-permute-start.2 = (bf16[128,1152]{1,0:T(8,128)(2,1)S(1)}, bf16[128,1152]{1,0:T(8,128)(2,1)S(1)}, u32[]{:S(2)}, u32[]{:S(2)}) collective-permute-start(bf16[128,1152]{1,0:T(8,128)(2,1)S(1)} %pad_maximum_fusion.1), channel_id=1, source_target_pairs={{0,16},{8,24},{16,32},{24,40},{32,48},{40,56},{48,64},{56,72},{64,... | collective-permute-start | bytes 884744 | tf_op jit(solution)/shard_map/ppermute | solution.py:15
  18.7 5.5 %collective-permute-start.1 = (bf16[128,1152]{1,0:T(8,128)(2,1)S(1)}, bf16[128,1152]{1,0:T(8,128)(2,1)S(1)}, u32[]{:S(2)}, u32[]{:S(2)}) collective-permute-start(bf16[128,1152]{1,0:T(8,128)(2,1)S(1)} %pad_maximum_fusion.1), channel_id=1, source_target_pairs={{0,8},{8,16},{16,24},{24,32},{32,40},{40,48},{48,56},{56,64},{64,7... | collective-permute-start | bytes 884744 | tf_op jit(solution)/shard_map/ppermute | solution.py:15
  24.2 16.9 %collective-permute-done.2 = bf16[128,1152]{1,0:T(8,128)(2,1)S(1)} collective-permute-done((bf16[128,1152]{1,0:T(8,128)(2,1)S(1)}, bf16[128,1152]{1,0:T(8,128)(2,1)S(1)}, u32[]{:S(2)}, u32[]{:S(2)}) %collective-permute-start.2) | collective-permute-done | bytes 294944 | tf_op jit(solution)/shard_map/ppermute | solution.py:15
  41.2 0.3 fusion.6
  41.5 0.6 multiply_reduce_fusion
  42.2 0.5 fusion.2
  42.8 12.0 %all_to_all.20 = bf16[8,144,256]{2,1,0:T(8,128)(2,1)S(1)} all-to-all(bf16[8,144,256]{2,1,0:T(8,128)(2,1)S(1)} %bitcast.41), channel_id=1, replica_groups=mesh['dp'=128,'emb'=8] {'emb'}, dimensions={0} | all-to-all | bytes 1179648 | tf_op jit(solution)/shard_map/all_to_all | solution.py:34
  54.9 0.4 convolution_convert_fusion
  55.5 0.8 pad.4
  56.2 12.5 %all-to-all-start.2 = ((bf16[8,168,128]{2,1,0:T(8,128)(2,1)}), bf16[8,168,128]{2,1,0:T(8,128)(2,1)}, u32[]{:S(2)}, u32[]{:S(2)}) async-start(bf16[8,168,128]{2,1,0:T(8,128)(2,1)} %bitcast.38), calls=%async_computation.2 | async-start | bytes 688128 | tf_op jit(solution)/shard_map/all_to_all | solution.py:34
  68.8 0.5 iota_compare_fusion.3
  69.3 0.6 iota_add_fusion.2
  69.9 0.6 iota_add_fusion.1
  70.5 0.7 fusion.78
  71.2 0.8 fusion.80
  72.0 0.4 fusion.22
  72.4 2.8 %fusion.81 = (bf16[192,1152]{1,0:T(8,128)(2,1)}, f32[192,1152]{1,0:T(8,128)}) fusion(f32[192,1152]{1,0:T(8,128)S(1)} %fusion.22, f32[256]{0:T(256)S(1)} %add_rsqrt_fusion, bf16[1152,512]{1,0:T(8,128)(2,1)S(1)} %bitcast.35, s32[]{:T(128)S(6)} %select_n.25, bf16[64,1152]{1,0:T(8,128)(2,1)} %get-tuple-element.19, bf16[64,1152]{1,0:T(8,128)(2,1)} %get-tuple-element.20, ...), kind=kOutput, calls=%fused_computation.113 | convolution fusion | flops 230842368 | bytes 3841024 | tf_op jit(solution)/shard_map/dot_general | solution.py:131
  75.2 1.0 fusion.79
  76.2 5.9 %collective-permute-start.4 = (bf16[64,1152]{1,0:T(8,128)(2,1)S(1)}, bf16[64,1152]{1,0:T(8,128)(2,1)S(1)}, u32[]{:S(2)}, u32[]{:S(2)}) collective-permute-start(bf16[64,1152]{1,0:T(8,128)(2,1)S(1)} %get-tuple-element.21), channel_id=1, source_target_pairs={{0,1008},{8,1016},{16,0},{24,8},{32,16},{40,24},{48,32},{56,40},{6... | collective-permute-start | bytes 442376 | tf_op jit(solution)/shard_map/ppermute | solution.py:15
  82.1 2.5 %collective-permute-start.3 = (bf16[64,1152]{1,0:T(8,128)(2,1)S(1)}, bf16[64,1152]{1,0:T(8,128)(2,1)S(1)}, u32[]{:S(2)}, u32[]{:S(2)}) collective-permute-start(bf16[64,1152]{1,0:T(8,128)(2,1)S(1)} %get-tuple-element.22), channel_id=1, source_target_pairs={{0,1016},{8,0},{16,8},{24,16},{32,24},{40,32},{48,40},{56,48},{64,... | collective-permute-start | bytes 442376 | tf_op jit(solution)/shard_map/ppermute | solution.py:15
  84.7 1.0 reduce_sum.95
  85.7 29.1 %all-gather = bf16[2688,128]{1,0:T(8,128)(2,1)S(1)} all-gather(bf16[168,128]{1,0:T(8,128)(2,1)S(1)} %reduce_sum.95), channel_id=2, replica_groups={{0,32,64,96,128,160,192,224,256,288,320,352,384,416,448,480},{8,40,72,1..., dimensions={0}, use_global_device_ids=true | all-gather | bytes 731136 | tf_op jit(solution)/shard_map/all_gather | solution.py:56
  115.0 0.8 broadcast_in_dim.39
  115.8 11.2 %all-to-all-start.3 = ((bf16[8,168,128]{2,1,0:T(8,128)(2,1)}), bf16[8,168,128]{2,1,0:T(8,128)(2,1)S(1)}, u32[]{:S(2)}, u32[]{:S(2)}) async-start(bf16[8,168,128]{2,1,0:T(8,128)(2,1)} %broadcast_in_dim.39), calls=%async_computation.3 | async-start | bytes 688128 | tf_op jit(solution)/shard_map/all_to_all | solution.py:34
  127.0 0.2 fusion.41
  127.2 0.8 fusion.43
  128.1 6.5 %all-to-all-done.3 = bf16[8,168,128]{2,1,0:T(8,128)(2,1)S(1)} async-done(((bf16[8,168,128]{2,1,0:T(8,128)(2,1)}), bf16[8,168,128]{2,1,0:T(8,128)(2,1)S(1)}, u32[]{:S(2)}, u32[]{:S(2)}) %all-to-all-start.3) | async-done | bytes 344096 | tf_op jit(solution)/shard_map/all_to_all | solution.py:34
  134.6 0.9 copy_bitcast_fusion
  (45 shorter events, 1.0 us)
Async XLA Ops:
  0.6 5.4 %copy-start = (bf16[512,1152]{1,0:T(8,128)(2,1)S(1)}, bf16[512,1152]{1,0:T(8,128)(2,1)}, u32[]{:S(2)}) copy-start(bf16[512,1152]{1,0:T(8,128)(2,1)} %param.5) | copy-start | bytes 3538948
  0.6 7.0 %collective-permute-start = (bf16[64,1152]{1,0:T(8,128)(2,1)}, bf16[64,1152]{1,0:T(8,128)(2,1)S(1)}, u32[]{:S(2)}, u32[]{:S(2)}) collective-permute-start(bf16[64,1152]{1,0:T(8,128)(2,1)} %param.7), channel_id=1, source_target_pairs={{0,1},{1,0},{2,3},{3,2},{4,5},{5,4},{6,7},{7,6},{8,9},{9,8},{10,11... | collective-permute-start | bytes 442376 | tf_op jit(solution)/shard_map/ppermute | solution.py:19
  6.1 2.7 %copy-start.1 = (bf16[64,1152]{1,0:T(8,128)(2,1)S(1)}, bf16[64,1152]{1,0:T(8,128)(2,1)}, u32[]{:S(2)}) copy-start(bf16[64,1152]{1,0:T(8,128)(2,1)} %param.7) | copy-start | bytes 442372
  8.9 32.4 %all-to-all-start = ((bf16[8,144,512]{2,1,0:T(8,128)(2,1)}), bf16[8,144,512]{2,1,0:T(8,128)(2,1)S(1)}, u32[]{:S(2)}, u32[]{:S(2)}) async-start(bf16[8,144,512]{2,1,0:T(8,128)(2,1)} %broadcast_in_dim.20), calls=%async_computation | async-start | bytes 2359296 | tf_op jit(solution)/shard_map/all_to_all | solution.py:34
  15.1 26.1 %collective-permute-start.2 = (bf16[128,1152]{1,0:T(8,128)(2,1)S(1)}, bf16[128,1152]{1,0:T(8,128)(2,1)S(1)}, u32[]{:S(2)}, u32[]{:S(2)}) collective-permute-start(bf16[128,1152]{1,0:T(8,128)(2,1)S(1)} %pad_maximum_fusion.1), channel_id=1, source_target_pairs={{0,16},{8,24},{16,32},{24,40},{32,48},{40,56},{48,64},{56,72},{64,... | collective-permute-start | bytes 884744 | tf_op jit(solution)/shard_map/ppermute | solution.py:15
  18.7 22.5 %collective-permute-start.1 = (bf16[128,1152]{1,0:T(8,128)(2,1)S(1)}, bf16[128,1152]{1,0:T(8,128)(2,1)S(1)}, u32[]{:S(2)}, u32[]{:S(2)}) collective-permute-start(bf16[128,1152]{1,0:T(8,128)(2,1)S(1)} %pad_maximum_fusion.1), channel_id=1, source_target_pairs={{0,8},{8,16},{16,24},{24,32},{32,40},{40,48},{48,56},{56,64},{64,7... | collective-permute-start | bytes 884744 | tf_op jit(solution)/shard_map/ppermute | solution.py:15
  41.2 0.9 copy-start.2
  42.1 0.7 copy-start.5
  55.3 15.1 %copy-start.3 = (bf16[384,1152]{1,0:T(8,128)(2,1)S(1)}, bf16[384,1152]{1,0:T(8,128)(2,1)}, u32[]{:S(2)}) copy-start(bf16[384,1152]{1,0:T(8,128)(2,1)} %copy-done.2) | copy-start | bytes 2654212
  56.2 28.5 %all-to-all-start.2 = ((bf16[8,168,128]{2,1,0:T(8,128)(2,1)}), bf16[8,168,128]{2,1,0:T(8,128)(2,1)}, u32[]{:S(2)}, u32[]{:S(2)}) async-start(bf16[8,168,128]{2,1,0:T(8,128)(2,1)} %bitcast.38), calls=%async_computation.2 | async-start | bytes 688128 | tf_op jit(solution)/shard_map/all_to_all | solution.py:34
  71.2 1.2 copy-start.6
  76.2 38.7 %collective-permute-start.4 = (bf16[64,1152]{1,0:T(8,128)(2,1)S(1)}, bf16[64,1152]{1,0:T(8,128)(2,1)S(1)}, u32[]{:S(2)}, u32[]{:S(2)}) collective-permute-start(bf16[64,1152]{1,0:T(8,128)(2,1)S(1)} %get-tuple-element.21), channel_id=1, source_target_pairs={{0,1008},{8,1016},{16,0},{24,8},{32,16},{40,24},{48,32},{56,40},{6... | collective-permute-start | bytes 442376 | tf_op jit(solution)/shard_map/ppermute | solution.py:15
  82.1 32.8 %collective-permute-start.3 = (bf16[64,1152]{1,0:T(8,128)(2,1)S(1)}, bf16[64,1152]{1,0:T(8,128)(2,1)S(1)}, u32[]{:S(2)}, u32[]{:S(2)}) collective-permute-start(bf16[64,1152]{1,0:T(8,128)(2,1)S(1)} %get-tuple-element.22), channel_id=1, source_target_pairs={{0,1016},{8,0},{16,8},{24,16},{32,24},{40,32},{48,40},{56,48},{64,... | collective-permute-start | bytes 442376 | tf_op jit(solution)/shard_map/ppermute | solution.py:15
  85.7 41.3 %copy-start.4 = (f32[192,1152]{1,0:T(8,128)S(1)}, f32[192,1152]{1,0:T(8,128)}, u32[]{:S(2)}) copy-start(f32[192,1152]{1,0:T(8,128)} %get-tuple-element.31) | copy-start | bytes 2654212
  115.8 18.8 %all-to-all-start.3 = ((bf16[8,168,128]{2,1,0:T(8,128)(2,1)}), bf16[8,168,128]{2,1,0:T(8,128)(2,1)S(1)}, u32[]{:S(2)}, u32[]{:S(2)}) async-start(bf16[8,168,128]{2,1,0:T(8,128)(2,1)} %broadcast_in_dim.39), calls=%async_computation.3 | async-start | bytes 688128 | tf_op jit(solution)/shard_map/all_to_all | solution.py:34

commit v12 on v7

--- a/solution.py
+++ b/solution.py
@@ -96,7 +96,7 @@
         w_proj, img_feat, (((0,), (1,)), ((), ())), preferred_element_type=jnp.float32
     ).astype(jnp.bfloat16)
     copies = jnp.broadcast_to(local_proj[None], (members,) + local_proj.shape)
-    copies, partner_txt = lax.optimization_barrier((copies, partner_txt))
+    copies, txt_emb, partner_txt = lax.optimization_barrier((copies, txt_emb, partner_txt))
     unit_txt, inv_txt = unit_rows(txt_emb)
     pair_txt = jnp.concatenate([unit_txt, unit_rows(partner_txt)[0]], axis=0).astype(jnp.bfloat16)
     visitors = [pair_txt] + [passed_along(pair_txt, "dp", k) for k in range(1, STEPS)]

time: 134 us -> 133 us (level)
  waiting for transfers between devices: 24.6 us -> 22.9 us
    all_to_all x3, starting transfers between devices: 26.7 us -> 28.6 us  [swap(): return lax.all_to_all(parts, axis, 0, 0, axis_index_groups=groups)]
    ppermute x4, waiting for transfers between devices: 18.1 us -> 16.3 us  [passed_along(): lax.ppermute(array, axis, [(i, (i + by) % count) for i in range(count)])]
  transfers between devices with their start and end apart: 8 -> 8, of which waited for: 2 -> 2; matrix products, arithmetic and copies ran while one was open for 6% -> 5% of each run, Pallas kernels for 0% -> 0%
where the time goes in v12:
time: 133 us; the launch traced here: 132 us
  starting transfers between devices  50.8 us (38%)
  blocking collectives  41.1 us (31%)
  waiting for transfers between devices  22.9 us (17%)
  matrix products  6.02 us (5%)
  local copies, waits for them, and re-layouts  5.25 us (4%)
  other arithmetic  3.78 us (3%)
  between operations  2.23 us (2%)
    all_gather x1, blocking collectives, sum_over_dp(): lax.all_gather(part, 'dp', axis=0, axis_index_groups=far)  29 us
    all_to_all x3, starting transfers between devices, swap(): return lax.all_to_all(parts, axis, 0, 0, axis_index_groups=groups)  28.6 us
    ppermute x4, starting transfers between devices, passed_along(): lax.ppermute(array, axis, [(i, (i + by) % count) for i in range(count)])  18.1 us
    ppermute x4, waiting for transfers between devices, passed_along(): lax.ppermute(array, axis, [(i, (i + by) % count) for i in range(count)])  16.3 us
    all_to_all x1, blocking collectives, swap(): return lax.all_to_all(parts, axis, 0, 0, axis_index_groups=groups)  12.1 us
    all_to_all x3, waiting for transfers between devices, swap(): return lax.all_to_all(parts, axis, 0, 0, axis_index_groups=groups)  6.54 us
    ppermute x1, starting transfers between devices, to_partner(): lax.ppermute(array, 'emb', [(i, i ^ 1) for i in range(lax.axis_size('emb'...  4.08 us
  transfers between devices with their start and end apart: 8, of which 2 were waited for; matrix products, arithmetic and copies ran while one was open for 5% of the time, Pallas kernels for 0%

profile of v12, /device:TPU:1, one launch (start us, length us, event | category | flops | bytes accessed | tf_op | source)
XLA Modules:
  0.0 132.1 jit_solution(6881558872497730061)
XLA Ops:
  0.6 4.1 %collective-permute-start = (bf16[64,1152]{1,0:T(8,128)(2,1)}, bf16[64,1152]{1,0:T(8,128)(2,1)S(1)}, u32[]{:S(2)}, u32[]{:S(2)}) collective-permute-start(bf16[64,1152]{1,0:T(8,128)(2,1)} %param.7), channel_id=1, source_target_pairs={{0,1},{1,0},{2,3},{3,2},{4,5},{5,4},{6,7},{7,6},{8,9},{9,8},{10,11... | collective-permute-start | bytes 442376 | tf_op jit(solution)/shard_map/ppermute | solution.py:19
  6.1 1.5 %convolution_convert_fusion.1 = bf16[144,512]{1,0:T(8,128)(2,1)S(1)} fusion(bf16[1152,144]{0,1:T(8,128)(2,1)} %param.6, bf16[512,1152]{1,0:T(8,128)(2,1)S(1)} %copy-done), kind=kOutput, calls=%fused_computation.21 | convolution fusion | flops 169943040 | bytes 1658880 | tf_op jit(solution)/shard_map/dot_general | solution.py:95
  7.6 1.1 broadcast_in_dim.20
  8.7 0.1 fusion.37
  8.9 5.9 %all-to-all-start = ((bf16[8,144,512]{2,1,0:T(8,128)(2,1)}), bf16[8,144,512]{2,1,0:T(8,128)(2,1)S(1)}, u32[]{:S(2)}, u32[]{:S(2)}) async-start(bf16[8,144,512]{2,1,0:T(8,128)(2,1)} %broadcast_in_dim.20), calls=%async_computation | async-start | bytes 2359296 | tf_op jit(solution)/shard_map/all_to_all | solution.py:34
  14.8 0.1 fusion.33
  15.1 3.5 %collective-permute-start.2 = (bf16[128,1152]{1,0:T(8,128)(2,1)S(1)}, bf16[128,1152]{1,0:T(8,128)(2,1)S(1)}, u32[]{:S(2)}, u32[]{:S(2)}) collective-permute-start(bf16[128,1152]{1,0:T(8,128)(2,1)S(1)} %pad_maximum_fusion.1), channel_id=1, source_target_pairs={{0,16},{8,24},{16,32},{24,40},{32,48},{40,56},{48,64},{56,72},{64,... | collective-permute-start | bytes 884744 | tf_op jit(solution)/shard_map/ppermute | solution.py:15
  18.6 5.5 %collective-permute-start.1 = (bf16[128,1152]{1,0:T(8,128)(2,1)S(1)}, bf16[128,1152]{1,0:T(8,128)(2,1)S(1)}, u32[]{:S(2)}, u32[]{:S(2)}) collective-permute-start(bf16[128,1152]{1,0:T(8,128)(2,1)S(1)} %pad_maximum_fusion.1), channel_id=1, source_target_pairs={{0,8},{8,16},{16,24},{24,32},{32,40},{40,48},{48,56},{56,64},{64,7... | collective-permute-start | bytes 884744 | tf_op jit(solution)/shard_map/ppermute | solution.py:15
  24.2 0.6 iota_compare_fusion.3
  24.8 16.3 %collective-permute-done.2 = bf16[128,1152]{1,0:T(8,128)(2,1)S(1)} collective-permute-done((bf16[128,1152]{1,0:T(8,128)(2,1)S(1)}, bf16[128,1152]{1,0:T(8,128)(2,1)S(1)}, u32[]{:S(2)}, u32[]{:S(2)}) %collective-permute-start.2) | collective-permute-done | bytes 294944 | tf_op jit(solution)/shard_map/ppermute | solution.py:15
  41.1 0.7 copy-done.2
  41.9 0.7 copy-done.3
  42.7 0.2 fusion.11
  42.9 1.3 multiply_reduce_fusion.1
  44.2 0.8 fusion.1
  45.0 12.1 %all_to_all.20 = bf16[8,144,256]{2,1,0:T(8,128)(2,1)S(1)} all-to-all(bf16[8,144,256]{2,1,0:T(8,128)(2,1)S(1)} %bitcast.40), channel_id=1, replica_groups=mesh['dp'=128,'emb'=8] {'emb'}, dimensions={0} | all-to-all | bytes 1179648 | tf_op jit(solution)/shard_map/all_to_all | solution.py:34
  57.2 0.4 convolution_convert_fusion
  57.7 0.8 pad.4
  58.4 10.7 %all-to-all-start.2 = ((bf16[8,168,128]{2,1,0:T(8,128)(2,1)}), bf16[8,168,128]{2,1,0:T(8,128)(2,1)S(1)}, u32[]{:S(2)}, u32[]{:S(2)}) async-start(bf16[8,168,128]{2,1,0:T(8,128)(2,1)} %bitcast.7), calls=%async_computation.2 | async-start | bytes 688128 | tf_op jit(solution)/shard_map/all_to_all | solution.py:34
  69.1 0.3 multiply_reduce_fusion
  69.4 2.0 %fusion.58 = (bf16[192,1152]{1,0:T(8,128)(2,1)}, f32[192,1152]{1,0:T(8,128)}) fusion(bf16[1152,512]{1,0:T(8,128)(2,1)S(1)} %bitcast.35, f32[512]{0:T(512)S(1)} %add_rsqrt_fusion, bf16[64,1152]{1,0:T(8,128)(2,1)S(1)} %slice-done, bf16[64,1152]{1,0:T(8,128)(2,1)S(1)} %slice-done.1, bf16[64,1152]{1,0:T(8,128)(2,1)S(1)} %get-tuple-element.24, f32[]{:T(128)} %bitcast.30, ...), kind=kOutput, calls=%fused_computation.95 | convolution fusion | flops 459472896 | bytes 2952136 | tf_op jit(solution)/shard_map/dot_general | solution.py:134
  71.5 1.0 fusion.57
  72.5 6.5 %collective-permute-start.4 = (bf16[64,1152]{1,0:T(8,128)(2,1)S(1)}, bf16[64,1152]{1,0:T(8,128)(2,1)S(1)}, u32[]{:S(2)}, u32[]{:S(2)}) collective-permute-start(bf16[64,1152]{1,0:T(8,128)(2,1)S(1)} %get-tuple-element.14), channel_id=1, source_target_pairs={{0,1008},{8,1016},{16,0},{24,8},{32,16},{40,24},{48,32},{56,40},{6... | collective-permute-start | bytes 442376 | tf_op jit(solution)/shard_map/ppermute | solution.py:15
  79.0 2.5 %collective-permute-start.3 = (bf16[64,1152]{1,0:T(8,128)(2,1)S(1)}, bf16[64,1152]{1,0:T(8,128)(2,1)S(1)}, u32[]{:S(2)}, u32[]{:S(2)}) collective-permute-start(bf16[64,1152]{1,0:T(8,128)(2,1)S(1)} %get-tuple-element.15), channel_id=1, source_target_pairs={{0,1016},{8,0},{16,8},{24,16},{32,24},{40,32},{48,40},{56,48},{64,... | collective-permute-start | bytes 442376 | tf_op jit(solution)/shard_map/ppermute | solution.py:15
  81.6 29.0 %all-gather = bf16[2688,128]{1,0:T(8,128)(2,1)S(1)} all-gather(bf16[168,128]{1,0:T(8,128)(2,1)S(1)} %reduce_sum.95), channel_id=2, replica_groups={{0,32,64,96,128,160,192,224,256,288,320,352,384,416,448,480},{8,40,72,1..., dimensions={0}, use_global_device_ids=true | all-gather | bytes 731136 | tf_op jit(solution)/shard_map/all_gather | solution.py:56
  110.6 0.1 reduce_sum.96
  110.7 0.8 broadcast_in_dim.39
  111.5 12.0 %all-to-all-start.3 = ((bf16[8,168,128]{2,1,0:T(8,128)(2,1)}), bf16[8,168,128]{2,1,0:T(8,128)(2,1)S(1)}, u32[]{:S(2)}, u32[]{:S(2)}) async-start(bf16[8,168,128]{2,1,0:T(8,128)(2,1)} %broadcast_in_dim.39), calls=%async_computation.3 | async-start | bytes 688128 | tf_op jit(solution)/shard_map/all_to_all | solution.py:34
  123.6 0.2 fusion.34
  123.8 0.8 fusion.36
  124.6 6.5 %all-to-all-done.3 = bf16[8,168,128]{2,1,0:T(8,128)(2,1)S(1)} async-done(((bf16[8,168,128]{2,1,0:T(8,128)(2,1)}), bf16[8,168,128]{2,1,0:T(8,128)(2,1)S(1)}, u32[]{:S(2)}, u32[]{:S(2)}) %all-to-all-start.3) | async-done | bytes 344096 | tf_op jit(solution)/shard_map/all_to_all | solution.py:34
  131.2 0.9 copy_bitcast_fusion
  (46 shorter events, 0.6 us)
Async XLA Ops:
  0.6 5.4 %copy-start = (bf16[512,1152]{1,0:T(8,128)(2,1)S(1)}, bf16[512,1152]{1,0:T(8,128)(2,1)}, u32[]{:S(2)}) copy-start(bf16[512,1152]{1,0:T(8,128)(2,1)} %param.5) | copy-start | bytes 3538948
  0.6 7.0 %collective-permute-start = (bf16[64,1152]{1,0:T(8,128)(2,1)}, bf16[64,1152]{1,0:T(8,128)(2,1)S(1)}, u32[]{:S(2)}, u32[]{:S(2)}) collective-permute-start(bf16[64,1152]{1,0:T(8,128)(2,1)} %param.7), channel_id=1, source_target_pairs={{0,1},{1,0},{2,3},{3,2},{4,5},{5,4},{6,7},{7,6},{8,9},{9,8},{10,11... | collective-permute-start | bytes 442376 | tf_op jit(solution)/shard_map/ppermute | solution.py:19
  6.1 2.7 %copy-start.1 = (bf16[64,1152]{1,0:T(8,128)(2,1)S(1)}, bf16[64,1152]{1,0:T(8,128)(2,1)}, u32[]{:S(2)}) copy-start(bf16[64,1152]{1,0:T(8,128)(2,1)} %param.7) | copy-start | bytes 442372
  8.9 33.8 %all-to-all-start = ((bf16[8,144,512]{2,1,0:T(8,128)(2,1)}), bf16[8,144,512]{2,1,0:T(8,128)(2,1)S(1)}, u32[]{:S(2)}, u32[]{:S(2)}) async-start(bf16[8,144,512]{2,1,0:T(8,128)(2,1)} %broadcast_in_dim.20), calls=%async_computation | async-start | bytes 2359296 | tf_op jit(solution)/shard_map/all_to_all | solution.py:34
  15.1 26.1 %collective-permute-start.2 = (bf16[128,1152]{1,0:T(8,128)(2,1)S(1)}, bf16[128,1152]{1,0:T(8,128)(2,1)S(1)}, u32[]{:S(2)}, u32[]{:S(2)}) collective-permute-start(bf16[128,1152]{1,0:T(8,128)(2,1)S(1)} %pad_maximum_fusion.1), channel_id=1, source_target_pairs={{0,16},{8,24},{16,32},{24,40},{32,48},{40,56},{48,64},{56,72},{64,... | collective-permute-start | bytes 884744 | tf_op jit(solution)/shard_map/ppermute | solution.py:15
  18.6 22.5 %collective-permute-start.1 = (bf16[128,1152]{1,0:T(8,128)(2,1)S(1)}, bf16[128,1152]{1,0:T(8,128)(2,1)S(1)}, u32[]{:S(2)}, u32[]{:S(2)}) collective-permute-start(bf16[128,1152]{1,0:T(8,128)(2,1)S(1)} %pad_maximum_fusion.1), channel_id=1, source_target_pairs={{0,8},{8,16},{16,24},{24,32},{32,40},{40,48},{48,56},{56,64},{64,7... | collective-permute-start | bytes 884744 | tf_op jit(solution)/shard_map/ppermute | solution.py:15
  41.1 0.7 copy-start.2
  41.9 0.7 copy-start.3
  42.9 1.3 %copy-start.5 = (pred[384]{0:T(512)(128)(4,1)S(1)}, pred[384]{0:T(512)(128)(4,1)}, u32[]{:S(2)}) copy-start(pred[384]{0:T(512)(128)(4,1)} %get-tuple-element.28) | copy-start | bytes 1156
  42.9 1.3 %copy-start.6 = (pred[384]{0:T(512)(128)(4,1)S(1)}, pred[384]{0:T(512)(128)(4,1)}, u32[]{:S(2)}) copy-start(pred[384]{0:T(512)(128)(4,1)} %get-tuple-element.29) | copy-start | bytes 1156
  58.4 11.0 %slice-start = ((bf16[128,1152]{1,0:T(8,128)(2,1)}), bf16[64,1152]{1,0:T(8,128)(2,1)S(1)}, s32[]{:S(2)}) async-start(bf16[128,1152]{1,0:T(8,128)(2,1)} %copy-done.2), calls=%async_computation.4 | async-start | bytes 294912 | tf_op jit(solution)/shard_map/slice | solution.py:127
  58.4 11.0 %slice-start.1 = ((bf16[128,1152]{1,0:T(8,128)(2,1)}), bf16[64,1152]{1,0:T(8,128)(2,1)S(1)}, s32[]{:S(2)}) async-start(bf16[128,1152]{1,0:T(8,128)(2,1)} %copy-done.3), calls=%async_computation.5 | async-start | bytes 294912 | tf_op jit(solution)/shard_map/slice | solution.py:127
  58.4 23.1 %all-to-all-start.2 = ((bf16[8,168,128]{2,1,0:T(8,128)(2,1)}), bf16[8,168,128]{2,1,0:T(8,128)(2,1)S(1)}, u32[]{:S(2)}, u32[]{:S(2)}) async-start(bf16[8,168,128]{2,1,0:T(8,128)(2,1)} %bitcast.7), calls=%async_computation.2 | async-start | bytes 688128 | tf_op jit(solution)/shard_map/all_to_all | solution.py:34
  72.5 38.2 %collective-permute-start.4 = (bf16[64,1152]{1,0:T(8,128)(2,1)S(1)}, bf16[64,1152]{1,0:T(8,128)(2,1)S(1)}, u32[]{:S(2)}, u32[]{:S(2)}) collective-permute-start(bf16[64,1152]{1,0:T(8,128)(2,1)S(1)} %get-tuple-element.14), channel_id=1, source_target_pairs={{0,1008},{8,1016},{16,0},{24,8},{32,16},{40,24},{48,32},{56,40},{6... | collective-permute-start | bytes 442376 | tf_op jit(solution)/shard_map/ppermute | solution.py:15
  79.0 31.8 %collective-permute-start.3 = (bf16[64,1152]{1,0:T(8,128)(2,1)S(1)}, bf16[64,1152]{1,0:T(8,128)(2,1)S(1)}, u32[]{:S(2)}, u32[]{:S(2)}) collective-permute-start(bf16[64,1152]{1,0:T(8,128)(2,1)S(1)} %get-tuple-element.15), channel_id=1, source_target_pairs={{0,1016},{8,0},{16,8},{24,16},{32,24},{40,32},{48,40},{56,48},{64,... | collective-permute-start | bytes 442376 | tf_op jit(solution)/shard_map/ppermute | solution.py:15
  81.6 42.0 %copy-start.4 = (f32[192,1152]{1,0:T(8,128)S(1)}, f32[192,1152]{1,0:T(8,128)}, u32[]{:S(2)}) copy-start(f32[192,1152]{1,0:T(8,128)} %get-tuple-element.23) | copy-start | bytes 2654212
  111.5 19.6 %all-to-all-start.3 = ((bf16[8,168,128]{2,1,0:T(8,128)(2,1)}), bf16[8,168,128]{2,1,0:T(8,128)(2,1)S(1)}, u32[]{:S(2)}, u32[]{:S(2)}) async-start(bf16[8,168,128]{2,1,0:T(8,128)(2,1)} %broadcast_in_dim.39), calls=%async_computation.3 | async-start | bytes 688128 | tf_op jit(solution)/shard_map/all_to_all | solution.py:34

commit v13 on v12

--- a/solution.py
+++ b/solution.py
@@ -53,8 +53,8 @@
     ).astype(jnp.bfloat16)
     rows = jnp.pad(rows, ((0, count * share - tiles * width), (0, 0)))
     part = summed(swap(rows.reshape(count, share, LANES), "dp", near)).astype(jnp.bfloat16)
+    part, early = lax.optimization_barrier((part, early))
     total = summed(lax.all_gather(part, "dp", axis=0, axis_index_groups=far)).astype(jnp.bfloat16)
-    total, early = lax.optimization_barrier((total, early))
     whole = gathered(total, count, "dp", near).reshape(count * share, LANES)[: tiles * width]
     whole = whole.astype(jnp.float32).reshape(tiles, width, LANES)
     return jnp.swapaxes(whole, 1, 2).reshape(features, width), early
@@ -134,11 +134,11 @@
     txt_terms = scale * lax.dot_general(
         own_grad, z_img, (((1,), (1,)), ((), ())), preferred_element_type=jnp.float32
     )
+    d_weight, txt_terms = sum_over_dp(local_weight, txt_terms)
     sent = [
         passed_along(txt_terms[k * text_rows : (k + 1) * text_rows].astype(jnp.bfloat16), "dp", -k)
         for k in range(1, STEPS)
     ]
-    d_weight, sent = sum_over_dp(local_weight, sent)
 
     grad_txt = txt_terms[:text_rows]
     for term in sent:

time: 133 us -> 136 us (1.023)
    ppermute x4, waiting for transfers between devices: 16.3 us -> 19.3 us  [passed_along(): lax.ppermute(array, axis, [(i, (i + by) % count) for i in range(count)])]
    all_to_all x3, waiting for transfers between devices: 6.54 us -> 4.04 us  [swap(): return lax.all_to_all(parts, axis, 0, 0, axis_index_groups=groups)]
  transfers between devices with their start and end apart: 8 -> 8, of which waited for: 2 -> 3; matrix products, arithmetic and copies ran while one was open for 5% -> 5% of each run, Pallas kernels for 0% -> 0%
where the time goes in v13:
time: 136 us
  starting transfers between devices  51.4 us (38%)
  blocking collectives  42.3 us (31%)
  waiting for transfers between devices  23.3 us (17%)
  matrix products  5.95 us (4%)
  local copies, waits for them, and re-layouts  5.58 us (4%)
  other arithmetic  4.79 us (4%)
  between operations  2.23 us (2%)
    all_gather x1, blocking collectives, sum_over_dp(): lax.all_gather(part, 'dp', axis=0, axis_index_groups=far)  30.3 us
    all_to_all x3, starting transfers between devices, swap(): return lax.all_to_all(parts, axis, 0, 0, axis_index_groups=groups)  28.8 us
    ppermute x4, waiting for transfers between devices, passed_along(): lax.ppermute(array, axis, [(i, (i + by) % count) for i in range(count)])  19.3 us
    ppermute x4, starting transfers between devices, passed_along(): lax.ppermute(array, axis, [(i, (i + by) % count) for i in range(count)])  18.5 us
    all_to_all x1, blocking collectives, swap(): return lax.all_to_all(parts, axis, 0, 0, axis_index_groups=groups)  12.1 us
    ppermute x1, starting transfers between devices, to_partner(): lax.ppermute(array, 'emb', [(i, i ^ 1) for i in range(lax.axis_size('emb'...  4.08 us
    all_to_all x3, waiting for transfers between devices, swap(): return lax.all_to_all(parts, axis, 0, 0, axis_index_groups=groups)  4.04 us
  transfers between devices with their start and end apart: 8, of which 3 were waited for; matrix products, arithmetic and copies ran while one was open for 5% of the time, Pallas kernels for 0%

profile of v13, /device:TPU:1, one launch (start us, length us, event | category | flops | bytes accessed | tf_op | source)
XLA Modules:
  0.0 135.6 jit_solution(18200255002790037232)
XLA Ops:
  0.6 4.1 %collective-permute-start = (bf16[64,1152]{1,0:T(8,128)(2,1)}, bf16[64,1152]{1,0:T(8,128)(2,1)S(1)}, u32[]{:S(2)}, u32[]{:S(2)}) collective-permute-start(bf16[64,1152]{1,0:T(8,128)(2,1)} %param.7), channel_id=1, source_target_pairs={{0,1},{1,0},{2,3},{3,2},{4,5},{5,4},{6,7},{7,6},{8,9},{9,8},{10,11... | collective-permute-start | bytes 442376 | tf_op jit(solution)/shard_map/ppermute | solution.py:19
  6.1 1.5 %convolution_convert_fusion.1 = bf16[144,512]{1,0:T(8,128)(2,1)S(1)} fusion(bf16[1152,144]{0,1:T(8,128)(2,1)} %param.6, bf16[512,1152]{1,0:T(8,128)(2,1)S(1)} %copy-done), kind=kOutput, calls=%fused_computation.21 | convolution fusion | flops 169943040 | bytes 1658880 | tf_op jit(solution)/shard_map/dot_general | solution.py:95
  7.6 1.1 broadcast_in_dim.20
  8.9 5.9 %all-to-all-start = ((bf16[8,144,512]{2,1,0:T(8,128)(2,1)}), bf16[8,144,512]{2,1,0:T(8,128)(2,1)S(1)}, u32[]{:S(2)}, u32[]{:S(2)}) async-start(bf16[8,144,512]{2,1,0:T(8,128)(2,1)} %broadcast_in_dim.20), calls=%async_computation | async-start | bytes 2359296 | tf_op jit(solution)/shard_map/all_to_all | solution.py:34
  15.1 3.5 %collective-permute-start.2 = (bf16[128,1152]{1,0:T(8,128)(2,1)S(1)}, bf16[128,1152]{1,0:T(8,128)(2,1)S(1)}, u32[]{:S(2)}, u32[]{:S(2)}) collective-permute-start(bf16[128,1152]{1,0:T(8,128)(2,1)S(1)} %pad_maximum_fusion.1), channel_id=1, source_target_pairs={{0,16},{8,24},{16,32},{24,40},{32,48},{40,56},{48,64},{56,72},{64,... | collective-permute-start | bytes 884744 | tf_op jit(solution)/shard_map/ppermute | solution.py:15
  18.6 5.5 %collective-permute-start.1 = (bf16[128,1152]{1,0:T(8,128)(2,1)S(1)}, bf16[128,1152]{1,0:T(8,128)(2,1)S(1)}, u32[]{:S(2)}, u32[]{:S(2)}) collective-permute-start(bf16[128,1152]{1,0:T(8,128)(2,1)S(1)} %pad_maximum_fusion.1), channel_id=1, source_target_pairs={{0,8},{8,16},{16,24},{24,32},{32,40},{40,48},{48,56},{56,64},{64,7... | collective-permute-start | bytes 884744 | tf_op jit(solution)/shard_map/ppermute | solution.py:15
  24.2 0.6 iota_compare_fusion.3
  24.8 16.4 %collective-permute-done.2 = bf16[128,1152]{1,0:T(8,128)(2,1)S(1)} collective-permute-done((bf16[128,1152]{1,0:T(8,128)(2,1)S(1)}, bf16[128,1152]{1,0:T(8,128)(2,1)S(1)}, u32[]{:S(2)}, u32[]{:S(2)}) %collective-permute-start.2) | collective-permute-done | bytes 294944 | tf_op jit(solution)/shard_map/ppermute | solution.py:15
  41.1 0.7 copy-done.2
  41.8 0.7 copy-done.4
  42.6 0.2 fusion.11
  42.9 1.3 multiply_reduce_fusion.1
  44.2 0.8 fusion.1
  45.0 12.1 %all_to_all.20 = bf16[8,144,256]{2,1,0:T(8,128)(2,1)S(1)} all-to-all(bf16[8,144,256]{2,1,0:T(8,128)(2,1)S(1)} %bitcast.40), channel_id=1, replica_groups=mesh['dp'=128,'emb'=8] {'emb'}, dimensions={0} | all-to-all | bytes 1179648 | tf_op jit(solution)/shard_map/all_to_all | solution.py:34
  57.1 0.4 convolution_convert_fusion
  57.7 0.8 pad.4
  58.4 11.1 %all-to-all-start.2 = ((bf16[8,168,128]{2,1,0:T(8,128)(2,1)}), bf16[8,168,128]{2,1,0:T(8,128)(2,1)}, u32[]{:S(2)}, u32[]{:S(2)}) async-start(bf16[8,168,128]{2,1,0:T(8,128)(2,1)} %bitcast.7), calls=%async_computation.2 | async-start | bytes 688128 | tf_op jit(solution)/shard_map/all_to_all | solution.py:34
  69.6 0.7 slice.95
  70.3 0.7 slice.94
  70.9 0.3 multiply_reduce_fusion
  71.3 2.0 %convolution_multiply_fusion = f32[192,1152]{1,0:T(8,128)S(1)} fusion(bf16[1152,512]{1,0:T(8,128)(2,1)S(1)} %bitcast.35, f32[512]{0:T(512)S(1)} %add_rsqrt_fusion, bf16[64,1152]{1,0:T(8,128)(2,1)} %slice.95, bf16[64,1152]{1,0:T(8,128)(2,1)} %slice.94, bf16[64,1152]{1,0:T(8,128)(2,1)S(1)} %get-tuple-element.20, f32[]{:T(128)} %bitcast.27, f32[]{:T(128)} %bitcast.30, ...), kind=kOutput, calls=%fused_computation.2 | convolution fusion | flops 459251712 | bytes 2509768 | tf_op jit(solution)/shard_map/dot_general | solution.py:134
  73.2 4.0 %all-to-all-done.2 = bf16[8,168,128]{2,1,0:T(8,128)(2,1)} async-done(((bf16[8,168,128]{2,1,0:T(8,128)(2,1)}), bf16[8,168,128]{2,1,0:T(8,128)(2,1)}, u32[]{:S(2)}, u32[]{:S(2)}) %all-to-all-start.2) | async-done | bytes 344096 | tf_op jit(solution)/shard_map/all_to_all | solution.py:34
  77.3 1.0 reduce_sum.95
  78.3 30.3 %all-gather = bf16[2688,128]{1,0:T(8,128)(2,1)S(1)} all-gather(bf16[168,128]{1,0:T(8,128)(2,1)S(1)} %reduce_sum.95), channel_id=2, replica_groups={{0,32,64,96,128,160,192,224,256,288,320,352,384,416,448,480},{8,40,72,1..., dimensions={0}, use_global_device_ids=true | all-gather | bytes 731136 | tf_op jit(solution)/shard_map/all_gather | solution.py:57
  108.7 0.8 broadcast_in_dim.39
  109.5 11.7 %all-to-all-start.3 = ((bf16[8,168,128]{2,1,0:T(8,128)(2,1)}), bf16[8,168,128]{2,1,0:T(8,128)(2,1)S(1)}, u32[]{:S(2)}, u32[]{:S(2)}) async-start(bf16[8,168,128]{2,1,0:T(8,128)(2,1)} %broadcast_in_dim.39), calls=%async_computation.3 | async-start | bytes 688128 | tf_op jit(solution)/shard_map/all_to_all | solution.py:34
  121.2 2.0 %collective-permute-start.3 = (bf16[64,1152]{1,0:T(8,128)(2,1)S(1)}, bf16[64,1152]{1,0:T(8,128)(2,1)S(1)}, u32[]{:S(2)}, u32[]{:S(2)}) collective-permute-start(bf16[64,1152]{1,0:T(8,128)(2,1)S(1)} %get-tuple-element.12), channel_id=1, source_target_pairs={{0,1016},{8,0},{16,8},{24,16},{32,24},{40,32},{48,40},{56,48},{64,... | collective-permute-start | bytes 442376 | tf_op jit(solution)/shard_map/ppermute | solution.py:15
  123.3 7.4 %collective-permute-start.4 = (bf16[64,1152]{1,0:T(8,128)(2,1)S(1)}, bf16[64,1152]{1,0:T(8,128)(2,1)S(1)}, u32[]{:S(2)}, u32[]{:S(2)}) collective-permute-start(bf16[64,1152]{1,0:T(8,128)(2,1)S(1)} %get-tuple-element.13), channel_id=1, source_target_pairs={{0,1008},{8,1016},{16,0},{24,8},{32,16},{40,24},{48,32},{56,40},{6... | collective-permute-start | bytes 442376 | tf_op jit(solution)/shard_map/ppermute | solution.py:15
  130.7 2.9 %collective-permute-done.4 = bf16[64,1152]{1,0:T(8,128)(2,1)S(1)} collective-permute-done((bf16[64,1152]{1,0:T(8,128)(2,1)S(1)}, bf16[64,1152]{1,0:T(8,128)(2,1)S(1)}, u32[]{:S(2)}, u32[]{:S(2)}) %collective-permute-start.4) | collective-permute-done | bytes 147488 | tf_op jit(solution)/shard_map/ppermute | solution.py:15
  133.6 0.2 fusion.34
  133.8 0.8 fusion.36
  134.7 0.9 copy_bitcast_fusion
  (47 shorter events, 0.9 us)
Async XLA Ops:
  0.6 5.4 %copy-start = (bf16[512,1152]{1,0:T(8,128)(2,1)S(1)}, bf16[512,1152]{1,0:T(8,128)(2,1)}, u32[]{:S(2)}) copy-start(bf16[512,1152]{1,0:T(8,128)(2,1)} %param.5) | copy-start | bytes 3538948
  0.6 7.0 %collective-permute-start = (bf16[64,1152]{1,0:T(8,128)(2,1)}, bf16[64,1152]{1,0:T(8,128)(2,1)S(1)}, u32[]{:S(2)}, u32[]{:S(2)}) collective-permute-start(bf16[64,1152]{1,0:T(8,128)(2,1)} %param.7), channel_id=1, source_target_pairs={{0,1},{1,0},{2,3},{3,2},{4,5},{5,4},{6,7},{7,6},{8,9},{9,8},{10,11... | collective-permute-start | bytes 442376 | tf_op jit(solution)/shard_map/ppermute | solution.py:19
  6.1 2.7 %copy-start.1 = (bf16[64,1152]{1,0:T(8,128)(2,1)S(1)}, bf16[64,1152]{1,0:T(8,128)(2,1)}, u32[]{:S(2)}) copy-start(bf16[64,1152]{1,0:T(8,128)(2,1)} %param.7) | copy-start | bytes 442372
  8.9 33.8 %all-to-all-start = ((bf16[8,144,512]{2,1,0:T(8,128)(2,1)}), bf16[8,144,512]{2,1,0:T(8,128)(2,1)S(1)}, u32[]{:S(2)}, u32[]{:S(2)}) async-start(bf16[8,144,512]{2,1,0:T(8,128)(2,1)} %broadcast_in_dim.20), calls=%async_computation | async-start | bytes 2359296 | tf_op jit(solution)/shard_map/all_to_all | solution.py:34
  15.1 26.1 %collective-permute-start.2 = (bf16[128,1152]{1,0:T(8,128)(2,1)S(1)}, bf16[128,1152]{1,0:T(8,128)(2,1)S(1)}, u32[]{:S(2)}, u32[]{:S(2)}) collective-permute-start(bf16[128,1152]{1,0:T(8,128)(2,1)S(1)} %pad_maximum_fusion.1), channel_id=1, source_target_pairs={{0,16},{8,24},{16,32},{24,40},{32,48},{40,56},{48,64},{56,72},{64,... | collective-permute-start | bytes 884744 | tf_op jit(solution)/shard_map/ppermute | solution.py:15
  18.6 22.5 %collective-permute-start.1 = (bf16[128,1152]{1,0:T(8,128)(2,1)S(1)}, bf16[128,1152]{1,0:T(8,128)(2,1)S(1)}, u32[]{:S(2)}, u32[]{:S(2)}) collective-permute-start(bf16[128,1152]{1,0:T(8,128)(2,1)S(1)} %pad_maximum_fusion.1), channel_id=1, source_target_pairs={{0,8},{8,16},{16,24},{24,32},{32,40},{40,48},{48,56},{56,64},{64,7... | collective-permute-start | bytes 884744 | tf_op jit(solution)/shard_map/ppermute | solution.py:15
  41.1 0.7 copy-start.2
  41.8 0.7 copy-start.4
  42.9 1.3 copy-start.6
  42.9 1.3 copy-start.7
  57.5 12.1 %copy-start.3 = (bf16[128,1152]{1,0:T(8,128)(2,1)S(1)}, bf16[128,1152]{1,0:T(8,128)(2,1)}, u32[]{:S(2)}) copy-start(bf16[128,1152]{1,0:T(8,128)(2,1)} %copy-done.2) | copy-start | bytes 884740
  57.5 12.7 %copy-start.5 = (bf16[128,1152]{1,0:T(8,128)(2,1)S(1)}, bf16[128,1152]{1,0:T(8,128)(2,1)}, u32[]{:S(2)}) copy-start(bf16[128,1152]{1,0:T(8,128)(2,1)} %copy-done.4) | copy-start | bytes 884740
  58.4 18.8 %all-to-all-start.2 = ((bf16[8,168,128]{2,1,0:T(8,128)(2,1)}), bf16[8,168,128]{2,1,0:T(8,128)(2,1)}, u32[]{:S(2)}, u32[]{:S(2)}) async-start(bf16[8,168,128]{2,1,0:T(8,128)(2,1)} %bitcast.7), calls=%async_computation.2 | async-start | bytes 688128 | tf_op jit(solution)/shard_map/all_to_all | solution.py:34
  109.5 25.2 %all-to-all-start.3 = ((bf16[8,168,128]{2,1,0:T(8,128)(2,1)}), bf16[8,168,128]{2,1,0:T(8,128)(2,1)S(1)}, u32[]{:S(2)}, u32[]{:S(2)}) async-start(bf16[8,168,128]{2,1,0:T(8,128)(2,1)} %broadcast_in_dim.39), calls=%async_computation.3 | async-start | bytes 688128 | tf_op jit(solution)/shard_map/all_to_all | solution.py:34
  121.2 9.4 %collective-permute-start.3 = (bf16[64,1152]{1,0:T(8,128)(2,1)S(1)}, bf16[64,1152]{1,0:T(8,128)(2,1)S(1)}, u32[]{:S(2)}, u32[]{:S(2)}) collective-permute-start(bf16[64,1152]{1,0:T(8,128)(2,1)S(1)} %get-tuple-element.12), channel_id=1, source_target_pairs={{0,1016},{8,0},{16,8},{24,16},{32,24},{40,32},{48,40},{56,48},{64,... | collective-permute-start | bytes 442376 | tf_op jit(solution)/shard_map/ppermute | solution.py:15
  123.3 10.3 %collective-permute-start.4 = (bf16[64,1152]{1,0:T(8,128)(2,1)S(1)}, bf16[64,1152]{1,0:T(8,128)(2,1)S(1)}, u32[]{:S(2)}, u32[]{:S(2)}) collective-permute-start(bf16[64,1152]{1,0:T(8,128)(2,1)S(1)} %get-tuple-element.13), channel_id=1, source_target_pairs={{0,1008},{8,1016},{16,0},{24,8},{32,16},{40,24},{48,32},{56,40},{6... | collective-permute-start | bytes 442376 | tf_op jit(solution)/shard_map/ppermute | solution.py:15

commit v14 on v12

--- a/solution.py
+++ b/solution.py
@@ -80,8 +80,21 @@
     member = lax.axis_index("emb")
     half_rows = image_rows // PAIR
     first_row = (member % PAIR) * half_rows
+
+    partner_txt = to_partner(txt_emb)
+    local_proj = lax.dot_general(
+        w_proj, img_feat, (((0,), (1,)), ((), ())), preferred_element_type=jnp.float32
+    ).astype(jnp.bfloat16)
+    copies = jnp.broadcast_to(local_proj[None], (members,) + local_proj.shape)
+    copies, txt_emb, partner_txt, logit_scale, logit_bias = lax.optimization_barrier(
+        (copies, txt_emb, partner_txt, logit_scale, logit_bias)
+    )
     scale = logit_scale[0]
     offset = logit_bias[0]
+    unit_txt, inv_txt = unit_rows(txt_emb)
+    pair_txt = jnp.concatenate([unit_txt, unit_rows(partner_txt)[0]], axis=0).astype(jnp.bfloat16)
+    visitors = [pair_txt] + [passed_along(pair_txt, "dp", k) for k in range(1, STEPS)]
+    projected = swap(copies, "emb").reshape(features, image_rows)
 
     def slopes(texts, images, matches):
         cosines = jnp.dot(texts, images, preferred_element_type=jnp.float32)
@@ -90,17 +103,6 @@
         signs = jnp.where(matches(text, image), 1.0, -1.0)
         grads = -signs * jax.nn.sigmoid(-signs * (scale * cosines + offset))
         return cosines, grads.astype(jnp.bfloat16)
-
-    partner_txt = to_partner(txt_emb)
-    local_proj = lax.dot_general(
-        w_proj, img_feat, (((0,), (1,)), ((), ())), preferred_element_type=jnp.float32
-    ).astype(jnp.bfloat16)
-    copies = jnp.broadcast_to(local_proj[None], (members,) + local_proj.shape)
-    copies, txt_emb, partner_txt = lax.optimization_barrier((copies, txt_emb, partner_txt))
-    unit_txt, inv_txt = unit_rows(txt_emb)
-    pair_txt = jnp.concatenate([unit_txt, unit_rows(partner_txt)[0]], axis=0).astype(jnp.bfloat16)
-    visitors = [pair_txt] + [passed_along(pair_txt, "dp", k) for k in range(1, STEPS)]
-    projected = swap(copies, "emb").reshape(features, image_rows)
 
     mine = lax.dynamic_slice_in_dim(projected, first_row, half_rows, 1)
     unit_img, inv_img = unit_columns(mine)

time: 133 us -> 133 us (level)
  no operation moved by 1% of the time
where the time goes in v14:
time: 133 us; the launch traced here: 132 us
  starting transfers between devices  50.8 us (38%)
  blocking collectives  41.1 us (31%)
  waiting for transfers between devices  22.9 us (17%)
  matrix products  6.02 us (5%)
  local copies, waits for them, and re-layouts  5.25 us (4%)
  other arithmetic  3.78 us (3%)
  between operations  2.23 us (2%)
    all_gather x1, blocking collectives, sum_over_dp(): lax.all_gather(part, 'dp', axis=0, axis_index_groups=far)  29 us
    all_to_all x3, starting transfers between devices, swap(): return lax.all_to_all(parts, axis, 0, 0, axis_index_groups=groups)  28.6 us
    ppermute x4, starting transfers between devices, passed_along(): lax.ppermute(array, axis, [(i, (i + by) % count) for i in range(count)])  18.1 us
    ppermute x4, waiting for transfers between devices, passed_along(): lax.ppermute(array, axis, [(i, (i + by) % count) for i in range(count)])  16.3 us
    all_to_all x1, blocking collectives, swap(): return lax.all_to_all(parts, axis, 0, 0, axis_index_groups=groups)  12.1 us
    all_to_all x3, waiting for transfers between devices, swap(): return lax.all_to_all(parts, axis, 0, 0, axis_index_groups=groups)  6.54 us
    ppermute x1, starting transfers between devices, to_partner(): lax.ppermute(array, 'emb', [(i, i ^ 1) for i in range(lax.axis_size('emb'...  4.08 us
  transfers between devices with their start and end apart: 8, of which 2 were waited for; matrix products, arithmetic and copies ran while one was open for 5% of the time, Pallas kernels for 0%

profile of v14, /device:TPU:1, one launch (start us, length us, event | category | flops | bytes accessed | tf_op | source)
XLA Modules:
  0.0 132.1 jit_solution(6881558872497730061)
XLA Ops:
  0.6 4.1 %collective-permute-start = (bf16[64,1152]{1,0:T(8,128)(2,1)}, bf16[64,1152]{1,0:T(8,128)(2,1)S(1)}, u32[]{:S(2)}, u32[]{:S(2)}) collective-permute-start(bf16[64,1152]{1,0:T(8,128)(2,1)} %param.7), channel_id=1, source_target_pairs={{0,1},{1,0},{2,3},{3,2},{4,5},{5,4},{6,7},{7,6},{8,9},{9,8},{10,11... | collective-permute-start | bytes 442376 | tf_op jit(solution)/shard_map/ppermute | solution.py:19
  6.1 1.5 %convolution_convert_fusion.1 = bf16[144,512]{1,0:T(8,128)(2,1)S(1)} fusion(bf16[1152,144]{0,1:T(8,128)(2,1)} %param.6, bf16[512,1152]{1,0:T(8,128)(2,1)S(1)} %copy-done), kind=kOutput, calls=%fused_computation.11 | convolution fusion | flops 169943040 | bytes 1658880 | tf_op jit(solution)/shard_map/dot_general | solution.py:85
  7.6 1.1 broadcast_in_dim.20
  8.7 0.1 fusion.23
  8.9 5.9 %all-to-all-start = ((bf16[8,144,512]{2,1,0:T(8,128)(2,1)}), bf16[8,144,512]{2,1,0:T(8,128)(2,1)S(1)}, u32[]{:S(2)}, u32[]{:S(2)}) async-start(bf16[8,144,512]{2,1,0:T(8,128)(2,1)} %broadcast_in_dim.20), calls=%async_computation | async-start | bytes 2359296 | tf_op jit(solution)/shard_map/all_to_all | solution.py:34
  14.8 0.1 fusion.19
  15.1 3.5 %collective-permute-start.2 = (bf16[128,1152]{1,0:T(8,128)(2,1)S(1)}, bf16[128,1152]{1,0:T(8,128)(2,1)S(1)}, u32[]{:S(2)}, u32[]{:S(2)}) collective-permute-start(bf16[128,1152]{1,0:T(8,128)(2,1)S(1)} %pad_maximum_fusion.1), channel_id=1, source_target_pairs={{0,16},{8,24},{16,32},{24,40},{32,48},{40,56},{48,64},{56,72},{64,... | collective-permute-start | bytes 884744 | tf_op jit(solution)/shard_map/ppermute | solution.py:15
  18.6 5.5 %collective-permute-start.1 = (bf16[128,1152]{1,0:T(8,128)(2,1)S(1)}, bf16[128,1152]{1,0:T(8,128)(2,1)S(1)}, u32[]{:S(2)}, u32[]{:S(2)}) collective-permute-start(bf16[128,1152]{1,0:T(8,128)(2,1)S(1)} %pad_maximum_fusion.1), channel_id=1, source_target_pairs={{0,8},{8,16},{16,24},{24,32},{32,40},{40,48},{48,56},{56,64},{64,7... | collective-permute-start | bytes 884744 | tf_op jit(solution)/shard_map/ppermute | solution.py:15
  24.2 0.6 iota_compare_fusion.3
  24.8 16.3 %collective-permute-done.2 = bf16[128,1152]{1,0:T(8,128)(2,1)S(1)} collective-permute-done((bf16[128,1152]{1,0:T(8,128)(2,1)S(1)}, bf16[128,1152]{1,0:T(8,128)(2,1)S(1)}, u32[]{:S(2)}, u32[]{:S(2)}) %collective-permute-start.2) | collective-permute-done | bytes 294944 | tf_op jit(solution)/shard_map/ppermute | solution.py:15
  41.1 0.7 copy-done.2
  41.9 0.7 copy-done.3
  42.7 0.2 fusion.4
  42.9 1.3 multiply_reduce_fusion.1
  44.2 0.8 fusion.1
  45.0 12.1 %all_to_all.20 = bf16[8,144,256]{2,1,0:T(8,128)(2,1)S(1)} all-to-all(bf16[8,144,256]{2,1,0:T(8,128)(2,1)S(1)} %bitcast.40), channel_id=1, replica_groups=mesh['dp'=128,'emb'=8] {'emb'}, dimensions={0} | all-to-all | bytes 1179648 | tf_op jit(solution)/shard_map/all_to_all | solution.py:34
  57.2 0.4 convolution_convert_fusion
  57.7 0.8 pad.4
  58.4 10.7 %all-to-all-start.2 = ((bf16[8,168,128]{2,1,0:T(8,128)(2,1)}), bf16[8,168,128]{2,1,0:T(8,128)(2,1)S(1)}, u32[]{:S(2)}, u32[]{:S(2)}) async-start(bf16[8,168,128]{2,1,0:T(8,128)(2,1)} %bitcast.7), calls=%async_computation.2 | async-start | bytes 688128 | tf_op jit(solution)/shard_map/all_to_all | solution.py:34
  69.1 0.3 multiply_reduce_fusion
  69.4 2.0 %fusion.48 = (bf16[192,1152]{1,0:T(8,128)(2,1)}, f32[192,1152]{1,0:T(8,128)}) fusion(bf16[1152,512]{1,0:T(8,128)(2,1)S(1)} %bitcast.35, f32[512]{0:T(512)S(1)} %add_rsqrt_fusion, bf16[64,1152]{1,0:T(8,128)(2,1)S(1)} %slice-done, bf16[64,1152]{1,0:T(8,128)(2,1)S(1)} %slice-done.1, bf16[64,1152]{1,0:T(8,128)(2,1)S(1)} %get-tuple-element.28, f32[]{:T(128)} %bitcast.30, ...), kind=kOutput, calls=%fused_computation.87 | convolution fusion | flops 459472896 | bytes 2952136 | tf_op jit(solution)/shard_map/dot_general | solution.py:136
  71.5 1.0 fusion.47
  72.5 6.5 %collective-permute-start.4 = (bf16[64,1152]{1,0:T(8,128)(2,1)S(1)}, bf16[64,1152]{1,0:T(8,128)(2,1)S(1)}, u32[]{:S(2)}, u32[]{:S(2)}) collective-permute-start(bf16[64,1152]{1,0:T(8,128)(2,1)S(1)} %get-tuple-element.18), channel_id=1, source_target_pairs={{0,1008},{8,1016},{16,0},{24,8},{32,16},{40,24},{48,32},{56,40},{6... | collective-permute-start | bytes 442376 | tf_op jit(solution)/shard_map/ppermute | solution.py:15
  79.0 2.5 %collective-permute-start.3 = (bf16[64,1152]{1,0:T(8,128)(2,1)S(1)}, bf16[64,1152]{1,0:T(8,128)(2,1)S(1)}, u32[]{:S(2)}, u32[]{:S(2)}) collective-permute-start(bf16[64,1152]{1,0:T(8,128)(2,1)S(1)} %get-tuple-element.19), channel_id=1, source_target_pairs={{0,1016},{8,0},{16,8},{24,16},{32,24},{40,32},{48,40},{56,48},{64,... | collective-permute-start | bytes 442376 | tf_op jit(solution)/shard_map/ppermute | solution.py:15
  81.6 29.0 %all-gather = bf16[2688,128]{1,0:T(8,128)(2,1)S(1)} all-gather(bf16[168,128]{1,0:T(8,128)(2,1)S(1)} %reduce_sum.95), channel_id=2, replica_groups={{0,32,64,96,128,160,192,224,256,288,320,352,384,416,448,480},{8,40,72,1..., dimensions={0}, use_global_device_ids=true | all-gather | bytes 731136 | tf_op jit(solution)/shard_map/all_gather | solution.py:56
  110.6 0.1 reduce_sum.96
  110.7 0.8 broadcast_in_dim.39
  111.5 12.0 %all-to-all-start.3 = ((bf16[8,168,128]{2,1,0:T(8,128)(2,1)}), bf16[8,168,128]{2,1,0:T(8,128)(2,1)S(1)}, u32[]{:S(2)}, u32[]{:S(2)}) async-start(bf16[8,168,128]{2,1,0:T(8,128)(2,1)} %broadcast_in_dim.39), calls=%async_computation.3 | async-start | bytes 688128 | tf_op jit(solution)/shard_map/all_to_all | solution.py:34
  123.6 0.2 fusion.20
  123.8 0.8 fusion.22
  124.6 6.5 %all-to-all-done.3 = bf16[8,168,128]{2,1,0:T(8,128)(2,1)S(1)} async-done(((bf16[8,168,128]{2,1,0:T(8,128)(2,1)}), bf16[8,168,128]{2,1,0:T(8,128)(2,1)S(1)}, u32[]{:S(2)}, u32[]{:S(2)}) %all-to-all-start.3) | async-done | bytes 344096 | tf_op jit(solution)/shard_map/all_to_all | solution.py:34
  131.2 0.9 copy_bitcast_fusion
  (46 shorter events, 0.6 us)
Async XLA Ops:
  0.6 5.4 %copy-start = (bf16[512,1152]{1,0:T(8,128)(2,1)S(1)}, bf16[512,1152]{1,0:T(8,128)(2,1)}, u32[]{:S(2)}) copy-start(bf16[512,1152]{1,0:T(8,128)(2,1)} %param.5) | copy-start | bytes 3538948
  0.6 7.0 %collective-permute-start = (bf16[64,1152]{1,0:T(8,128)(2,1)}, bf16[64,1152]{1,0:T(8,128)(2,1)S(1)}, u32[]{:S(2)}, u32[]{:S(2)}) collective-permute-start(bf16[64,1152]{1,0:T(8,128)(2,1)} %param.7), channel_id=1, source_target_pairs={{0,1},{1,0},{2,3},{3,2},{4,5},{5,4},{6,7},{7,6},{8,9},{9,8},{10,11... | collective-permute-start | bytes 442376 | tf_op jit(solution)/shard_map/ppermute | solution.py:19
  6.1 2.7 %copy-start.1 = (bf16[64,1152]{1,0:T(8,128)(2,1)S(1)}, bf16[64,1152]{1,0:T(8,128)(2,1)}, u32[]{:S(2)}) copy-start(bf16[64,1152]{1,0:T(8,128)(2,1)} %param.7) | copy-start | bytes 442372
  8.9 33.8 %all-to-all-start = ((bf16[8,144,512]{2,1,0:T(8,128)(2,1)}), bf16[8,144,512]{2,1,0:T(8,128)(2,1)S(1)}, u32[]{:S(2)}, u32[]{:S(2)}) async-start(bf16[8,144,512]{2,1,0:T(8,128)(2,1)} %broadcast_in_dim.20), calls=%async_computation | async-start | bytes 2359296 | tf_op jit(solution)/shard_map/all_to_all | solution.py:34
  15.1 26.1 %collective-permute-start.2 = (bf16[128,1152]{1,0:T(8,128)(2,1)S(1)}, bf16[128,1152]{1,0:T(8,128)(2,1)S(1)}, u32[]{:S(2)}, u32[]{:S(2)}) collective-permute-start(bf16[128,1152]{1,0:T(8,128)(2,1)S(1)} %pad_maximum_fusion.1), channel_id=1, source_target_pairs={{0,16},{8,24},{16,32},{24,40},{32,48},{40,56},{48,64},{56,72},{64,... | collective-permute-start | bytes 884744 | tf_op jit(solution)/shard_map/ppermute | solution.py:15
  18.6 22.5 %collective-permute-start.1 = (bf16[128,1152]{1,0:T(8,128)(2,1)S(1)}, bf16[128,1152]{1,0:T(8,128)(2,1)S(1)}, u32[]{:S(2)}, u32[]{:S(2)}) collective-permute-start(bf16[128,1152]{1,0:T(8,128)(2,1)S(1)} %pad_maximum_fusion.1), channel_id=1, source_target_pairs={{0,8},{8,16},{16,24},{24,32},{32,40},{40,48},{48,56},{56,64},{64,7... | collective-permute-start | bytes 884744 | tf_op jit(solution)/shard_map/ppermute | solution.py:15
  41.1 0.7 copy-start.2
  41.9 0.7 copy-start.3
  42.9 1.3 %copy-start.5 = (pred[384]{0:T(512)(128)(4,1)S(1)}, pred[384]{0:T(512)(128)(4,1)}, u32[]{:S(2)}) copy-start(pred[384]{0:T(512)(128)(4,1)} %get-tuple-element.32) | copy-start | bytes 1156
  42.9 1.3 %copy-start.6 = (pred[384]{0:T(512)(128)(4,1)S(1)}, pred[384]{0:T(512)(128)(4,1)}, u32[]{:S(2)}) copy-start(pred[384]{0:T(512)(128)(4,1)} %get-tuple-element.33) | copy-start | bytes 1156
  58.4 11.0 %slice-start = ((bf16[128,1152]{1,0:T(8,128)(2,1)}), bf16[64,1152]{1,0:T(8,128)(2,1)S(1)}, s32[]{:S(2)}) async-start(bf16[128,1152]{1,0:T(8,128)(2,1)} %copy-done.2), calls=%async_computation.4 | async-start | bytes 294912 | tf_op jit(solution)/shard_map/slice | solution.py:129
  58.4 11.0 %slice-start.1 = ((bf16[128,1152]{1,0:T(8,128)(2,1)}), bf16[64,1152]{1,0:T(8,128)(2,1)S(1)}, s32[]{:S(2)}) async-start(bf16[128,1152]{1,0:T(8,128)(2,1)} %copy-done.3), calls=%async_computation.5 | async-start | bytes 294912 | tf_op jit(solution)/shard_map/slice | solution.py:129
  58.4 23.1 %all-to-all-start.2 = ((bf16[8,168,128]{2,1,0:T(8,128)(2,1)}), bf16[8,168,128]{2,1,0:T(8,128)(2,1)S(1)}, u32[]{:S(2)}, u32[]{:S(2)}) async-start(bf16[8,168,128]{2,1,0:T(8,128)(2,1)} %bitcast.7), calls=%async_computation.2 | async-start | bytes 688128 | tf_op jit(solution)/shard_map/all_to_all | solution.py:34
  72.5 38.2 %collective-permute-start.4 = (bf16[64,1152]{1,0:T(8,128)(2,1)S(1)}, bf16[64,1152]{1,0:T(8,128)(2,1)S(1)}, u32[]{:S(2)}, u32[]{:S(2)}) collective-permute-start(bf16[64,1152]{1,0:T(8,128)(2,1)S(1)} %get-tuple-element.18), channel_id=1, source_target_pairs={{0,1008},{8,1016},{16,0},{24,8},{32,16},{40,24},{48,32},{56,40},{6... | collective-permute-start | bytes 442376 | tf_op jit(solution)/shard_map/ppermute | solution.py:15
  79.0 31.8 %collective-permute-start.3 = (bf16[64,1152]{1,0:T(8,128)(2,1)S(1)}, bf16[64,1152]{1,0:T(8,128)(2,1)S(1)}, u32[]{:S(2)}, u32[]{:S(2)}) collective-permute-start(bf16[64,1152]{1,0:T(8,128)(2,1)S(1)} %get-tuple-element.19), channel_id=1, source_target_pairs={{0,1016},{8,0},{16,8},{24,16},{32,24},{40,32},{48,40},{56,48},{64,... | collective-permute-start | bytes 442376 | tf_op jit(solution)/shard_map/ppermute | solution.py:15
  81.6 42.0 %copy-start.4 = (f32[192,1152]{1,0:T(8,128)S(1)}, f32[192,1152]{1,0:T(8,128)}, u32[]{:S(2)}) copy-start(f32[192,1152]{1,0:T(8,128)} %get-tuple-element.27) | copy-start | bytes 2654212
  111.5 19.6 %all-to-all-start.3 = ((bf16[8,168,128]{2,1,0:T(8,128)(2,1)}), bf16[8,168,128]{2,1,0:T(8,128)(2,1)S(1)}, u32[]{:S(2)}, u32[]{:S(2)}) async-start(bf16[8,168,128]{2,1,0:T(8,128)(2,1)} %broadcast_in_dim.39), calls=%async_computation.3 | async-start | bytes 688128 | tf_op jit(solution)/shard_map/all_to_all | solution.py:34

commit v15 on v14

--- a/solution.py
+++ b/solution.py
@@ -86,8 +86,8 @@
         w_proj, img_feat, (((0,), (1,)), ((), ())), preferred_element_type=jnp.float32
     ).astype(jnp.bfloat16)
     copies = jnp.broadcast_to(local_proj[None], (members,) + local_proj.shape)
-    copies, txt_emb, partner_txt, logit_scale, logit_bias = lax.optimization_barrier(
-        (copies, txt_emb, partner_txt, logit_scale, logit_bias)
+    copies, txt_emb, logit_scale, logit_bias = lax.optimization_barrier(
+        (copies, txt_emb, logit_scale, logit_bias)
     )
     scale = logit_scale[0]
     offset = logit_bias[0]

time: 133 us -> 132 us (level)
  starting transfers between devices: 50.8 us -> 47.3 us
  waiting for transfers between devices: 22.9 us -> 24.4 us
    all_to_all x3, starting transfers between devices: 28.6 us -> 26.1 us  [swap(): return lax.all_to_all(parts, axis, 0, 0, axis_index_groups=groups)]
    ppermute x4, waiting for transfers between devices: 16.3 us -> 17.9 us  [passed_along(): lax.ppermute(array, axis, [(i, (i + by) % count) for i in range(count)])]
  transfers between devices with their start and end apart: 8 -> 8, of which waited for: 2 -> 2; matrix products, arithmetic and copies ran while one was open for 5% -> 6% of each run, Pallas kernels for 0% -> 0%
where the time goes in v15:
time: 132 us; the launch traced here: 131 us
  starting transfers between devices  47.3 us (36%)
  blocking collectives  42.4 us (32%)
  waiting for transfers between devices  24.4 us (18%)
  matrix products  5.93 us (4%)
  local copies, waits for them, and re-layouts  5.25 us (4%)
  other arithmetic  3.83 us (3%)
  between operations  2.23 us (2%)
    all_gather x1, blocking collectives, sum_over_dp(): lax.all_gather(part, 'dp', axis=0, axis_index_groups=far)  30.3 us
    all_to_all x3, starting transfers between devices, swap(): return lax.all_to_all(parts, axis, 0, 0, axis_index_groups=groups)  26.1 us
    ppermute x4, waiting for transfers between devices, passed_along(): lax.ppermute(array, axis, [(i, (i + by) % count) for i in range(count)])  17.9 us
    ppermute x4, starting transfers between devices, passed_along(): lax.ppermute(array, axis, [(i, (i + by) % count) for i in range(count)])  17.2 us
    all_to_all x1, blocking collectives, swap(): return lax.all_to_all(parts, axis, 0, 0, axis_index_groups=groups)  12 us
    all_to_all x3, waiting for transfers between devices, swap(): return lax.all_to_all(parts, axis, 0, 0, axis_index_groups=groups)  6.54 us
    ppermute x1, starting transfers between devices, to_partner(): lax.ppermute(array, 'emb', [(i, i ^ 1) for i in range(lax.axis_size('emb'...  4.08 us
  transfers between devices with their start and end apart: 8, of which 2 were waited for; matrix products, arithmetic and copies ran while one was open for 6% of the time, Pallas kernels for 0%

profile of v15, /device:TPU:1, one launch (start us, length us, event | category | flops | bytes accessed | tf_op | source)
XLA Modules:
  0.0 131.3 jit_solution(6761441718263038997)
XLA Ops:
  0.6 4.1 %collective-permute-start = (bf16[64,1152]{1,0:T(8,128)(2,1)}, bf16[64,1152]{1,0:T(8,128)(2,1)S(1)}, u32[]{:S(2)}, u32[]{:S(2)}) collective-permute-start(bf16[64,1152]{1,0:T(8,128)(2,1)} %param.7), channel_id=1, source_target_pairs={{0,1},{1,0},{2,3},{3,2},{4,5},{5,4},{6,7},{7,6},{8,9},{9,8},{10,11... | collective-permute-start | bytes 442376 | tf_op jit(solution)/shard_map/ppermute | solution.py:19
  4.7 1.5 %convolution_convert_fusion.1 = bf16[144,512]{1,0:T(8,128)(2,1)S(1)} fusion(bf16[1152,144]{0,1:T(8,128)(2,1)} %param.6, bf16[512,1152]{1,0:T(8,128)(2,1)S(1)} %copy-done), kind=kOutput, calls=%fused_computation.21 | convolution fusion | flops 169943040 | bytes 1658880 | tf_op jit(solution)/shard_map/dot_general | solution.py:85
  6.3 1.1 broadcast_in_dim.20
  7.4 4.3 %all-to-all-start = ((bf16[8,144,512]{2,1,0:T(8,128)(2,1)}), bf16[8,144,512]{2,1,0:T(8,128)(2,1)S(1)}, u32[]{:S(2)}, u32[]{:S(2)}) async-start(bf16[8,144,512]{2,1,0:T(8,128)(2,1)} %broadcast_in_dim.20), calls=%async_computation | async-start | bytes 2359296 | tf_op jit(solution)/shard_map/all_to_all | solution.py:34
  11.7 0.1 fusion.37
  13.3 0.1 fusion.38
  13.6 3.5 %collective-permute-start.2 = (bf16[128,1152]{1,0:T(8,128)(2,1)S(1)}, bf16[128,1152]{1,0:T(8,128)(2,1)S(1)}, u32[]{:S(2)}, u32[]{:S(2)}) collective-permute-start(bf16[128,1152]{1,0:T(8,128)(2,1)S(1)} %pad_maximum_fusion.1), channel_id=1, source_target_pairs={{0,16},{8,24},{16,32},{24,40},{32,48},{40,56},{48,64},{56,72},{64,... | collective-permute-start | bytes 884744 | tf_op jit(solution)/shard_map/ppermute | solution.py:15
  17.1 4.9 %collective-permute-start.1 = (bf16[128,1152]{1,0:T(8,128)(2,1)S(1)}, bf16[128,1152]{1,0:T(8,128)(2,1)S(1)}, u32[]{:S(2)}, u32[]{:S(2)}) collective-permute-start(bf16[128,1152]{1,0:T(8,128)(2,1)S(1)} %pad_maximum_fusion.1), channel_id=1, source_target_pairs={{0,8},{8,16},{16,24},{24,32},{32,40},{40,48},{48,56},{56,64},{64,7... | collective-permute-start | bytes 884744 | tf_op jit(solution)/shard_map/ppermute | solution.py:15
  22.1 0.5 iota_compare_fusion.3
  22.6 17.9 %collective-permute-done.2 = bf16[128,1152]{1,0:T(8,128)(2,1)S(1)} collective-permute-done((bf16[128,1152]{1,0:T(8,128)(2,1)S(1)}, bf16[128,1152]{1,0:T(8,128)(2,1)S(1)}, u32[]{:S(2)}, u32[]{:S(2)}) %collective-permute-start.2) | collective-permute-done | bytes 294944 | tf_op jit(solution)/shard_map/ppermute | solution.py:15
  40.5 0.7 copy-done.2
  41.2 0.7 copy-done.3
  42.0 0.2 fusion.11
  42.2 1.3 multiply_reduce_fusion.1
  43.5 0.8 fusion.1
  44.3 12.0 %all_to_all.20 = bf16[8,144,256]{2,1,0:T(8,128)(2,1)S(1)} all-to-all(bf16[8,144,256]{2,1,0:T(8,128)(2,1)S(1)} %bitcast.40), channel_id=1, replica_groups=mesh['dp'=128,'emb'=8] {'emb'}, dimensions={0} | all-to-all | bytes 1179648 | tf_op jit(solution)/shard_map/all_to_all | solution.py:34
  56.4 0.4 convolution_convert_fusion
  56.9 0.8 pad.4
  57.7 9.5 %all-to-all-start.2 = ((bf16[8,168,128]{2,1,0:T(8,128)(2,1)}), bf16[8,168,128]{2,1,0:T(8,128)(2,1)S(1)}, u32[]{:S(2)}, u32[]{:S(2)}) async-start(bf16[8,168,128]{2,1,0:T(8,128)(2,1)} %bitcast.7), calls=%async_computation.2 | async-start | bytes 688128 | tf_op jit(solution)/shard_map/all_to_all | solution.py:34
  67.2 0.3 multiply_reduce_fusion
  67.6 2.0 %fusion.58 = (bf16[192,1152]{1,0:T(8,128)(2,1)}, f32[192,1152]{1,0:T(8,128)}) fusion(bf16[1152,512]{1,0:T(8,128)(2,1)S(1)} %bitcast.35, f32[512]{0:T(512)S(1)} %add_rsqrt_fusion, bf16[64,1152]{1,0:T(8,128)(2,1)S(1)} %slice-done, bf16[64,1152]{1,0:T(8,128)(2,1)S(1)} %slice-done.1, bf16[64,1152]{1,0:T(8,128)(2,1)S(1)} %fusion.33, f32[]{:T(128)} %bitcast.30, ...), kind=kOutput, calls=%fused_computation.95 | convolution fusion | flops 459472896 | bytes 2952136 | tf_op jit(solution)/shard_map/dot_general | solution.py:136
  69.6 1.0 fusion.57
  70.6 6.1 %collective-permute-start.4 = (bf16[64,1152]{1,0:T(8,128)(2,1)S(1)}, bf16[64,1152]{1,0:T(8,128)(2,1)S(1)}, u32[]{:S(2)}, u32[]{:S(2)}) collective-permute-start(bf16[64,1152]{1,0:T(8,128)(2,1)S(1)} %get-tuple-element.16), channel_id=1, source_target_pairs={{0,1008},{8,1016},{16,0},{24,8},{32,16},{40,24},{48,32},{56,40},{6... | collective-permute-start | bytes 442376 | tf_op jit(solution)/shard_map/ppermute | solution.py:15
  76.7 2.5 %collective-permute-start.3 = (bf16[64,1152]{1,0:T(8,128)(2,1)S(1)}, bf16[64,1152]{1,0:T(8,128)(2,1)S(1)}, u32[]{:S(2)}, u32[]{:S(2)}) collective-permute-start(bf16[64,1152]{1,0:T(8,128)(2,1)S(1)} %get-tuple-element.17), channel_id=1, source_target_pairs={{0,1016},{8,0},{16,8},{24,16},{32,24},{40,32},{48,40},{56,48},{64,... | collective-permute-start | bytes 442376 | tf_op jit(solution)/shard_map/ppermute | solution.py:15
  79.4 30.3 %all-gather = bf16[2688,128]{1,0:T(8,128)(2,1)S(1)} all-gather(bf16[168,128]{1,0:T(8,128)(2,1)S(1)} %reduce_sum.95), channel_id=2, replica_groups={{0,32,64,96,128,160,192,224,256,288,320,352,384,416,448,480},{8,40,72,1..., dimensions={0}, use_global_device_ids=true | all-gather | bytes 731136 | tf_op jit(solution)/shard_map/all_gather | solution.py:56
  109.7 0.1 reduce_sum.96
  109.8 0.8 broadcast_in_dim.39
  110.6 12.3 %all-to-all-start.3 = ((bf16[8,168,128]{2,1,0:T(8,128)(2,1)}), bf16[8,168,128]{2,1,0:T(8,128)(2,1)S(1)}, u32[]{:S(2)}, u32[]{:S(2)}) async-start(bf16[8,168,128]{2,1,0:T(8,128)(2,1)} %broadcast_in_dim.39), calls=%async_computation.3 | async-start | bytes 688128 | tf_op jit(solution)/shard_map/all_to_all | solution.py:34
  122.8 0.2 fusion.34
  123.0 0.8 fusion.36
  123.9 6.5 %all-to-all-done.3 = bf16[8,168,128]{2,1,0:T(8,128)(2,1)S(1)} async-done(((bf16[8,168,128]{2,1,0:T(8,128)(2,1)}), bf16[8,168,128]{2,1,0:T(8,128)(2,1)S(1)}, u32[]{:S(2)}, u32[]{:S(2)}) %all-to-all-start.3) | async-done | bytes 344096 | tf_op jit(solution)/shard_map/all_to_all | solution.py:34
  130.4 0.9 copy_bitcast_fusion
  (47 shorter events, 0.7 us)
Async XLA Ops:
  0.6 4.1 %copy-start = (bf16[512,1152]{1,0:T(8,128)(2,1)S(1)}, bf16[512,1152]{1,0:T(8,128)(2,1)}, u32[]{:S(2)}) copy-start(bf16[512,1152]{1,0:T(8,128)(2,1)} %param.5) | copy-start | bytes 3538948
  0.6 12.6 %collective-permute-start = (bf16[64,1152]{1,0:T(8,128)(2,1)}, bf16[64,1152]{1,0:T(8,128)(2,1)S(1)}, u32[]{:S(2)}, u32[]{:S(2)}) collective-permute-start(bf16[64,1152]{1,0:T(8,128)(2,1)} %param.7), channel_id=1, source_target_pairs={{0,1},{1,0},{2,3},{3,2},{4,5},{5,4},{6,7},{7,6},{8,9},{9,8},{10,11... | collective-permute-start | bytes 442376 | tf_op jit(solution)/shard_map/ppermute | solution.py:19
  7.4 4.3 %copy-start.1 = (bf16[64,1152]{1,0:T(8,128)(2,1)S(1)}, bf16[64,1152]{1,0:T(8,128)(2,1)}, u32[]{:S(2)}) copy-start(bf16[64,1152]{1,0:T(8,128)(2,1)} %param.7) | copy-start | bytes 442372
  7.4 34.6 %all-to-all-start = ((bf16[8,144,512]{2,1,0:T(8,128)(2,1)}), bf16[8,144,512]{2,1,0:T(8,128)(2,1)S(1)}, u32[]{:S(2)}, u32[]{:S(2)}) async-start(bf16[8,144,512]{2,1,0:T(8,128)(2,1)} %broadcast_in_dim.20), calls=%async_computation | async-start | bytes 2359296 | tf_op jit(solution)/shard_map/all_to_all | solution.py:34
  13.6 26.9 %collective-permute-start.2 = (bf16[128,1152]{1,0:T(8,128)(2,1)S(1)}, bf16[128,1152]{1,0:T(8,128)(2,1)S(1)}, u32[]{:S(2)}, u32[]{:S(2)}) collective-permute-start(bf16[128,1152]{1,0:T(8,128)(2,1)S(1)} %pad_maximum_fusion.1), channel_id=1, source_target_pairs={{0,16},{8,24},{16,32},{24,40},{32,48},{40,56},{48,64},{56,72},{64,... | collective-permute-start | bytes 884744 | tf_op jit(solution)/shard_map/ppermute | solution.py:15
  17.1 23.4 %collective-permute-start.1 = (bf16[128,1152]{1,0:T(8,128)(2,1)S(1)}, bf16[128,1152]{1,0:T(8,128)(2,1)S(1)}, u32[]{:S(2)}, u32[]{:S(2)}) collective-permute-start(bf16[128,1152]{1,0:T(8,128)(2,1)S(1)} %pad_maximum_fusion.1), channel_id=1, source_target_pairs={{0,8},{8,16},{16,24},{24,32},{32,40},{40,48},{48,56},{56,64},{64,7... | collective-permute-start | bytes 884744 | tf_op jit(solution)/shard_map/ppermute | solution.py:15
  40.5 0.7 copy-start.2
  41.2 0.7 copy-start.3
  42.2 1.3 copy-start.5
  42.2 1.3 copy-start.6
  57.7 9.8 %slice-start = ((bf16[128,1152]{1,0:T(8,128)(2,1)}), bf16[64,1152]{1,0:T(8,128)(2,1)S(1)}, s32[]{:S(2)}) async-start(bf16[128,1152]{1,0:T(8,128)(2,1)} %copy-done.2), calls=%async_computation.4 | async-start | bytes 294912 | tf_op jit(solution)/shard_map/slice | solution.py:129
  57.7 9.8 %slice-start.1 = ((bf16[128,1152]{1,0:T(8,128)(2,1)}), bf16[64,1152]{1,0:T(8,128)(2,1)S(1)}, s32[]{:S(2)}) async-start(bf16[128,1152]{1,0:T(8,128)(2,1)} %copy-done.3), calls=%async_computation.5 | async-start | bytes 294912 | tf_op jit(solution)/shard_map/slice | solution.py:129
  57.7 21.6 %all-to-all-start.2 = ((bf16[8,168,128]{2,1,0:T(8,128)(2,1)}), bf16[8,168,128]{2,1,0:T(8,128)(2,1)S(1)}, u32[]{:S(2)}, u32[]{:S(2)}) async-start(bf16[8,168,128]{2,1,0:T(8,128)(2,1)} %bitcast.7), calls=%async_computation.2 | async-start | bytes 688128 | tf_op jit(solution)/shard_map/all_to_all | solution.py:34
  70.6 39.2 %collective-permute-start.4 = (bf16[64,1152]{1,0:T(8,128)(2,1)S(1)}, bf16[64,1152]{1,0:T(8,128)(2,1)S(1)}, u32[]{:S(2)}, u32[]{:S(2)}) collective-permute-start(bf16[64,1152]{1,0:T(8,128)(2,1)S(1)} %get-tuple-element.16), channel_id=1, source_target_pairs={{0,1008},{8,1016},{16,0},{24,8},{32,16},{40,24},{48,32},{56,40},{6... | collective-permute-start | bytes 442376 | tf_op jit(solution)/shard_map/ppermute | solution.py:15
  76.7 33.1 %collective-permute-start.3 = (bf16[64,1152]{1,0:T(8,128)(2,1)S(1)}, bf16[64,1152]{1,0:T(8,128)(2,1)S(1)}, u32[]{:S(2)}, u32[]{:S(2)}) collective-permute-start(bf16[64,1152]{1,0:T(8,128)(2,1)S(1)} %get-tuple-element.17), channel_id=1, source_target_pairs={{0,1016},{8,0},{16,8},{24,16},{32,24},{40,32},{48,40},{56,48},{64,... | collective-permute-start | bytes 442376 | tf_op jit(solution)/shard_map/ppermute | solution.py:15
  79.4 43.5 %copy-start.4 = (f32[192,1152]{1,0:T(8,128)S(1)}, f32[192,1152]{1,0:T(8,128)}, u32[]{:S(2)}) copy-start(f32[192,1152]{1,0:T(8,128)} %get-tuple-element.25) | copy-start | bytes 2654212
  110.6 19.8 %all-to-all-start.3 = ((bf16[8,168,128]{2,1,0:T(8,128)(2,1)}), bf16[8,168,128]{2,1,0:T(8,128)(2,1)S(1)}, u32[]{:S(2)}, u32[]{:S(2)}) async-start(bf16[8,168,128]{2,1,0:T(8,128)(2,1)} %broadcast_in_dim.39), calls=%async_computation.3 | async-start | bytes 688128 | tf_op jit(solution)/shard_map/all_to_all | solution.py:34

commit v16 on v15

--- a/solution.py
+++ b/solution.py
@@ -91,8 +91,8 @@
     )
     scale = logit_scale[0]
     offset = logit_bias[0]
-    unit_txt, inv_txt = unit_rows(txt_emb)
-    pair_txt = jnp.concatenate([unit_txt, unit_rows(partner_txt)[0]], axis=0).astype(jnp.bfloat16)
+    unit_txt, inv_txt = lax.optimization_barrier(unit_rows(txt_emb))
+    pair_txt = jnp.concatenate([txt_emb, partner_txt], axis=0)
     visitors = [pair_txt] + [passed_along(pair_txt, "dp", k) for k in range(1, STEPS)]
     projected = swap(copies, "emb").reshape(features, image_rows)
 
@@ -106,7 +106,8 @@
 
     mine = lax.dynamic_slice_in_dim(projected, first_row, half_rows, 1)
     unit_img, inv_img = unit_columns(mine)
-    texts = lax.optimization_barrier(jnp.concatenate(visitors, axis=0))
+    texts = unit_rows(jnp.concatenate(visitors, axis=0))[0].astype(jnp.bfloat16)
+    texts = lax.optimization_barrier(texts)
 
     def pair_matches(text, image):
         row = image + first_row
@@ -126,7 +127,8 @@
     grad_part = jnp.concatenate([grad_part[h] for h in range(PAIR)], axis=1)
     local_weight = jnp.dot(grad_part, img_feat, preferred_element_type=jnp.float32)
 
-    own_texts = jnp.concatenate([visitor[:text_rows] for visitor in visitors], axis=0)
+    firsts = [k * PAIR * text_rows for k in range(STEPS)]
+    own_texts = jnp.concatenate([texts[i : i + text_rows] for i in firsts], axis=0)
     z_img = unit_columns(projected)[0].astype(jnp.bfloat16)
     own_grad = slopes(
         own_texts,

time: 132 us -> 133 us (level)
  starting transfers between devices: 47.3 us -> 44.4 us
  other arithmetic: 3.83 us -> 5.93 us
  blocking collectives: 42.4 us -> 43.8 us
    all_to_all x3, starting transfers between devices: 26.1 us -> 24.1 us  [swap(): return lax.all_to_all(parts, axis, 0, 0, axis_index_groups=groups)]
    all_gather x1, blocking collectives: 30.3 us -> 31.8 us  [sum_over_dp(): lax.all_gather(part, 'dp', axis=0, axis_index_groups=far)]
  transfers between devices with their start and end apart: 8 -> 8, of which waited for: 2 -> 2; matrix products, arithmetic and copies ran while one was open for 6% -> 9% of each run, Pallas kernels for 0% -> 0%
where the time goes in v16:
time: 133 us; the launch traced here: 132 us
  starting transfers between devices  44.4 us (33%)
  blocking collectives  43.8 us (33%)
  waiting for transfers between devices  24.2 us (18%)
  matrix products  6.64 us (5%)
  other arithmetic  5.93 us (4%)
  local copies, waits for them, and re-layouts  5.12 us (4%)
  between operations  2.23 us (2%)
    all_gather x1, blocking collectives, sum_over_dp(): lax.all_gather(part, 'dp', axis=0, axis_index_groups=far)  31.8 us
    all_to_all x3, starting transfers between devices, swap(): return lax.all_to_all(parts, axis, 0, 0, axis_index_groups=groups)  24.1 us
    ppermute x4, waiting for transfers between devices, passed_along(): lax.ppermute(array, axis, [(i, (i + by) % count) for i in range(count)])  17.9 us
    ppermute x4, starting transfers between devices, passed_along(): lax.ppermute(array, axis, [(i, (i + by) % count) for i in range(count)])  16.2 us
    all_to_all x1, blocking collectives, swap(): return lax.all_to_all(parts, axis, 0, 0, axis_index_groups=groups)  12.1 us
    all_to_all x3, waiting for transfers between devices, swap(): return lax.all_to_all(parts, axis, 0, 0, axis_index_groups=groups)  6.34 us
    ppermute x1, starting transfers between devices, to_partner(): lax.ppermute(array, 'emb', [(i, i ^ 1) for i in range(lax.axis_size('emb'...  4.08 us
    dot_general x1, matrix products, local(): lax.dot_general(own_grad, z_img, (((1,), (1,)), ((), ())), preferred_elem...  2.74 us
  transfers between devices with their start and end apart: 8, of which 2 were waited for; matrix products, arithmetic and copies ran while one was open for 9% of the time, Pallas kernels for 0%

profile of v16, /device:TPU:1, one launch (start us, length us, event | category | flops | bytes accessed | tf_op | source)
XLA Modules:
  0.0 132.3 jit_solution(8635122020647682621)
XLA Ops:
  0.6 4.1 %collective-permute-start = (bf16[64,1152]{1,0:T(8,128)(2,1)}, bf16[64,1152]{1,0:T(8,128)(2,1)S(1)}, u32[]{:S(2)}, u32[]{:S(2)}) collective-permute-start(bf16[64,1152]{1,0:T(8,128)(2,1)} %param.7), channel_id=1, source_target_pairs={{0,1},{1,0},{2,3},{3,2},{4,5},{5,4},{6,7},{7,6},{8,9},{9,8},{10,11... | collective-permute-start | bytes 442376 | tf_op jit(solution)/shard_map/ppermute | solution.py:19
  4.7 1.5 %convolution_convert_fusion.1 = bf16[144,512]{1,0:T(8,128)(2,1)S(1)} fusion(bf16[1152,144]{0,1:T(8,128)(2,1)} %param.6, bf16[512,1152]{1,0:T(8,128)(2,1)S(1)} %copy-done), kind=kOutput, calls=%fused_computation.25 | convolution fusion | flops 169943040 | bytes 1658880 | tf_op jit(solution)/shard_map/dot_general | solution.py:85
  6.3 1.1 broadcast_in_dim.20
  7.4 4.3 %all-to-all-start = ((bf16[8,144,512]{2,1,0:T(8,128)(2,1)}), bf16[8,144,512]{2,1,0:T(8,128)(2,1)S(1)}, u32[]{:S(2)}, u32[]{:S(2)}) async-start(bf16[8,144,512]{2,1,0:T(8,128)(2,1)} %broadcast_in_dim.20), calls=%async_computation | async-start | bytes 2359296 | tf_op jit(solution)/shard_map/all_to_all | solution.py:34
  13.1 3.5 %collective-permute-start.2 = (bf16[128,1152]{1,0:T(8,128)(2,1)S(1)}, bf16[128,1152]{1,0:T(8,128)(2,1)S(1)}, u32[]{:S(2)}, u32[]{:S(2)}) collective-permute-start(bf16[128,1152]{1,0:T(8,128)(2,1)S(1)} %constant_dynamic-update-slice_fusion), channel_id=1, source_target_pairs={{0,16},{8,24},{16,32},{24,40},{32,48},{40,56},{48,64},{56,72},{64,... | collective-permute-start | bytes 884744 | tf_op jit(solution)/shard_map/ppermute | solution.py:15
  16.6 4.9 %collective-permute-start.1 = (bf16[128,1152]{1,0:T(8,128)(2,1)S(1)}, bf16[128,1152]{1,0:T(8,128)(2,1)S(1)}, u32[]{:S(2)}, u32[]{:S(2)}) collective-permute-start(bf16[128,1152]{1,0:T(8,128)(2,1)S(1)} %constant_dynamic-update-slice_fusion), channel_id=1, source_target_pairs={{0,8},{8,16},{16,24},{24,32},{32,40},{40,48},{48,56},{56,64},{64,7... | collective-permute-start | bytes 884744 | tf_op jit(solution)/shard_map/ppermute | solution.py:15
  21.6 0.5 iota_compare_fusion.3
  22.1 17.9 %collective-permute-done.2 = bf16[128,1152]{1,0:T(8,128)(2,1)S(1)} collective-permute-done((bf16[128,1152]{1,0:T(8,128)(2,1)S(1)}, bf16[128,1152]{1,0:T(8,128)(2,1)S(1)}, u32[]{:S(2)}, u32[]{:S(2)}) %collective-permute-start.2) | collective-permute-done | bytes 294944 | tf_op jit(solution)/shard_map/ppermute | solution.py:15
  40.0 0.3 fusion.2
  40.2 0.5 copy-done.4
  40.8 1.3 fusion.3
  42.1 0.2 fusion.13
  42.3 1.3 multiply_reduce_fusion.1
  43.6 0.8 fusion.1
  44.4 12.1 %all_to_all.20 = bf16[8,144,256]{2,1,0:T(8,128)(2,1)S(1)} all-to-all(bf16[8,144,256]{2,1,0:T(8,128)(2,1)S(1)} %bitcast.44), channel_id=1, replica_groups=mesh['dp'=128,'emb'=8] {'emb'}, dimensions={0} | all-to-all | bytes 1179648 | tf_op jit(solution)/shard_map/all_to_all | solution.py:34
  56.5 0.4 convolution_convert_fusion
  57.1 0.8 pad.4
  57.8 10.6 %all-to-all-start.2 = ((bf16[8,168,128]{2,1,0:T(8,128)(2,1)}), bf16[8,168,128]{2,1,0:T(8,128)(2,1)}, u32[]{:S(2)}, u32[]{:S(2)}) async-start(bf16[8,168,128]{2,1,0:T(8,128)(2,1)} %bitcast.41), calls=%async_computation.2 | async-start | bytes 688128 | tf_op jit(solution)/shard_map/all_to_all | solution.py:34
  68.5 0.7 fusion.52
  69.2 0.3 multiply_reduce_fusion
  69.5 2.7 %fusion.54 = (bf16[192,1152]{1,0:T(8,128)(2,1)}, f32[192,1152]{1,0:T(8,128)S(1)}) fusion(bf16[1152,512]{1,0:T(8,128)(2,1)S(1)} %bitcast.38, f32[512]{0:T(512)S(1)} %add_rsqrt_fusion, bf16[64,1152]{1,0:T(8,128)(2,1)} %get-tuple-element.21, bf16[64,1152]{1,0:T(8,128)(2,1)} %get-tuple-element.22, bf16[64,1152]{1,0:T(8,128)(2,1)S(1)} %get-tuple-element.20, ...), kind=kOutput, calls=%fused_computation.94 | convolution fusion | flops 459472896 | bytes 2952136 | tf_op jit(solution)/shard_map/dot_general | solution.py:138
  72.2 1.0 fusion.53
  73.3 2.1 %collective-permute-start.3 = (bf16[64,1152]{1,0:T(8,128)(2,1)S(1)}, bf16[64,1152]{1,0:T(8,128)(2,1)S(1)}, u32[]{:S(2)}, u32[]{:S(2)}) collective-permute-start(bf16[64,1152]{1,0:T(8,128)(2,1)S(1)} %get-tuple-element.24), channel_id=1, source_target_pairs={{0,1016},{8,0},{16,8},{24,16},{32,24},{40,32},{48,40},{56,48},{64,... | collective-permute-start | bytes 442376 | tf_op jit(solution)/shard_map/ppermute | solution.py:15
  75.3 5.7 %collective-permute-start.4 = (bf16[64,1152]{1,0:T(8,128)(2,1)S(1)}, bf16[64,1152]{1,0:T(8,128)(2,1)S(1)}, u32[]{:S(2)}, u32[]{:S(2)}) collective-permute-start(bf16[64,1152]{1,0:T(8,128)(2,1)S(1)} %get-tuple-element.23), channel_id=1, source_target_pairs={{0,1008},{8,1016},{16,0},{24,8},{32,16},{40,24},{48,32},{56,40},{6... | collective-permute-start | bytes 442376 | tf_op jit(solution)/shard_map/ppermute | solution.py:15
  81.0 1.0 reduce_sum.94
  82.0 31.8 %all-gather = bf16[2688,128]{1,0:T(8,128)(2,1)S(1)} all-gather(bf16[168,128]{1,0:T(8,128)(2,1)S(1)} %reduce_sum.94), channel_id=2, replica_groups={{0,32,64,96,128,160,192,224,256,288,320,352,384,416,448,480},{8,40,72,1..., dimensions={0}, use_global_device_ids=true | all-gather | bytes 731136 | tf_op jit(solution)/shard_map/all_gather | solution.py:56
  113.9 0.8 broadcast_in_dim.39
  114.7 9.1 %all-to-all-start.3 = ((bf16[8,168,128]{2,1,0:T(8,128)(2,1)}), bf16[8,168,128]{2,1,0:T(8,128)(2,1)S(1)}, u32[]{:S(2)}, u32[]{:S(2)}) async-start(bf16[8,168,128]{2,1,0:T(8,128)(2,1)} %broadcast_in_dim.39), calls=%async_computation.3 | async-start | bytes 688128 | tf_op jit(solution)/shard_map/all_to_all | solution.py:34
  124.1 0.2 multiply_reduce_fusion.2
  124.2 0.8 subtract_multiply_fusion
  125.1 6.3 %all-to-all-done.3 = bf16[8,168,128]{2,1,0:T(8,128)(2,1)S(1)} async-done(((bf16[8,168,128]{2,1,0:T(8,128)(2,1)}), bf16[8,168,128]{2,1,0:T(8,128)(2,1)S(1)}, u32[]{:S(2)}, u32[]{:S(2)}) %all-to-all-start.3) | async-done | bytes 344096 | tf_op jit(solution)/shard_map/all_to_all | solution.py:34
  131.4 0.9 copy_bitcast_fusion
  (44 shorter events, 0.8 us)
Async XLA Ops:
  0.6 4.1 %copy-start = (bf16[512,1152]{1,0:T(8,128)(2,1)S(1)}, bf16[512,1152]{1,0:T(8,128)(2,1)}, u32[]{:S(2)}) copy-start(bf16[512,1152]{1,0:T(8,128)(2,1)} %param.5) | copy-start | bytes 3538948
  0.6 12.4 %collective-permute-start = (bf16[64,1152]{1,0:T(8,128)(2,1)}, bf16[64,1152]{1,0:T(8,128)(2,1)S(1)}, u32[]{:S(2)}, u32[]{:S(2)}) collective-permute-start(bf16[64,1152]{1,0:T(8,128)(2,1)} %param.7), channel_id=1, source_target_pairs={{0,1},{1,0},{2,3},{3,2},{4,5},{5,4},{6,7},{7,6},{8,9},{9,8},{10,11... | collective-permute-start | bytes 442376 | tf_op jit(solution)/shard_map/ppermute | solution.py:19
  7.4 5.6 %copy-start.1 = (bf16[64,1152]{1,0:T(8,128)(2,1)S(1)}, bf16[64,1152]{1,0:T(8,128)(2,1)}, u32[]{:S(2)}) copy-start(bf16[64,1152]{1,0:T(8,128)(2,1)} %param.7) | copy-start | bytes 442372
  7.4 34.7 %all-to-all-start = ((bf16[8,144,512]{2,1,0:T(8,128)(2,1)}), bf16[8,144,512]{2,1,0:T(8,128)(2,1)S(1)}, u32[]{:S(2)}, u32[]{:S(2)}) async-start(bf16[8,144,512]{2,1,0:T(8,128)(2,1)} %broadcast_in_dim.20), calls=%async_computation | async-start | bytes 2359296 | tf_op jit(solution)/shard_map/all_to_all | solution.py:34
  13.1 26.9 %collective-permute-start.2 = (bf16[128,1152]{1,0:T(8,128)(2,1)S(1)}, bf16[128,1152]{1,0:T(8,128)(2,1)S(1)}, u32[]{:S(2)}, u32[]{:S(2)}) collective-permute-start(bf16[128,1152]{1,0:T(8,128)(2,1)S(1)} %constant_dynamic-update-slice_fusion), channel_id=1, source_target_pairs={{0,16},{8,24},{16,32},{24,40},{32,48},{40,56},{48,64},{56,72},{64,... | collective-permute-start | bytes 884744 | tf_op jit(solution)/shard_map/ppermute | solution.py:15
  16.6 23.4 %collective-permute-start.1 = (bf16[128,1152]{1,0:T(8,128)(2,1)S(1)}, bf16[128,1152]{1,0:T(8,128)(2,1)S(1)}, u32[]{:S(2)}, u32[]{:S(2)}) collective-permute-start(bf16[128,1152]{1,0:T(8,128)(2,1)S(1)} %constant_dynamic-update-slice_fusion), channel_id=1, source_target_pairs={{0,8},{8,16},{16,24},{24,32},{32,40},{40,48},{48,56},{56,64},{64,7... | collective-permute-start | bytes 884744 | tf_op jit(solution)/shard_map/ppermute | solution.py:15
  40.0 0.7 copy-start.4
  40.0 0.8 copy-start.5
  42.1 1.5 %copy-start.2 = (bf16[384,1152]{1,0:T(8,128)(2,1)}, bf16[384,1152]{1,0:T(8,128)(2,1)S(1)}, u32[]{:S(2)}) copy-start(bf16[384,1152]{1,0:T(8,128)(2,1)S(1)} %fusion.3) | copy-start | bytes 2654212
  42.3 1.3 copy-start.6
  56.9 11.5 %copy-start.3 = (bf16[384,1152]{1,0:T(8,128)(2,1)S(1)}, bf16[384,1152]{1,0:T(8,128)(2,1)}, u32[]{:S(2)}) copy-start(bf16[384,1152]{1,0:T(8,128)(2,1)} %copy-done.2) | copy-start | bytes 2654212
  57.8 23.2 %all-to-all-start.2 = ((bf16[8,168,128]{2,1,0:T(8,128)(2,1)}), bf16[8,168,128]{2,1,0:T(8,128)(2,1)}, u32[]{:S(2)}, u32[]{:S(2)}) async-start(bf16[8,168,128]{2,1,0:T(8,128)(2,1)} %bitcast.41), calls=%async_computation.2 | async-start | bytes 688128 | tf_op jit(solution)/shard_map/all_to_all | solution.py:34
  73.3 40.6 %collective-permute-start.3 = (bf16[64,1152]{1,0:T(8,128)(2,1)S(1)}, bf16[64,1152]{1,0:T(8,128)(2,1)S(1)}, u32[]{:S(2)}, u32[]{:S(2)}) collective-permute-start(bf16[64,1152]{1,0:T(8,128)(2,1)S(1)} %get-tuple-element.24), channel_id=1, source_target_pairs={{0,1016},{8,0},{16,8},{24,16},{32,24},{40,32},{48,40},{56,48},{64,... | collective-permute-start | bytes 442376 | tf_op jit(solution)/shard_map/ppermute | solution.py:15
  75.3 38.6 %collective-permute-start.4 = (bf16[64,1152]{1,0:T(8,128)(2,1)S(1)}, bf16[64,1152]{1,0:T(8,128)(2,1)S(1)}, u32[]{:S(2)}, u32[]{:S(2)}) collective-permute-start(bf16[64,1152]{1,0:T(8,128)(2,1)S(1)} %get-tuple-element.23), channel_id=1, source_target_pairs={{0,1008},{8,1016},{16,0},{24,8},{32,16},{40,24},{48,32},{56,40},{6... | collective-permute-start | bytes 442376 | tf_op jit(solution)/shard_map/ppermute | solution.py:15
  114.7 16.7 %all-to-all-start.3 = ((bf16[8,168,128]{2,1,0:T(8,128)(2,1)}), bf16[8,168,128]{2,1,0:T(8,128)(2,1)S(1)}, u32[]{:S(2)}, u32[]{:S(2)}) async-start(bf16[8,168,128]{2,1,0:T(8,128)(2,1)} %broadcast_in_dim.39), calls=%async_computation.3 | async-start | bytes 688128 | tf_op jit(solution)/shard_map/all_to_all | solution.py:34
